TPU v7x, 256 devices: a whole 4x4x8 slice. The times are simulated.
256 devices in a mesh: tm: 32 (over x, y, core), space: 8 (over z).
Axes of the slice: x: 4, y: 4, z: 8, core: 2. Of those that a mesh axis runs over, the one named last changes fastest.
Arguments:
- starts: float32 [32, 3, 32, 128, 128], P('tm', None, 'space'), may hold values from 0 to 2
- velocity: float32 [3, 32, 128, 128], P(None, 'space'), may hold values from -1 to 1
- diffusivity: float32 [32, 128, 128], P('space'), may hold values from 0.2 to 0.8
- rate: float32 [32, 128, 128], P('space'), may hold values from 0.2 to 1
Outputs:
- new_starts: float32 [32, 3, 32, 128, 128], P('tm', None, 'space')
- new_ends: float32 [32, 3, 32, 128, 128], P('tm', None, 'space')
All inputs are finite; a program needn't handle non-finite values.
Results may differ from a plain program's by a relative error of at most 0.000029.
Values sent between devices are 32-bit elements; how exact they have to be, the bound alone decides.
No kernel may reach another device: no remote copies, remote signals or barrier semaphores. Data moves between devices by JAX's collectives and lax.ppermute only.
A program may use at most 128 MiB of HBM per device.

v0:
```python
import jax
import jax.numpy as jnp
from jax import lax
from jax.sharding import PartitionSpec as P

FINE = 8
COARSE_STEPS = 2


species_weights = (1.0, 0.6, 0.3)
decay_rate = 0.5


def with_halo(cells, sides, width):
    for axis, dim in sides:
        count = lax.axis_size(axis)
        ends = count - 1
        head = lax.slice_in_dim(cells, 0, width, axis=dim)
        tail = lax.slice_in_dim(cells, cells.shape[dim] - width, cells.shape[dim], axis=dim)
        cells = jnp.concatenate(
            [
                lax.ppermute(tail, axis, [(i, (i + 1) % count) for i in range(ends)]),
                cells,
                lax.ppermute(head, axis, [((i + 1) % count, i) for i in range(ends)]),
            ],
            axis=dim,
        )
    return cells


def shifted(block, axis, distance):
    devices = range(lax.axis_size(axis))
    route = [(i - distance, i) for i in devices if i - distance in devices]
    return lax.ppermute(block, axis, route)


def stencil(padded, coefs, inv_h, step_dt):
    center = padded[:, 1:-1]
    lower = padded[:, :-2]
    upper = padded[:, 2:]
    x_minus = jnp.roll(center, 1, axis=3)
    x_plus = jnp.roll(center, -1, axis=3)
    y_minus = jnp.roll(center, 1, axis=2)
    y_plus = jnp.roll(center, -1, axis=2)
    laplace = (x_minus + x_plus + y_minus + y_plus + lower + upper - 6.0 * center) * (inv_h * inv_h)
    vel_x = coefs[0][None]
    vel_y = coefs[1][None]
    vel_z = coefs[2][None]
    advect = (
        jnp.maximum(vel_x, 0.0) * (center - x_minus)
        + jnp.minimum(vel_x, 0.0) * (x_plus - center)
        + jnp.maximum(vel_y, 0.0) * (center - y_minus)
        + jnp.minimum(vel_y, 0.0) * (y_plus - center)
        + jnp.maximum(vel_z, 0.0) * (center - lower)
        + jnp.minimum(vel_z, 0.0) * (upper - center)
    ) * inv_h
    weights = jnp.array(species_weights, jnp.float32)[:, None, None, None]
    diffuse = weights * coefs[3][None] * laplace
    react_term = coefs[4] * center[0] * center[1]
    react = jnp.stack([-react_term, -react_term, react_term - decay_rate * center[2]], 0)
    return center + step_dt * (diffuse - advect + react)


def restrict(values):
    comps, depth, rows, cols = values.shape
    blocks = values.reshape(comps, depth // 4, 4, rows // 4, 4, cols // 4, 4)
    return jnp.mean(blocks, axis=(2, 4, 6))


def prolong(coarse_vals):
    comps, depth, rows, cols = coarse_vals.shape
    wide = jnp.broadcast_to(
        coarse_vals[:, :, None, :, None, :, None], (comps, depth, 4, rows, 4, cols, 4)
    )
    return wide.reshape(comps, depth * 4, rows * 4, cols * 4)


def coarse_prop(state, coarse_coefs):
    for _ in range(COARSE_STEPS):
        padded = jnp.pad(state, ((0, 0), (1, 1), (0, 0), (0, 0)))
        state = stencil(padded, coarse_coefs, 0.25, 0.4)
    return state


def shards(starts, velocity, diffusivity, rate):
    slab_state = starts[0]
    coefs = jnp.concatenate([velocity, diffusivity[None], rate[None]], 0)
    coarse_coefs = lax.all_gather(restrict(coefs), "space", axis=1, tiled=True)
    end_state = slab_state
    for _ in range(FINE):
        padded = with_halo(end_state, (("space", 1),), 1)
        end_state = stencil(padded, coefs, 1.0, 0.1)
    end_coarse, start_coarse = (
        lax.all_gather(restrict(end_state), "space", axis=1, tiled=True),
        lax.all_gather(restrict(slab_state), "space", axis=1, tiled=True),
    )
    old_coarse = coarse_prop(start_coarse, coarse_coefs)
    defect = end_coarse - old_coarse
    slice_index = lax.axis_index("tm")
    is_first = slice_index == 0
    slice_count = lax.axis_size("tm")

    def chain_turn(turn_index, advanced):
        incoming = shifted(advanced + defect, "tm", 1)
        return coarse_prop(jnp.where(is_first, start_coarse, incoming), coarse_coefs)

    advanced = lax.fori_loop(0, slice_count - 1, chain_turn, old_coarse)
    correction = advanced - old_coarse
    coarse_planes = end_state.shape[1] // 4
    own_part = lax.dynamic_slice_in_dim(
        correction, lax.axis_index("space") * coarse_planes, coarse_planes, 1
    )
    corrected = end_state + prolong(own_part)
    arrived = shifted(corrected, "tm", 1)
    result = jnp.where(is_first, slab_state, arrived)
    return (result[None], corrected[None])


def solution(mesh):
    placed = (
        P("tm", None, "space", None, None),
        P(None, "space", None, None),
        P("space", None, None),
        P("space", None, None),
    )
    return jax.shard_map(
        shards,
        mesh=mesh,
        in_specs=placed,
        out_specs=(P("tm", None, "space", None, None), P("tm", None, "space", None, None)),
        check_vma=False,
    )
```

profile of v0, /device:TPU:6, one launch (start us, length us, event | category | flops | bytes accessed | tf_op | source)
XLA Modules:
  0.0 769.7 jit_solution(7932093157417420389)
XLA Ops:
  16.3 27.3 %concatenate.290 = f32[3,1,4,32,4,32,4]{6,5,4,3,2,0,1:T(8,128)} reshape(f32[3,4,128,128]{3,2,1,0:T(8,128)S(1)} %copy-done.7) | data formatting | bytes 1572864 | tf_op jit(solution)/shard_map/concatenate | solution.py:87
  44.5 10.0 %concatenate.292 = f32[1,1,4,32,4,32,4]{6,5,4,3,2,1,0:T(8,128)} reshape(f32[4,128,128]{2,1,0:T(8,128)S(1)} %copy-done.4) | data formatting | bytes 524288 | tf_op jit(solution)/shard_map/concatenate | solution.py:87
  65.6 29.0 %all-gather = f32[3,256,32]{2,1,0:T(8,128)S(1)} all-gather(f32[3,32,32]{2,1,0:T(8,128)S(1)} %broadcast_multiply_fusion.2), channel_id=2, replica_groups=mesh['tm'=32,'space'=8] {'space'}, dimensions={1}, use_global_device_ids=true | all-gather | bytes 110592 | tf_op jit(solution)/shard_map/all_gather | solution.py:95
  99.0 18.2 %copy.22 = f32[3,1,4,32,4,32,4]{5,3,6,4,2,1,0:T(8,128)} copy(f32[3,1,4,32,4,32,4]{6,5,4,3,2,0,1:T(8,128)} %concatenate.290) | data formatting | bytes 1572864 | tf_op jit(solution)/shard_map/concatenate | solution.py:87
  117.2 10.0 %concatenate.291 = f32[1,1,4,32,4,32,4]{6,5,4,3,2,1,0:T(8,128)} reshape(f32[4,128,128]{2,1,0:T(8,128)S(1)} %copy-done.1) | data formatting | bytes 524288 | tf_op jit(solution)/shard_map/concatenate | solution.py:87
  143.6 26.1 %all-gather.1 = f32[5,256,32]{2,1,0:T(8,128)S(1)} all-gather(f32[5,32,32]{2,1,0:T(8,128)S(1)} %broadcast_multiply_fusion), channel_id=3, replica_groups=mesh['tm'=32,'space'=8] {'space'}, dimensions={1}, use_global_device_ids=true | all-gather | bytes 184320 | tf_op jit(solution)/shard_map/all_gather | solution.py:88
  286.3 25.3 %all-gather.2 = f32[3,256,32]{2,1,0:T(8,128)S(1)} all-gather(f32[3,32,32]{2,1,0:T(8,128)S(1)} %broadcast_multiply_fusion.1), channel_id=4, replica_groups=mesh['tm'=32,'space'=8] {'space'}, dimensions={1}, use_global_device_ids=true | all-gather | bytes 110592 | tf_op jit(solution)/shard_map/all_gather | solution.py:94
  314.3 428.9 %while.14 = (s32[]{:T(128)}, f32[3,8,32,32]{3,2,1,0:T(8,128)S(1)}, pred[]{:T(512)}, f32[3,8,32,32]{3,2,1,0:T(8,128)S(1)}, f32[3,8,32,32]{3,2,1,0:T(8,128)S(1)}, ...) while((s32[]{:T(128)}, f32[3,8,32,32]{3,2,1,0:T(8,128)S(1)}, ...), condition=%wide.region_6.7_spmd.clone.clone, body=%wide.region_5.6_spmd.sunk.clone.clone.sunk | while | flops 2048002 | bytes 5079190 | solution.py:107
  316.3 9.3 %collective-permute-done = f32[3,8,32,32]{3,2,1,0:T(8,128)S(1)} collective-permute-done((f32[3,8,32,32]{3,2,1,0:T(8,128)S(1)}, f32[3,8,32,32]{3,2,1,0:T(8,128)S(1)}, u32[]{:S(2)}, u32[]{:S(2)}) %collective-permute-start) | collective-permute-done | bytes 98336 | tf_op jit(solution)/shard_map/while/body/eval_jaxpr/ppermute | solution.py:34
  330.1 9.3 %collective-permute-done = f32[3,8,32,32]{3,2,1,0:T(8,128)S(1)} collective-permute-done((f32[3,8,32,32]{3,2,1,0:T(8,128)S(1)}, f32[3,8,32,32]{3,2,1,0:T(8,128)S(1)}, u32[]{:S(2)}, u32[]{:S(2)}) %collective-permute-start) | collective-permute-done | bytes 98336 | tf_op jit(solution)/shard_map/while/body/eval_jaxpr/ppermute | solution.py:34
  344.0 9.3 %collective-permute-done = f32[3,8,32,32]{3,2,1,0:T(8,128)S(1)} collective-permute-done((f32[3,8,32,32]{3,2,1,0:T(8,128)S(1)}, f32[3,8,32,32]{3,2,1,0:T(8,128)S(1)}, u32[]{:S(2)}, u32[]{:S(2)}) %collective-permute-start) | collective-permute-done | bytes 98336 | tf_op jit(solution)/shard_map/while/body/eval_jaxpr/ppermute | solution.py:34
  357.8 9.3 %collective-permute-done = f32[3,8,32,32]{3,2,1,0:T(8,128)S(1)} collective-permute-done((f32[3,8,32,32]{3,2,1,0:T(8,128)S(1)}, f32[3,8,32,32]{3,2,1,0:T(8,128)S(1)}, u32[]{:S(2)}, u32[]{:S(2)}) %collective-permute-start) | collective-permute-done | bytes 98336 | tf_op jit(solution)/shard_map/while/body/eval_jaxpr/ppermute | solution.py:34
  371.6 9.3 %collective-permute-done = f32[3,8,32,32]{3,2,1,0:T(8,128)S(1)} collective-permute-done((f32[3,8,32,32]{3,2,1,0:T(8,128)S(1)}, f32[3,8,32,32]{3,2,1,0:T(8,128)S(1)}, u32[]{:S(2)}, u32[]{:S(2)}) %collective-permute-start) | collective-permute-done | bytes 98336 | tf_op jit(solution)/shard_map/while/body/eval_jaxpr/ppermute | solution.py:34
  385.5 9.3 %collective-permute-done = f32[3,8,32,32]{3,2,1,0:T(8,128)S(1)} collective-permute-done((f32[3,8,32,32]{3,2,1,0:T(8,128)S(1)}, f32[3,8,32,32]{3,2,1,0:T(8,128)S(1)}, u32[]{:S(2)}, u32[]{:S(2)}) %collective-permute-start) | collective-permute-done | bytes 98336 | tf_op jit(solution)/shard_map/while/body/eval_jaxpr/ppermute | solution.py:34
  399.3 9.3 %collective-permute-done = f32[3,8,32,32]{3,2,1,0:T(8,128)S(1)} collective-permute-done((f32[3,8,32,32]{3,2,1,0:T(8,128)S(1)}, f32[3,8,32,32]{3,2,1,0:T(8,128)S(1)}, u32[]{:S(2)}, u32[]{:S(2)}) %collective-permute-start) | collective-permute-done | bytes 98336 | tf_op jit(solution)/shard_map/while/body/eval_jaxpr/ppermute | solution.py:34
  413.1 9.3 %collective-permute-done = f32[3,8,32,32]{3,2,1,0:T(8,128)S(1)} collective-permute-done((f32[3,8,32,32]{3,2,1,0:T(8,128)S(1)}, f32[3,8,32,32]{3,2,1,0:T(8,128)S(1)}, u32[]{:S(2)}, u32[]{:S(2)}) %collective-permute-start) | collective-permute-done | bytes 98336 | tf_op jit(solution)/shard_map/while/body/eval_jaxpr/ppermute | solution.py:34
  427.0 9.3 %collective-permute-done = f32[3,8,32,32]{3,2,1,0:T(8,128)S(1)} collective-permute-done((f32[3,8,32,32]{3,2,1,0:T(8,128)S(1)}, f32[3,8,32,32]{3,2,1,0:T(8,128)S(1)}, u32[]{:S(2)}, u32[]{:S(2)}) %collective-permute-start) | collective-permute-done | bytes 98336 | tf_op jit(solution)/shard_map/while/body/eval_jaxpr/ppermute | solution.py:34
  440.8 9.3 %collective-permute-done = f32[3,8,32,32]{3,2,1,0:T(8,128)S(1)} collective-permute-done((f32[3,8,32,32]{3,2,1,0:T(8,128)S(1)}, f32[3,8,32,32]{3,2,1,0:T(8,128)S(1)}, u32[]{:S(2)}, u32[]{:S(2)}) %collective-permute-start) | collective-permute-done | bytes 98336 | tf_op jit(solution)/shard_map/while/body/eval_jaxpr/ppermute | solution.py:34
  454.7 9.3 %collective-permute-done = f32[3,8,32,32]{3,2,1,0:T(8,128)S(1)} collective-permute-done((f32[3,8,32,32]{3,2,1,0:T(8,128)S(1)}, f32[3,8,32,32]{3,2,1,0:T(8,128)S(1)}, u32[]{:S(2)}, u32[]{:S(2)}) %collective-permute-start) | collective-permute-done | bytes 98336 | tf_op jit(solution)/shard_map/while/body/eval_jaxpr/ppermute | solution.py:34
  468.5 9.3 %collective-permute-done = f32[3,8,32,32]{3,2,1,0:T(8,128)S(1)} collective-permute-done((f32[3,8,32,32]{3,2,1,0:T(8,128)S(1)}, f32[3,8,32,32]{3,2,1,0:T(8,128)S(1)}, u32[]{:S(2)}, u32[]{:S(2)}) %collective-permute-start) | collective-permute-done | bytes 98336 | tf_op jit(solution)/shard_map/while/body/eval_jaxpr/ppermute | solution.py:34
  482.3 9.3 %collective-permute-done = f32[3,8,32,32]{3,2,1,0:T(8,128)S(1)} collective-permute-done((f32[3,8,32,32]{3,2,1,0:T(8,128)S(1)}, f32[3,8,32,32]{3,2,1,0:T(8,128)S(1)}, u32[]{:S(2)}, u32[]{:S(2)}) %collective-permute-start) | collective-permute-done | bytes 98336 | tf_op jit(solution)/shard_map/while/body/eval_jaxpr/ppermute | solution.py:34
  496.2 9.3 %collective-permute-done = f32[3,8,32,32]{3,2,1,0:T(8,128)S(1)} collective-permute-done((f32[3,8,32,32]{3,2,1,0:T(8,128)S(1)}, f32[3,8,32,32]{3,2,1,0:T(8,128)S(1)}, u32[]{:S(2)}, u32[]{:S(2)}) %collective-permute-start) | collective-permute-done | bytes 98336 | tf_op jit(solution)/shard_map/while/body/eval_jaxpr/ppermute | solution.py:34
  510.0 9.3 %collective-permute-done = f32[3,8,32,32]{3,2,1,0:T(8,128)S(1)} collective-permute-done((f32[3,8,32,32]{3,2,1,0:T(8,128)S(1)}, f32[3,8,32,32]{3,2,1,0:T(8,128)S(1)}, u32[]{:S(2)}, u32[]{:S(2)}) %collective-permute-start) | collective-permute-done | bytes 98336 | tf_op jit(solution)/shard_map/while/body/eval_jaxpr/ppermute | solution.py:34
  523.8 9.3 %collective-permute-done = f32[3,8,32,32]{3,2,1,0:T(8,128)S(1)} collective-permute-done((f32[3,8,32,32]{3,2,1,0:T(8,128)S(1)}, f32[3,8,32,32]{3,2,1,0:T(8,128)S(1)}, u32[]{:S(2)}, u32[]{:S(2)}) %collective-permute-start) | collective-permute-done | bytes 98336 | tf_op jit(solution)/shard_map/while/body/eval_jaxpr/ppermute | solution.py:34
  537.7 9.3 %collective-permute-done = f32[3,8,32,32]{3,2,1,0:T(8,128)S(1)} collective-permute-done((f32[3,8,32,32]{3,2,1,0:T(8,128)S(1)}, f32[3,8,32,32]{3,2,1,0:T(8,128)S(1)}, u32[]{:S(2)}, u32[]{:S(2)}) %collective-permute-start) | collective-permute-done | bytes 98336 | tf_op jit(solution)/shard_map/while/body/eval_jaxpr/ppermute | solution.py:34
  551.5 9.3 %collective-permute-done = f32[3,8,32,32]{3,2,1,0:T(8,128)S(1)} collective-permute-done((f32[3,8,32,32]{3,2,1,0:T(8,128)S(1)}, f32[3,8,32,32]{3,2,1,0:T(8,128)S(1)}, u32[]{:S(2)}, u32[]{:S(2)}) %collective-permute-start) | collective-permute-done | bytes 98336 | tf_op jit(solution)/shard_map/while/body/eval_jaxpr/ppermute | solution.py:34
  565.3 9.3 %collective-permute-done = f32[3,8,32,32]{3,2,1,0:T(8,128)S(1)} collective-permute-done((f32[3,8,32,32]{3,2,1,0:T(8,128)S(1)}, f32[3,8,32,32]{3,2,1,0:T(8,128)S(1)}, u32[]{:S(2)}, u32[]{:S(2)}) %collective-permute-start) | collective-permute-done | bytes 98336 | tf_op jit(solution)/shard_map/while/body/eval_jaxpr/ppermute | solution.py:34
  579.2 9.3 %collective-permute-done = f32[3,8,32,32]{3,2,1,0:T(8,128)S(1)} collective-permute-done((f32[3,8,32,32]{3,2,1,0:T(8,128)S(1)}, f32[3,8,32,32]{3,2,1,0:T(8,128)S(1)}, u32[]{:S(2)}, u32[]{:S(2)}) %collective-permute-start) | collective-permute-done | bytes 98336 | tf_op jit(solution)/shard_map/while/body/eval_jaxpr/ppermute | solution.py:34
  593.0 9.3 %collective-permute-done = f32[3,8,32,32]{3,2,1,0:T(8,128)S(1)} collective-permute-done((f32[3,8,32,32]{3,2,1,0:T(8,128)S(1)}, f32[3,8,32,32]{3,2,1,0:T(8,128)S(1)}, u32[]{:S(2)}, u32[]{:S(2)}) %collective-permute-start) | collective-permute-done | bytes 98336 | tf_op jit(solution)/shard_map/while/body/eval_jaxpr/ppermute | solution.py:34
  606.9 9.3 %collective-permute-done = f32[3,8,32,32]{3,2,1,0:T(8,128)S(1)} collective-permute-done((f32[3,8,32,32]{3,2,1,0:T(8,128)S(1)}, f32[3,8,32,32]{3,2,1,0:T(8,128)S(1)}, u32[]{:S(2)}, u32[]{:S(2)}) %collective-permute-start) | collective-permute-done | bytes 98336 | tf_op jit(solution)/shard_map/while/body/eval_jaxpr/ppermute | solution.py:34
  689.9 9.3 %collective-permute-done = f32[3,8,32,32]{3,2,1,0:T(8,128)S(1)} collective-permute-done((f32[3,8,32,32]{3,2,1,0:T(8,128)S(1)}, f32[3,8,32,32]{3,2,1,0:T(8,128)S(1)}, u32[]{:S(2)}, u32[]{:S(2)}) %collective-permute-start) | collective-permute-done | bytes 98336 | tf_op jit(solution)/shard_map/while/body/eval_jaxpr/ppermute | solution.py:34
  756.2 12.5 %collective-permute-done.17 = f32[3,4,128,128]{3,2,1,0:T(8,128)S(1)} collective-permute-done((f32[3,4,128,128]{3,2,1,0:T(8,128)S(1)}, f32[3,4,128,128]{3,2,1,0:T(8,128)S(1)}, u32[]{:S(2)}, u32[]{:S(2)}) %collective-permute-start.17) | collective-permute-done | bytes 786464 | tf_op jit(solution)/shard_map/ppermute | solution.py:34
  (651 shorter events, 393.9 us)
Async XLA Ops:
  2.6 172.6 %collective-permute-start.1 = (f32[3,1,128,128]{3,2,1,0:T(8,128)}, f32[3,1,128,128]{3,2,1,0:T(8,128)}, u32[]{:S(2)}, u32[]{:S(2)}) collective-permute-start(f32[3,1,128,128]{3,2,1,0:T(8,128)} %get-tuple-element.289), channel_id=1, source_target_pairs={{0,1},{1,2},{2,3},{3,4},{4,5},{5,6},{6,7},{8,9},{9,10},{10,11},{11... | collective-permute-start | bytes 589832 | tf_op jit(solution)/shard_map/ppermute | solution.py:22
  7.0 168.1 %collective-permute-start.2 = (f32[3,1,128,128]{3,2,1,0:T(8,128)}, f32[3,1,128,128]{3,2,1,0:T(8,128)}, u32[]{:S(2)}, u32[]{:S(2)}) collective-permute-start(f32[3,1,128,128]{3,2,1,0:T(8,128)} %get-tuple-element.290), channel_id=1, source_target_pairs={{1,0},{2,1},{3,2},{4,3},{5,4},{6,5},{7,6},{9,8},{10,9},{11,10},{12... | collective-permute-start | bytes 589832 | tf_op jit(solution)/shard_map/ppermute | solution.py:24
  314.4 11.2 %collective-permute-start = (f32[3,8,32,32]{3,2,1,0:T(8,128)S(1)}, f32[3,8,32,32]{3,2,1,0:T(8,128)S(1)}, u32[]{:S(2)}, u32[]{:S(2)}) collective-permute-start(f32[3,8,32,32]{3,2,1,0:T(8,128)S(1)} %add.1080), channel_id=1, source_target_pairs={{0,8},{8,16},{16,24},{24,32},{32,40},{40,48},{48,56},{56,64},{64,7... | collective-permute-start | bytes 294920 | tf_op jit(solution)/shard_map/while/body/eval_jaxpr/ppermute | solution.py:34
  328.2 11.2 %collective-permute-start = (f32[3,8,32,32]{3,2,1,0:T(8,128)S(1)}, f32[3,8,32,32]{3,2,1,0:T(8,128)S(1)}, u32[]{:S(2)}, u32[]{:S(2)}) collective-permute-start(f32[3,8,32,32]{3,2,1,0:T(8,128)S(1)} %add.1080), channel_id=1, source_target_pairs={{0,8},{8,16},{16,24},{24,32},{32,40},{40,48},{48,56},{56,64},{64,7... | collective-permute-start | bytes 294920 | tf_op jit(solution)/shard_map/while/body/eval_jaxpr/ppermute | solution.py:34
  342.0 11.2 %collective-permute-start = (f32[3,8,32,32]{3,2,1,0:T(8,128)S(1)}, f32[3,8,32,32]{3,2,1,0:T(8,128)S(1)}, u32[]{:S(2)}, u32[]{:S(2)}) collective-permute-start(f32[3,8,32,32]{3,2,1,0:T(8,128)S(1)} %add.1080), channel_id=1, source_target_pairs={{0,8},{8,16},{16,24},{24,32},{32,40},{40,48},{48,56},{56,64},{64,7... | collective-permute-start | bytes 294920 | tf_op jit(solution)/shard_map/while/body/eval_jaxpr/ppermute | solution.py:34
  355.9 11.2 %collective-permute-start = (f32[3,8,32,32]{3,2,1,0:T(8,128)S(1)}, f32[3,8,32,32]{3,2,1,0:T(8,128)S(1)}, u32[]{:S(2)}, u32[]{:S(2)}) collective-permute-start(f32[3,8,32,32]{3,2,1,0:T(8,128)S(1)} %add.1080), channel_id=1, source_target_pairs={{0,8},{8,16},{16,24},{24,32},{32,40},{40,48},{48,56},{56,64},{64,7... | collective-permute-start | bytes 294920 | tf_op jit(solution)/shard_map/while/body/eval_jaxpr/ppermute | solution.py:34
  369.7 11.2 %collective-permute-start = (f32[3,8,32,32]{3,2,1,0:T(8,128)S(1)}, f32[3,8,32,32]{3,2,1,0:T(8,128)S(1)}, u32[]{:S(2)}, u32[]{:S(2)}) collective-permute-start(f32[3,8,32,32]{3,2,1,0:T(8,128)S(1)} %add.1080), channel_id=1, source_target_pairs={{0,8},{8,16},{16,24},{24,32},{32,40},{40,48},{48,56},{56,64},{64,7... | collective-permute-start | bytes 294920 | tf_op jit(solution)/shard_map/while/body/eval_jaxpr/ppermute | solution.py:34
  383.5 11.2 %collective-permute-start = (f32[3,8,32,32]{3,2,1,0:T(8,128)S(1)}, f32[3,8,32,32]{3,2,1,0:T(8,128)S(1)}, u32[]{:S(2)}, u32[]{:S(2)}) collective-permute-start(f32[3,8,32,32]{3,2,1,0:T(8,128)S(1)} %add.1080), channel_id=1, source_target_pairs={{0,8},{8,16},{16,24},{24,32},{32,40},{40,48},{48,56},{56,64},{64,7... | collective-permute-start | bytes 294920 | tf_op jit(solution)/shard_map/while/body/eval_jaxpr/ppermute | solution.py:34
  397.4 11.2 %collective-permute-start = (f32[3,8,32,32]{3,2,1,0:T(8,128)S(1)}, f32[3,8,32,32]{3,2,1,0:T(8,128)S(1)}, u32[]{:S(2)}, u32[]{:S(2)}) collective-permute-start(f32[3,8,32,32]{3,2,1,0:T(8,128)S(1)} %add.1080), channel_id=1, source_target_pairs={{0,8},{8,16},{16,24},{24,32},{32,40},{40,48},{48,56},{56,64},{64,7... | collective-permute-start | bytes 294920 | tf_op jit(solution)/shard_map/while/body/eval_jaxpr/ppermute | solution.py:34
  411.2 11.2 %collective-permute-start = (f32[3,8,32,32]{3,2,1,0:T(8,128)S(1)}, f32[3,8,32,32]{3,2,1,0:T(8,128)S(1)}, u32[]{:S(2)}, u32[]{:S(2)}) collective-permute-start(f32[3,8,32,32]{3,2,1,0:T(8,128)S(1)} %add.1080), channel_id=1, source_target_pairs={{0,8},{8,16},{16,24},{24,32},{32,40},{40,48},{48,56},{56,64},{64,7... | collective-permute-start | bytes 294920 | tf_op jit(solution)/shard_map/while/body/eval_jaxpr/ppermute | solution.py:34
  425.1 11.2 %collective-permute-start = (f32[3,8,32,32]{3,2,1,0:T(8,128)S(1)}, f32[3,8,32,32]{3,2,1,0:T(8,128)S(1)}, u32[]{:S(2)}, u32[]{:S(2)}) collective-permute-start(f32[3,8,32,32]{3,2,1,0:T(8,128)S(1)} %add.1080), channel_id=1, source_target_pairs={{0,8},{8,16},{16,24},{24,32},{32,40},{40,48},{48,56},{56,64},{64,7... | collective-permute-start | bytes 294920 | tf_op jit(solution)/shard_map/while/body/eval_jaxpr/ppermute | solution.py:34
  438.9 11.2 %collective-permute-start = (f32[3,8,32,32]{3,2,1,0:T(8,128)S(1)}, f32[3,8,32,32]{3,2,1,0:T(8,128)S(1)}, u32[]{:S(2)}, u32[]{:S(2)}) collective-permute-start(f32[3,8,32,32]{3,2,1,0:T(8,128)S(1)} %add.1080), channel_id=1, source_target_pairs={{0,8},{8,16},{16,24},{24,32},{32,40},{40,48},{48,56},{56,64},{64,7... | collective-permute-start | bytes 294920 | tf_op jit(solution)/shard_map/while/body/eval_jaxpr/ppermute | solution.py:34
  452.7 11.2 %collective-permute-start = (f32[3,8,32,32]{3,2,1,0:T(8,128)S(1)}, f32[3,8,32,32]{3,2,1,0:T(8,128)S(1)}, u32[]{:S(2)}, u32[]{:S(2)}) collective-permute-start(f32[3,8,32,32]{3,2,1,0:T(8,128)S(1)} %add.1080), channel_id=1, source_target_pairs={{0,8},{8,16},{16,24},{24,32},{32,40},{40,48},{48,56},{56,64},{64,7... | collective-permute-start | bytes 294920 | tf_op jit(solution)/shard_map/while/body/eval_jaxpr/ppermute | solution.py:34
  466.6 11.2 %collective-permute-start = (f32[3,8,32,32]{3,2,1,0:T(8,128)S(1)}, f32[3,8,32,32]{3,2,1,0:T(8,128)S(1)}, u32[]{:S(2)}, u32[]{:S(2)}) collective-permute-start(f32[3,8,32,32]{3,2,1,0:T(8,128)S(1)} %add.1080), channel_id=1, source_target_pairs={{0,8},{8,16},{16,24},{24,32},{32,40},{40,48},{48,56},{56,64},{64,7... | collective-permute-start | bytes 294920 | tf_op jit(solution)/shard_map/while/body/eval_jaxpr/ppermute | solution.py:34
  480.4 11.2 %collective-permute-start = (f32[3,8,32,32]{3,2,1,0:T(8,128)S(1)}, f32[3,8,32,32]{3,2,1,0:T(8,128)S(1)}, u32[]{:S(2)}, u32[]{:S(2)}) collective-permute-start(f32[3,8,32,32]{3,2,1,0:T(8,128)S(1)} %add.1080), channel_id=1, source_target_pairs={{0,8},{8,16},{16,24},{24,32},{32,40},{40,48},{48,56},{56,64},{64,7... | collective-permute-start | bytes 294920 | tf_op jit(solution)/shard_map/while/body/eval_jaxpr/ppermute | solution.py:34
  494.2 11.2 %collective-permute-start = (f32[3,8,32,32]{3,2,1,0:T(8,128)S(1)}, f32[3,8,32,32]{3,2,1,0:T(8,128)S(1)}, u32[]{:S(2)}, u32[]{:S(2)}) collective-permute-start(f32[3,8,32,32]{3,2,1,0:T(8,128)S(1)} %add.1080), channel_id=1, source_target_pairs={{0,8},{8,16},{16,24},{24,32},{32,40},{40,48},{48,56},{56,64},{64,7... | collective-permute-start | bytes 294920 | tf_op jit(solution)/shard_map/while/body/eval_jaxpr/ppermute | solution.py:34
  508.1 11.2 %collective-permute-start = (f32[3,8,32,32]{3,2,1,0:T(8,128)S(1)}, f32[3,8,32,32]{3,2,1,0:T(8,128)S(1)}, u32[]{:S(2)}, u32[]{:S(2)}) collective-permute-start(f32[3,8,32,32]{3,2,1,0:T(8,128)S(1)} %add.1080), channel_id=1, source_target_pairs={{0,8},{8,16},{16,24},{24,32},{32,40},{40,48},{48,56},{56,64},{64,7... | collective-permute-start | bytes 294920 | tf_op jit(solution)/shard_map/while/body/eval_jaxpr/ppermute | solution.py:34
  521.9 11.2 %collective-permute-start = (f32[3,8,32,32]{3,2,1,0:T(8,128)S(1)}, f32[3,8,32,32]{3,2,1,0:T(8,128)S(1)}, u32[]{:S(2)}, u32[]{:S(2)}) collective-permute-start(f32[3,8,32,32]{3,2,1,0:T(8,128)S(1)} %add.1080), channel_id=1, source_target_pairs={{0,8},{8,16},{16,24},{24,32},{32,40},{40,48},{48,56},{56,64},{64,7... | collective-permute-start | bytes 294920 | tf_op jit(solution)/shard_map/while/body/eval_jaxpr/ppermute | solution.py:34
  535.7 11.2 %collective-permute-start = (f32[3,8,32,32]{3,2,1,0:T(8,128)S(1)}, f32[3,8,32,32]{3,2,1,0:T(8,128)S(1)}, u32[]{:S(2)}, u32[]{:S(2)}) collective-permute-start(f32[3,8,32,32]{3,2,1,0:T(8,128)S(1)} %add.1080), channel_id=1, source_target_pairs={{0,8},{8,16},{16,24},{24,32},{32,40},{40,48},{48,56},{56,64},{64,7... | collective-permute-start | bytes 294920 | tf_op jit(solution)/shard_map/while/body/eval_jaxpr/ppermute | solution.py:34
  549.6 11.2 %collective-permute-start = (f32[3,8,32,32]{3,2,1,0:T(8,128)S(1)}, f32[3,8,32,32]{3,2,1,0:T(8,128)S(1)}, u32[]{:S(2)}, u32[]{:S(2)}) collective-permute-start(f32[3,8,32,32]{3,2,1,0:T(8,128)S(1)} %add.1080), channel_id=1, source_target_pairs={{0,8},{8,16},{16,24},{24,32},{32,40},{40,48},{48,56},{56,64},{64,7... | collective-permute-start | bytes 294920 | tf_op jit(solution)/shard_map/while/body/eval_jaxpr/ppermute | solution.py:34
  563.4 11.2 %collective-permute-start = (f32[3,8,32,32]{3,2,1,0:T(8,128)S(1)}, f32[3,8,32,32]{3,2,1,0:T(8,128)S(1)}, u32[]{:S(2)}, u32[]{:S(2)}) collective-permute-start(f32[3,8,32,32]{3,2,1,0:T(8,128)S(1)} %add.1080), channel_id=1, source_target_pairs={{0,8},{8,16},{16,24},{24,32},{32,40},{40,48},{48,56},{56,64},{64,7... | collective-permute-start | bytes 294920 | tf_op jit(solution)/shard_map/while/body/eval_jaxpr/ppermute | solution.py:34
  577.3 11.2 %collective-permute-start = (f32[3,8,32,32]{3,2,1,0:T(8,128)S(1)}, f32[3,8,32,32]{3,2,1,0:T(8,128)S(1)}, u32[]{:S(2)}, u32[]{:S(2)}) collective-permute-start(f32[3,8,32,32]{3,2,1,0:T(8,128)S(1)} %add.1080), channel_id=1, source_target_pairs={{0,8},{8,16},{16,24},{24,32},{32,40},{40,48},{48,56},{56,64},{64,7... | collective-permute-start | bytes 294920 | tf_op jit(solution)/shard_map/while/body/eval_jaxpr/ppermute | solution.py:34
  591.1 11.2 %collective-permute-start = (f32[3,8,32,32]{3,2,1,0:T(8,128)S(1)}, f32[3,8,32,32]{3,2,1,0:T(8,128)S(1)}, u32[]{:S(2)}, u32[]{:S(2)}) collective-permute-start(f32[3,8,32,32]{3,2,1,0:T(8,128)S(1)} %add.1080), channel_id=1, source_target_pairs={{0,8},{8,16},{16,24},{24,32},{32,40},{40,48},{48,56},{56,64},{64,7... | collective-permute-start | bytes 294920 | tf_op jit(solution)/shard_map/while/body/eval_jaxpr/ppermute | solution.py:34
  604.9 11.2 %collective-permute-start = (f32[3,8,32,32]{3,2,1,0:T(8,128)S(1)}, f32[3,8,32,32]{3,2,1,0:T(8,128)S(1)}, u32[]{:S(2)}, u32[]{:S(2)}) collective-permute-start(f32[3,8,32,32]{3,2,1,0:T(8,128)S(1)} %add.1080), channel_id=1, source_target_pairs={{0,8},{8,16},{16,24},{24,32},{32,40},{40,48},{48,56},{56,64},{64,7... | collective-permute-start | bytes 294920 | tf_op jit(solution)/shard_map/while/body/eval_jaxpr/ppermute | solution.py:34
  618.8 11.2 %collective-permute-start = (f32[3,8,32,32]{3,2,1,0:T(8,128)S(1)}, f32[3,8,32,32]{3,2,1,0:T(8,128)S(1)}, u32[]{:S(2)}, u32[]{:S(2)}) collective-permute-start(f32[3,8,32,32]{3,2,1,0:T(8,128)S(1)} %add.1080), channel_id=1, source_target_pairs={{0,8},{8,16},{16,24},{24,32},{32,40},{40,48},{48,56},{56,64},{64,7... | collective-permute-start | bytes 294920 | tf_op jit(solution)/shard_map/while/body/eval_jaxpr/ppermute | solution.py:34
  632.6 11.2 %collective-permute-start = (f32[3,8,32,32]{3,2,1,0:T(8,128)S(1)}, f32[3,8,32,32]{3,2,1,0:T(8,128)S(1)}, u32[]{:S(2)}, u32[]{:S(2)}) collective-permute-start(f32[3,8,32,32]{3,2,1,0:T(8,128)S(1)} %add.1080), channel_id=1, source_target_pairs={{0,8},{8,16},{16,24},{24,32},{32,40},{40,48},{48,56},{56,64},{64,7... | collective-permute-start | bytes 294920 | tf_op jit(solution)/shard_map/while/body/eval_jaxpr/ppermute | solution.py:34
  646.4 11.2 %collective-permute-start = (f32[3,8,32,32]{3,2,1,0:T(8,128)S(1)}, f32[3,8,32,32]{3,2,1,0:T(8,128)S(1)}, u32[]{:S(2)}, u32[]{:S(2)}) collective-permute-start(f32[3,8,32,32]{3,2,1,0:T(8,128)S(1)} %add.1080), channel_id=1, source_target_pairs={{0,8},{8,16},{16,24},{24,32},{32,40},{40,48},{48,56},{56,64},{64,7... | collective-permute-start | bytes 294920 | tf_op jit(solution)/shard_map/while/body/eval_jaxpr/ppermute | solution.py:34
  660.3 11.2 %collective-permute-start = (f32[3,8,32,32]{3,2,1,0:T(8,128)S(1)}, f32[3,8,32,32]{3,2,1,0:T(8,128)S(1)}, u32[]{:S(2)}, u32[]{:S(2)}) collective-permute-start(f32[3,8,32,32]{3,2,1,0:T(8,128)S(1)} %add.1080), channel_id=1, source_target_pairs={{0,8},{8,16},{16,24},{24,32},{32,40},{40,48},{48,56},{56,64},{64,7... | collective-permute-start | bytes 294920 | tf_op jit(solution)/shard_map/while/body/eval_jaxpr/ppermute | solution.py:34
  674.1 11.2 %collective-permute-start = (f32[3,8,32,32]{3,2,1,0:T(8,128)S(1)}, f32[3,8,32,32]{3,2,1,0:T(8,128)S(1)}, u32[]{:S(2)}, u32[]{:S(2)}) collective-permute-start(f32[3,8,32,32]{3,2,1,0:T(8,128)S(1)} %add.1080), channel_id=1, source_target_pairs={{0,8},{8,16},{16,24},{24,32},{32,40},{40,48},{48,56},{56,64},{64,7... | collective-permute-start | bytes 294920 | tf_op jit(solution)/shard_map/while/body/eval_jaxpr/ppermute | solution.py:34
  687.9 11.2 %collective-permute-start = (f32[3,8,32,32]{3,2,1,0:T(8,128)S(1)}, f32[3,8,32,32]{3,2,1,0:T(8,128)S(1)}, u32[]{:S(2)}, u32[]{:S(2)}) collective-permute-start(f32[3,8,32,32]{3,2,1,0:T(8,128)S(1)} %add.1080), channel_id=1, source_target_pairs={{0,8},{8,16},{16,24},{24,32},{32,40},{40,48},{48,56},{56,64},{64,7... | collective-permute-start | bytes 294920 | tf_op jit(solution)/shard_map/while/body/eval_jaxpr/ppermute | solution.py:34
  701.8 11.2 %collective-permute-start = (f32[3,8,32,32]{3,2,1,0:T(8,128)S(1)}, f32[3,8,32,32]{3,2,1,0:T(8,128)S(1)}, u32[]{:S(2)}, u32[]{:S(2)}) collective-permute-start(f32[3,8,32,32]{3,2,1,0:T(8,128)S(1)} %add.1080), channel_id=1, source_target_pairs={{0,8},{8,16},{16,24},{24,32},{32,40},{40,48},{48,56},{56,64},{64,7... | collective-permute-start | bytes 294920 | tf_op jit(solution)/shard_map/while/body/eval_jaxpr/ppermute | solution.py:34
  753.3 15.4 %collective-permute-start.17 = (f32[3,4,128,128]{3,2,1,0:T(8,128)S(1)}, f32[3,4,128,128]{3,2,1,0:T(8,128)S(1)}, u32[]{:S(2)}, u32[]{:S(2)}) collective-permute-start(f32[3,4,128,128]{3,2,1,0:T(8,128)S(1)} %broadcast_add_fusion), channel_id=1, source_target_pairs={{0,8},{8,16},{16,24},{24,32},{32,40},{40,48},{48,56},{56,64},{64,7... | collective-permute-start | bytes 2359304 | tf_op jit(solution)/shard_map/ppermute | solution.py:34
  (44 other events, 668.4 us)
where the time goes:
time: 772 us; the launch traced here: 770 us
  waiting for transfers between devices  341 us (44%)
  local copies, waits for them, and re-layouts  156 us (20%)
  starting transfers between devices  105 us (14%)
  other arithmetic  83.1 us (11%)
  blocking collectives  80.3 us (10%)
    ppermute x32, waiting for transfers between devices, shifted(): return lax.ppermute(block, axis, route)  300 us
    concatenate x6, local copies, waits for them, and re-layouts, shards(): coefs = jnp.concatenate([velocity, diffusivity[None], rate[None]], 0)  78.8 us
    ppermute x32, starting transfers between devices, shifted(): return lax.ppermute(block, axis, route)  61.5 us
    add x70, other arithmetic, stencil(): return center + step_dt * (diffuse - advect + react)  53.8 us
    slice x144, local copies, waits for them, and re-layouts, stencil(): x_minus = jnp.roll(center, 1, axis=3)  37.1 us
    ppermute x8, starting transfers between devices, with_halo(): lax.ppermute(tail, axis, [(i, (i + 1) % count) for i in range(ends)])  33.5 us
    all_gather x1, blocking collectives, shards(): lax.all_gather(restrict(slab_state), 'space', axis=1, tiled=True)  29 us
    ppermute x8, waiting for transfers between devices, with_halo(): lax.ppermute(head, axis, [((i + 1) % count, i) for i in range(ends)])  28.7 us
  transfers between devices with their start and end apart: 48, of which 46 were waited for; matrix products, arithmetic and copies ran while one was open for 15% of the time, Pallas kernels for 0%

commit v1 on v0

v1 whole, which is shorter than its diff:
```python
import functools

import jax
import jax.numpy as jnp
import numpy as np
from jax import lax
from jax.experimental import pallas as pl
from jax.experimental.pallas import tpu as pltpu
from jax.sharding import PartitionSpec as P


SPECIES_K = (1.0, 0.6, 0.3)
DECAY = 0.5
FINE_DT = 0.1
COARSE_Q = 0.25
COARSE_DT = 0.4
HALF = 4
VMEM_BYTES = 48 * 1024 * 1024
F32 = jnp.float32
EXACT = lax.Precision.HIGHEST


def coarse_maps(comps):
    x = np.arange(128)
    lane = np.arange(128)
    spread = (x[:, None] // 4 == lane[None, :] // 4).astype(np.float32)
    comp, yv, s = np.meshgrid(np.arange(comps), np.arange(4), np.arange(8), indexing="ij")
    row_to = (comp * 8 + 4 * (s % 2) + yv).reshape(-1)
    fold = (np.arange(comps * 8)[:, None] == row_to[None, :]).astype(np.float32)
    keep = ((s // 2).reshape(-1)[:, None] == lane[None, :] % 4).astype(np.float32)
    return spread, fold, keep


def fold_rows(rows, spread, fold, keep):
    wide = jnp.dot(rows, spread, precision=EXACT, preferred_element_type=F32) * keep
    return jnp.dot(fold, wide, precision=EXACT, preferred_element_type=F32) * (1.0 / 64.0)


def unfold_rows(coarse, spread, fold, keep):
    wide = lax.dot_general(
        fold, coarse, (((0,), (0,)), ((), ())), precision=EXACT, preferred_element_type=F32
    )
    return lax.dot_general(
        wide * keep, spread, (((1,), (1,)), ((), ())), precision=EXACT, preferred_element_type=F32
    )


def block_rows(load, comps):
    out = []
    for comp in range(comps):
        for yv in range(4):
            parts = [load(comp, z, 4 * yv + j) for z in range(4) for j in range(4)]
            while len(parts) > 1:
                parts = [a + b for a, b in zip(parts[::2], parts[1::2])]
            out.append(parts[0])
    return jnp.concatenate(out, 0)


def strided(ref, *lead):
    return lambda v: ref[(*lead, pl.ds(v, 8, stride=16), slice(None))]


def prep_kernel(starts, vel, dif, rate, spread, fold, keep, out):
    def load(comp, z, v):
        if comp < 3:
            return strided(starts, comp, z)(v)
        if comp < 6:
            return strided(vel, comp - 3, z)(v)
        return strided(dif if comp == 6 else rate, z)(v)

    own = fold_rows(block_rows(load, 8), spread[...], fold[...], keep[...])
    for z in range(8):
        out[z] = own


def fine_kernel(native, *refs):
    if native:
        (pos, own, low, high, vel, dif, rate, c_low, c_high, out, cf, buf_a, buf_b) = refs
    else:
        (pos, own, low, high, vel, dif, rate, c_low, c_high, old, spread, fold, keep,
         out, mine, sent, cf, buf_a, buf_b) = refs
    z_at = pos[1]
    has_low = jnp.where(z_at > 0, 1.0, 0.0).astype(F32)
    has_high = jnp.where(z_at < pos[2] - 1, 1.0, 0.0).astype(F32)

    def prepare(plane, loads, scale):
        for v in range(16):
            vx, vy, vz, d, r = [f(v) for f in loads]
            total = None
            for i, w in enumerate((vx, vy, vz)):
                w = w * (FINE_DT * scale)
                up = jnp.maximum(w, 0.0)
                down = up - w
                cf[plane, 2 * i, v] = up
                cf[plane, 2 * i + 1, v] = down
                both = up + down
                total = both if total is None else total + both
            cf[plane, 6, v] = d * (FINE_DT * scale)
            cf[plane, 7, v] = r * (FINE_DT * scale)
            cf[plane, 8, v] = 1.0 - total

    @pl.loop(0, 3)
    def _(z):
        prepare(z, [strided(c_low, c, z) for c in range(5)], has_low)
        prepare(z + 7, [strided(c_high, c, z) for c in range(5)], has_high)

    @pl.loop(0, 4)
    def _(z):
        prepare(z + 3, [strided(vel, c, z) for c in range(3)] + [strided(dif, z), strided(rate, z)], 1.0)

    @pl.loop(0, 4)
    def _(z):
        for src, at, scale in ((low, 0, has_low), (own, 4, None), (high, 8, has_high)):
            for sp in range(3):
                for v in range(16):
                    val = strided(src, sp, z)(v) if native else src[sp, z, v]
                    buf_a[sp, z + at, v] = val if scale is None else val * scale

    def step(src, dst, lo, hi):
        @pl.loop(lo, hi)
        def _(p):
            rows = [[src[sp, p, v] for v in range(16)] for sp in range(3)]
            for v in range(16):
                w = [cf[p - 1, i, v] for i in range(9)]
                d = w[6]
                new = []
                for sp in range(3):
                    u = rows[sp][v]
                    below = rows[sp][v - 1] if v > 0 else pltpu.roll(rows[sp][15], 1, 0)
                    above = rows[sp][v + 1] if v < 15 else pltpu.roll(rows[sp][0], 7, 0)
                    near = (
                        pltpu.roll(u, 1, 1), pltpu.roll(u, 127, 1),
                        below, above,
                        src[sp, p - 1, v], src[sp, p + 1, v],
                    )
                    flow = (w[0] * near[0] + w[1] * near[1]) + (w[2] * near[2] + w[3] * near[3]) + (
                        w[4] * near[4] + w[5] * near[5])
                    lap = (near[0] + near[1]) + (near[2] + near[3]) + (near[4] + near[5])
                    k = SPECIES_K[sp]
                    mid = w[8] - d * (6.0 * k)
                    if sp == 2:
                        mid = mid - FINE_DT * DECAY
                    new.append(mid * u + (d * k if k != 1.0 else d) * lap + flow)
                r = w[7] * rows[0][v] * rows[1][v]
                for sp, val in enumerate((new[0] - r, new[1] - r, new[2] + r)):
                    dst[sp, p, v] = val

    step(buf_a, buf_b, 1, 11)
    step(buf_b, buf_a, 2, 10)
    step(buf_a, buf_b, 3, 9)
    step(buf_b, buf_a, 4, 8)

    if native:
        for sp in range(3):
            out[sp] = buf_a[sp, 4:8]
        return
    part = fold_rows(
        block_rows(lambda sp, z, v: buf_a[sp, 4 + z, v], 3), spread[...], fold[...], keep[...]
    )
    back = unfold_rows(part, spread[...], fold[...], keep[...])
    for sp in range(3):
        for yv in range(4):
            at = (sp * 4 + yv) * 8
            cell = back[at:at + 8]
            for z in range(4):
                for j in range(4):
                    v = 4 * yv + j
                    out[sp, z, v] = buf_a[sp, 4 + z, v] - cell
    mine[...] = part
    here = lax.broadcasted_iota(jnp.int32, (24, 8, 128), 1) == z_at
    before = jnp.sum(jnp.where(here, old[...], 0.0), axis=1)
    diff = part - before
    for z in range(8):
        sent[z] = diff


def coarse_step(load, cf, store):
    lane = lax.broadcasted_iota(jnp.int32, (8, 128), 1) % 4
    rows = [[load(sp, y) for y in range(8)] for sp in range(3)]
    for y in range(8):
        new = []
        for sp in range(3):
            u = rows[sp][y]
            if y > 0:
                below = rows[sp][y - 1]
            else:
                below = jnp.where(lane == 0, pltpu.roll(rows[sp][7], 125, 1), pltpu.roll(rows[sp][7], 1, 1))
            if y < 7:
                above = rows[sp][y + 1]
            else:
                above = jnp.where(lane == 3, pltpu.roll(rows[sp][0], 3, 1), pltpu.roll(rows[sp][0], 127, 1))
            w = [cf[7 * sp + i, y] for i in range(7)]
            val = (w[6] * u + w[2] * below) + (w[3] * above + w[0] * pltpu.roll(u, 4, 1)) + (
                w[1] * pltpu.roll(u, 124, 1) + (w[4] * pltpu.roll(u, 1, 0) + w[5] * pltpu.roll(u, 7, 0)))
            new.append(val)
        r = cf[21, y] * rows[0][y] * rows[1][y]
        store(0, y, new[0] - r)
        store(1, y, new[1] - r)
        store(2, y, new[2] + r)


def old_kernel(pos, got, cf, old, tmp):
    slice_at = pos[0]
    sub = lax.broadcasted_iota(jnp.int32, (8, 128), 0)

    def row(r):
        return got[pl.ds(r, 8, stride=64), :]

    for y in range(8):
        vel = [row(24 + 8 * c + y) * (COARSE_DT * COARSE_Q) for c in range(3)]
        d = row(48 + y) * (COARSE_DT * COARSE_Q * COARSE_Q)
        up = [jnp.maximum(v, 0.0) for v in vel]
        down = [a - v for a, v in zip(up, vel)]
        for sp, k in enumerate(SPECIES_K):
            kd = d * k
            total = 6.0 * kd
            for c in range(3):
                total = total + up[c] + down[c]
                lo, hi = kd + up[c], kd + down[c]
                if c == 2:
                    lo = jnp.where(sub == 0, 0.0, lo)
                    hi = jnp.where(sub == 7, 0.0, hi)
                cf[7 * sp + 2 * c, y] = lo
                cf[7 * sp + 2 * c + 1, y] = hi
            mid = 1.0 - total
            if sp == 2:
                mid = mid - COARSE_DT * DECAY
            cf[7 * sp + 6, y] = mid
        cf[21, y] = row(56 + y) * COARSE_DT

    def put(sp, y, val):
        tmp[8 * sp + y] = val

    def put_old(sp, y, val):
        old[8 * sp + y] = jnp.where(slice_at == 0, 0.0, val)

    coarse_step(lambda sp, y: row(8 * sp + y), cf, put)
    coarse_step(lambda sp, y: tmp[8 * sp + y], cf, put_old)


def chain_kernel(turn, pos, c_in, kept, cf, *refs):
    defects, (c_out, keep, state, tmp, line) = refs[:8], refs[8:]
    group, at_y, core = pos[3], pos[4], pos[5]

    @pl.when(group != turn)
    def _():
        c_out[...] = c_in[...]
        keep[...] = kept[...]

    @pl.when(group == turn)
    def _():
        for k in range(4):
            slot = lax.rem(at_y - k + 4, 4) * 2
            line[slot + core] = defects[k][...]
            line[slot + 1 - core] = defects[4 + k][...]
        state[...] = jnp.zeros_like(state) if turn == 0 else c_in[...]
        own = 2 * at_y + core

        def put(ref):
            def store(sp, y, val):
                ref[8 * sp + y] = val
            return store

        @pl.loop(0, 8)
        def _(i):
            @pl.when(i == own)
            def _():
                keep[0] = state[...]

            def add(sp, y, val):
                r = 8 * sp + y
                state[r] = val + line[i, pl.ds(r, 8, stride=24), :]

            coarse_step(lambda sp, y: state[8 * sp + y], cf, put(tmp))
            coarse_step(lambda sp, y: tmp[8 * sp + y], cf, add)

            @pl.when(i == own)
            def _():
                keep[1] = state[...]

        c_out[...] = state[...]


def last_kernel(pos, ends, arrived, keep_c, starts, spread, fold, keep, new_starts, new_ends):
    z_at, slice_at = pos[1], pos[0]
    here = lax.broadcasted_iota(jnp.int32, (24, 8, 128), 1) == z_at
    for which, src, dst in ((1, ends, new_ends), (0, arrived, new_starts)):
        own = jnp.sum(jnp.where(here, keep_c[which], 0.0), axis=1)
        back = unfold_rows(own, spread[...], fold[...], keep[...])
        for sp in range(3):
            for yv in range(4):
                at = (sp * 4 + yv) * 8
                cell = back[at:at + 8]
                for z in range(4):
                    for j in range(4):
                        v = 4 * yv + j
                        dst[sp, z, pl.ds(v, 8, stride=16), :] = src[sp, z, v] + cell

    @pl.when(slice_at == 0)
    def _():
        new_starts[...] = starts[...]


def call(kernel, outs, scratch, *args, smem=True):
    specs = [pl.BlockSpec(memory_space=pltpu.VMEM)] * len(args)
    if smem:
        specs[0] = pl.BlockSpec(memory_space=pltpu.SMEM)
    return pl.pallas_call(
        kernel,
        out_shape=[jax.ShapeDtypeStruct(s, F32) for s in outs],
        in_specs=specs,
        out_specs=[pl.BlockSpec(memory_space=pltpu.VMEM)] * len(outs),
        scratch_shapes=[pltpu.VMEM(s, F32) for s in scratch],
        compiler_params=pltpu.CompilerParams(vmem_limit_bytes=VMEM_BYTES),
    )(*args)


def over_z(block, shift):
    count = lax.axis_size("space")
    return lax.ppermute(block, "space", [(i, (i + shift) % count) for i in range(count)])


def over_tm(block, move):
    pairs = []
    for i in range(32):
        x, y, c = i // 8, i // 2 % 4, i % 2
        x, y, c = move(x, y, c)
        pairs.append((i, (x % 4) * 8 + (y % 4) * 2 + c))
    return lax.ppermute(block, "tm", pairs)


def shards(starts, velocity, diffusivity, rate):
    slab = starts[0]
    slice_at = lax.axis_index("tm")
    z_at = lax.axis_index("space")
    pos = jnp.stack(
        [slice_at, z_at, lax.axis_size("space"), slice_at // 8, slice_at // 2 % 4, slice_at % 2]
    ).astype(jnp.int32)
    coefs = jnp.concatenate([velocity, diffusivity[None], rate[None]], 0)

    c_low = over_z(coefs[:, 1:], 1)
    c_high = over_z(coefs[:, :3], -1)
    low = over_z(slab, 1)
    high = over_z(slab, -1)

    maps8 = [jnp.asarray(m) for m in coarse_maps(8)]
    maps3 = [jnp.asarray(m) for m in coarse_maps(3)]
    (thin,) = call(prep_kernel, [(8, 64, 128)], [], slab, velocity, diffusivity, rate, *maps8, smem=False)
    full = lax.all_to_all(thin, "space", 0, 0, tiled=True)
    coarse_cf, old = call(
        old_kernel, [(22, 8, 8, 128), (24, 8, 128)], [(24, 8, 128)], pos, full.reshape(512, 128)
    )

    fine_scratch = [(10, 9, 16, 8, 128), (3, 12, 16, 8, 128), (3, 12, 16, 8, 128)]
    (middle,) = call(
        functools.partial(fine_kernel, True), [(3, 4, 16, 8, 128)], fine_scratch,
        pos, slab, low, high, velocity, diffusivity, rate, c_low, c_high,
    )
    low = over_z(middle, 1)
    high = over_z(middle, -1)
    ends, _, diff = call(
        functools.partial(fine_kernel, False),
        [(3, 4, 16, 8, 128), (24, 128), (8, 24, 128)], fine_scratch,
        pos, middle, low, high, velocity, diffusivity, rate, c_low, c_high, old, *maps3,
    )

    arrived = over_tm(ends, lambda x, y, c: (x + (y + c) // 4, y + c, 1 - c))
    defect = lax.all_to_all(diff, "space", 0, 0, tiled=True).reshape(192, 128)
    rows = [defect] + [over_tm(defect, lambda x, y, c, k=k: (x, y + k, c)) for k in (1, 2, 3)]
    rows += [over_tm(r, lambda x, y, c: (x, y, 1 - c)) for r in rows]

    state = jnp.zeros((24, 8, 128), F32)
    kept = jnp.zeros((2, 24, 8, 128), F32)
    for turn in range(4):
        state, kept = call(
            functools.partial(chain_kernel, turn),
            [(24, 8, 128), (2, 24, 8, 128)],
            [(24, 8, 128), (24, 8, 128), (8, 192, 128)],
            pos, state, kept, coarse_cf, *rows,
        )
        if turn < 3:
            state = over_tm(state, lambda x, y, c: (x + 1, y, c))

    new_starts, new_ends = call(
        last_kernel, [(3, 4, 128, 128), (3, 4, 128, 128)], [],
        pos, ends, arrived, kept, slab, *maps3,
    )
    return (new_starts[None], new_ends[None])


def solution(mesh):
    placed = (
        P("tm", None, "space", None, None),
        P(None, "space", None, None),
        P("space", None, None),
        P("space", None, None),
    )
    return jax.shard_map(
        shards,
        mesh=mesh,
        in_specs=placed,
        out_specs=(P("tm", None, "space", None, None), P("tm", None, "space", None, None)),
        check_vma=False,
    )
```

time: 772 us -> 146 us (0.19)
  waiting for transfers between devices: 341 us -> 47.2 us
  local copies, waits for them, and re-layouts: 156 us -> 1.65 us
  other arithmetic: 83.1 us -> 1.41 us
  starting transfers between devices: 105 us -> 29.7 us
  blocking collectives: 80.3 us -> 36.8 us
  Pallas kernels: 0 us -> 27.8 us
    ppermute x48 -> x17, waiting for transfers between devices: 341 us -> 47.2 us  [the longest x6 35.6 us: over_z(): lax.ppermute(block, 'space', [(i, (i + shift) % count) for i in range(cou...]
    all_gather x3 -> x0, blocking collectives: 80.3 us -> none  [the longest x1 29 us: shards(): lax.all_gather(restrict(slab_state), 'space', axis=1, tiled=True)]
    concatenate x6 -> x0, local copies, waits for them, and re-layouts: 78.8 us -> none  [shards(): coefs = jnp.concatenate([velocity, diffusivity[None], rate[None]], 0)]
    ppermute x48 -> x17, starting transfers between devices: 105 us -> 29.7 us  [the longest x11 17.3 us: over_tm(): return lax.ppermute(block, 'tm', pairs)]
    add x102 -> x0, other arithmetic: 55.6 us -> none  [the longest x70 53.8 us: stencil(): return center + step_dt * (diffuse - advect + react)]
    slice x296 -> x1, local copies, waits for them, and re-layouts: 50.1 us -> 1.5 us  [shards(): c_high = over_z(coefs[:, :3], -1)]
    all_to_all x0 -> x2, blocking collectives: none -> 36.8 us  [the longest x1 21.9 us: shards(): full = lax.all_to_all(thin, 'space', 0, 0, tiled=True)]
    pallas_call x0 -> x9, Pallas kernels: none -> 27.8 us  [call(): pl.pallas_call(kernel, out_shape=[jax.ShapeDtypeStruct(s, F32) for s in o...]
  transfers between devices with their start and end apart: 48 -> 17, of which waited for: 46 -> 9; matrix products, arithmetic and copies ran while one was open for 15% -> 0% of each run, Pallas kernels for 0% -> 5%
where the time goes in v1:
time: 146 us; the launch traced here: 145 us
  waiting for transfers between devices  47.2 us (32%)
  blocking collectives  36.8 us (25%)
  starting transfers between devices  29.7 us (20%)
  Pallas kernels  27.8 us (19%)
  local copies, waits for them, and re-layouts  1.65 us (1%)
    ppermute x6, waiting for transfers between devices, over_z(): lax.ppermute(block, 'space', [(i, (i + shift) % count) for i in range(cou...  35.6 us
    pallas_call x9, Pallas kernels, call(): pl.pallas_call(kernel, out_shape=[jax.ShapeDtypeStruct(s, F32) for s in o...  27.8 us
    all_to_all x1, blocking collectives, shards(): full = lax.all_to_all(thin, 'space', 0, 0, tiled=True)  21.9 us
    ppermute x11, starting transfers between devices, over_tm(): return lax.ppermute(block, 'tm', pairs)  17.3 us
    all_to_all x1, blocking collectives, shards(): defect = lax.all_to_all(diff, 'space', 0, 0, tiled=True).reshape(192, 128)  14.8 us
    ppermute x6, starting transfers between devices, over_z(): lax.ppermute(block, 'space', [(i, (i + shift) % count) for i in range(cou...  12.4 us
    ppermute x11, waiting for transfers between devices, over_tm(): return lax.ppermute(block, 'tm', pairs)  11.6 us
  transfers between devices with their start and end apart: 17, of which 9 were waited for; matrix products, arithmetic and copies ran while one was open for 0% of the time, Pallas kernels for 5%

profile of v1, /device:TPU:6, one launch (start us, length us, event | category | flops | bytes accessed | tf_op | source)
XLA Modules:
  0.0 145.4 jit_solution(2805960509051077148)
XLA Ops:
  0.6 1.4 pad_maximum_fusion
  2.1 1.5 %fusion = (f32[5,3,128,128]{3,2,1,0:T(8,128)}, f32[5,3,128,128]{3,2,1,0:T(8,128)}) fusion(f32[5,4,128,128]{3,2,1,0:T(8,128)S(1)} %pad_maximum_fusion), kind=kLoop, calls=%fused_computation.1 | loop fusion | bytes 3932160 | tf_op jit(solution)/shard_map/slice | solution.py:342
  3.6 1.9 %collective-permute-start.2 = (f32[5,3,128,128]{3,2,1,0:T(8,128)}, f32[5,3,128,128]{3,2,1,0:T(8,128)S(1)}, u32[]{:S(2)}, u32[]{:S(2)}) collective-permute-start(f32[5,3,128,128]{3,2,1,0:T(8,128)} %get-tuple-element.29), channel_id=1, source_target_pairs={{0,1},{1,2},{2,3},{3,4},{4,5},{5,6},{6,7},{7,0},{8,9},{9,10},{10,1... | collective-permute-start | bytes 2949128 | tf_op jit(solution)/shard_map/ppermute | solution.py:320
  5.5 3.9 %collective-permute-start.3 = (f32[5,3,128,128]{3,2,1,0:T(8,128)}, f32[5,3,128,128]{3,2,1,0:T(8,128)}, u32[]{:S(2)}, u32[]{:S(2)}) collective-permute-start(f32[5,3,128,128]{3,2,1,0:T(8,128)} %get-tuple-element.28), channel_id=1, source_target_pairs={{0,7},{1,0},{2,1},{3,2},{4,3},{5,4},{6,5},{7,6},{8,15},{9,8},{10,9... | collective-permute-start | bytes 2949128 | tf_op jit(solution)/shard_map/ppermute | solution.py:320
  9.5 3.2 %collective-permute-start.1 = (f32[3,4,128,128]{3,2,1,0:T(8,128)S(1)}, f32[3,4,128,128]{3,2,1,0:T(8,128)}, u32[]{:S(2)}, u32[]{:S(2)}) collective-permute-start(f32[3,4,128,128]{3,2,1,0:T(8,128)S(1)} %bitcast.13), channel_id=1, source_target_pairs={{0,7},{1,0},{2,1},{3,2},{4,3},{5,4},{6,5},{7,6},{8,15},{9,8},{10,9... | collective-permute-start | bytes 2359304 | tf_op jit(solution)/shard_map/ppermute | solution.py:320
  12.8 35.6 %collective-permute-done.refs_2_ = f32[3,4,128,128]{3,2,1,0:T(8,128)} collective-permute-done((f32[3,4,128,128]{3,2,1,0:T(8,128)S(1)}, f32[3,4,128,128]{3,2,1,0:T(8,128)}, u32[]{:S(2)}, u32[]{:S(2)}) %collective-permute-start) | collective-permute-done | bytes 786464 | tf_op jit(solution)/shard_map/ppermute | solution.py:320
  48.4 8.9 %shard_map.113.refs_1_ = f32[3,4,16,8,128]{4,3,2,1,0:T(8,128)S(1)} custom-call(s32[6]{0:T(128)S(1)} %stack.23.refs_0_.pos, f32[3,4,128,128]{3,2,1,0:T(8,128)S(1)} %bitcast.14, f32[3,4,128,128]{3,2,1,0:T(8,128)} %collective-permute-done.refs_2_, f32[3,4,128,128]{3,2,1,0:T(8,128)} %collective-permute-done.1.refs_3_, f32[3,4,128,128]{3,2,1,0:T(8,128)S(1)} %copy-done, ...), custom_call_target="tpu_custom_call" | custom-call | tf_op jit(solution)/shard_map/pallas_call | solution.py:308
  57.4 3.2 %collective-permute-start.5 = (f32[3,4,16,8,128]{4,3,2,1,0:T(8,128)S(1)}, f32[3,4,16,8,128]{4,3,2,1,0:T(8,128)S(1)}, u32[]{:S(2)}, u32[]{:S(2)}) collective-permute-start(f32[3,4,16,8,128]{4,3,2,1,0:T(8,128)S(1)} %shard_map.113.refs_1_), channel_id=1, source_target_pairs={{0,7},{1,0},{2,1},{3,2},{4,3},{5,4},{6,5},{7,6},{8,15},{9,8},{10,9... | collective-permute-start | bytes 2359304 | tf_op jit(solution)/shard_map/ppermute | solution.py:320
  60.7 1.0 shard_map.114
  61.7 21.9 %all_to_all.10 = f32[8,64,128]{2,1,0:T(8,128)S(1)} all-to-all(f32[8,64,128]{2,1,0:T(8,128)S(1)} %shard_map.114), channel_id=1, replica_groups=mesh['tm'=32,'space'=8] {'space'}, dimensions={0} | all-to-all | bytes 524288 | tf_op jit(solution)/shard_map/all_to_all | solution.py:349
  83.7 0.9 shard_map.115
  84.6 9.0 %shard_map.116 = (f32[3,4,16,8,128]{4,3,2,1,0:T(8,128)S(1)}, f32[24,128]{1,0:T(8,128)}, f32[8,24,128]{2,1,0:T(8,128)S(1)}) custom-call(s32[6]{0:T(128)S(1)} %stack.23.refs_0_.pos, f32[3,4,16,8,128]{4,3,2,1,0:T(8,128)S(1)} %shard_map.113.refs_1_, f32[3,4,16,8,128]{4,3,2,1,0:T(8,128)S(1)} %collective-permute-done.4.refs_2_, ...), custom_call_target="tpu_custom_call" | custom-call | tf_op jit(solution)/shard_map/pallas_call | solution.py:308
  93.6 14.8 %all_to_all.11 = f32[8,24,128]{2,1,0:T(8,128)S(1)} all-to-all(f32[8,24,128]{2,1,0:T(8,128)S(1)} %get-tuple-element.18), channel_id=1, replica_groups=mesh['tm'=32,'space'=8] {'space'}, dimensions={0} | all-to-all | bytes 196608 | tf_op jit(solution)/shard_map/all_to_all | solution.py:368
  108.4 1.6 %collective-permute-start.7 = (f32[192,128]{1,0:T(8,128)S(1)}, f32[192,128]{1,0:T(8,128)S(1)}, u32[]{:S(2)}, u32[]{:S(2)}) collective-permute-start(f32[192,128]{1,0:T(8,128)S(1)} %bitcast.19), channel_id=1, source_target_pairs={{0,16},{8,24},{16,32},{24,40},{32,48},{40,56},{48,0},{56,8},{64,80... | collective-permute-start | bytes 294920 | tf_op jit(solution)/shard_map/ppermute | solution.py:329
  110.0 2.1 %collective-permute-start.8 = (f32[192,128]{1,0:T(8,128)S(1)}, f32[192,128]{1,0:T(8,128)S(1)}, u32[]{:S(2)}, u32[]{:S(2)}) collective-permute-start(f32[192,128]{1,0:T(8,128)S(1)} %bitcast.20), channel_id=1, source_target_pairs={{0,32},{8,40},{16,48},{24,56},{32,0},{40,8},{48,16},{56,24},{64,96... | collective-permute-start | bytes 294920 | tf_op jit(solution)/shard_map/ppermute | solution.py:329
  112.1 2.2 %collective-permute-start.9 = (f32[192,128]{1,0:T(8,128)S(1)}, f32[192,128]{1,0:T(8,128)S(1)}, u32[]{:S(2)}, u32[]{:S(2)}) collective-permute-start(f32[192,128]{1,0:T(8,128)S(1)} %bitcast.21), channel_id=1, source_target_pairs={{0,48},{8,56},{16,0},{24,8},{32,16},{40,24},{48,32},{56,40},{64,11... | collective-permute-start | bytes 294920 | tf_op jit(solution)/shard_map/ppermute | solution.py:329
  114.3 0.7 collective-permute-done.7.refs_1_
  115.0 1.9 %collective-permute-done.8.refs_2_ = f32[192,128]{1,0:T(8,128)S(1)} collective-permute-done((f32[192,128]{1,0:T(8,128)S(1)}, f32[192,128]{1,0:T(8,128)S(1)}, u32[]{:S(2)}, u32[]{:S(2)}) %collective-permute-start.8) | collective-permute-done | bytes 98336 | tf_op jit(solution)/shard_map/ppermute | solution.py:329
  116.9 0.4 collective-permute-done.9.refs_3_
  117.4 0.8 collective-permute-done.12.refs_6_
  118.2 0.4 collective-permute-done.13.refs_7_
  118.6 0.6 shard_map.117
  119.1 3.8 %collective-permute-start.14 = (f32[24,8,128]{2,1,0:T(8,128)S(1)}, f32[24,8,128]{2,1,0:T(8,128)S(1)}, u32[]{:S(2)}, u32[]{:S(2)}) collective-permute-start(f32[24,8,128]{2,1,0:T(8,128)S(1)} %get-tuple-element.19), channel_id=1, source_target_pairs={{0,64},{8,72},{16,80},{24,88},{32,96},{40,104},{48,112},{56,120},{... | collective-permute-start | bytes 294920 | tf_op jit(solution)/shard_map/ppermute | solution.py:329
  123.0 2.6 %collective-permute-done.14.c_in = f32[24,8,128]{2,1,0:T(8,128)S(1)} collective-permute-done((f32[24,8,128]{2,1,0:T(8,128)S(1)}, f32[24,8,128]{2,1,0:T(8,128)S(1)}, u32[]{:S(2)}, u32[]{:S(2)}) %collective-permute-start.14) | collective-permute-done | bytes 98336 | tf_op jit(solution)/shard_map/ppermute | solution.py:329
  125.6 0.6 shard_map.118
  126.1 3.8 %collective-permute-start.15 = (f32[24,8,128]{2,1,0:T(8,128)S(1)}, f32[24,8,128]{2,1,0:T(8,128)S(1)}, u32[]{:S(2)}, u32[]{:S(2)}) collective-permute-start(f32[24,8,128]{2,1,0:T(8,128)S(1)} %get-tuple-element.21), channel_id=1, source_target_pairs={{0,64},{8,72},{16,80},{24,88},{32,96},{40,104},{48,112},{56,120},{... | collective-permute-start | bytes 294920 | tf_op jit(solution)/shard_map/ppermute | solution.py:329
  129.9 2.2 %collective-permute-done.15.c_in = f32[24,8,128]{2,1,0:T(8,128)S(1)} collective-permute-done((f32[24,8,128]{2,1,0:T(8,128)S(1)}, f32[24,8,128]{2,1,0:T(8,128)S(1)}, u32[]{:S(2)}, u32[]{:S(2)}) %collective-permute-start.15) | collective-permute-done | bytes 98336 | tf_op jit(solution)/shard_map/ppermute | solution.py:329
  132.1 0.6 shard_map.119
  132.7 3.7 %collective-permute-start.16 = (f32[24,8,128]{2,1,0:T(8,128)S(1)}, f32[24,8,128]{2,1,0:T(8,128)S(1)}, u32[]{:S(2)}, u32[]{:S(2)}) collective-permute-start(f32[24,8,128]{2,1,0:T(8,128)S(1)} %get-tuple-element.23), channel_id=1, source_target_pairs={{0,64},{8,72},{16,80},{24,88},{32,96},{40,104},{48,112},{56,120},{... | collective-permute-start | bytes 294920 | tf_op jit(solution)/shard_map/ppermute | solution.py:329
  136.4 2.8 %collective-permute-done.16.c_in = f32[24,8,128]{2,1,0:T(8,128)S(1)} collective-permute-done((f32[24,8,128]{2,1,0:T(8,128)S(1)}, f32[24,8,128]{2,1,0:T(8,128)S(1)}, u32[]{:S(2)}, u32[]{:S(2)}) %collective-permute-start.16) | collective-permute-done | bytes 98336 | tf_op jit(solution)/shard_map/ppermute | solution.py:329
  139.1 3.6 %shard_map.120 = (f32[24,8,128]{2,1,0:T(8,128)}, f32[2,24,8,128]{3,2,1,0:T(8,128)S(1)}) custom-call(s32[6]{0:T(128)S(1)} %stack.23.refs_0_.pos, f32[24,8,128]{2,1,0:T(8,128)S(1)} %collective-permute-done.16.c_in, f32[2,24,8,128]{3,2,1,0:T(8,128)S(1)} %get-tuple-element.24.kept, f32[22,8,8,128]{3,2,1,0:T(8,128)S(1)} %get-tuple-element.17.cf, ...), custom_call_target="tpu_custom_call" | custom-call | tf_op jit(solution)/shard_map/pallas_call | solution.py:308
  142.8 2.7 %shard_map.121 = (f32[3,4,128,128]{3,2,1,0:T(8,128)}, f32[3,4,128,128]{3,2,1,0:T(8,128)}) custom-call(s32[6]{0:T(128)S(1)} %stack.23.refs_0_.pos, f32[3,4,16,8,128]{4,3,2,1,0:T(8,128)S(1)} %get-tuple-element.16.ends, f32[3,4,16,8,128]{4,3,2,1,0:T(8,128)S(1)} %collective-permute-done.6.arrived, f32[2,24,8,128]{3,2,1,0:T(8,128)S(1)} %get-tuple-element.25.keep_c, ...), custom_call_target="tpu_custom_call" | custom-call | tf_op jit(solution)/shard_map/pallas_call | solution.py:308
  (36 shorter events, 0.4 us)
Async XLA Ops:
  2.0 7.4 %copy-start.1 = (f32[1,3,4,128,128]{4,3,2,1,0:T(8,128)S(1)}, f32[1,3,4,128,128]{4,3,2,1,0:T(8,128)}, u32[]{:S(2)}) copy-start(f32[1,3,4,128,128]{4,3,2,1,0:T(8,128)} %param.10) | copy-start | bytes 2359300
  2.1 46.3 %copy-start = (f32[3,4,128,128]{3,2,1,0:T(8,128)S(1)}, f32[3,4,128,128]{3,2,1,0:T(8,128)}, u32[]{:S(2)}) copy-start(f32[3,4,128,128]{3,2,1,0:T(8,128)} %refs_4_.3) | copy-start | bytes 2359300
  2.1 46.3 %copy-start.2 = (f32[4,128,128]{2,1,0:T(8,128)S(1)}, f32[4,128,128]{2,1,0:T(8,128)}, u32[]{:S(2)}) copy-start(f32[4,128,128]{2,1,0:T(8,128)} %refs_5_.3) | copy-start | bytes 786436
  2.1 46.3 %copy-start.3 = (f32[4,128,128]{2,1,0:T(8,128)S(1)}, f32[4,128,128]{2,1,0:T(8,128)}, u32[]{:S(2)}) copy-start(f32[4,128,128]{2,1,0:T(8,128)} %refs_6_.3) | copy-start | bytes 786436
  3.6 44.8 %collective-permute-start.2 = (f32[5,3,128,128]{3,2,1,0:T(8,128)}, f32[5,3,128,128]{3,2,1,0:T(8,128)S(1)}, u32[]{:S(2)}, u32[]{:S(2)}) collective-permute-start(f32[5,3,128,128]{3,2,1,0:T(8,128)} %get-tuple-element.29), channel_id=1, source_target_pairs={{0,1},{1,2},{2,3},{3,4},{4,5},{5,6},{6,7},{7,0},{8,9},{9,10},{10,1... | collective-permute-start | bytes 2949128 | tf_op jit(solution)/shard_map/ppermute | solution.py:320
  5.5 42.9 %collective-permute-start.3 = (f32[5,3,128,128]{3,2,1,0:T(8,128)}, f32[5,3,128,128]{3,2,1,0:T(8,128)}, u32[]{:S(2)}, u32[]{:S(2)}) collective-permute-start(f32[5,3,128,128]{3,2,1,0:T(8,128)} %get-tuple-element.28), channel_id=1, source_target_pairs={{0,7},{1,0},{2,1},{3,2},{4,3},{5,4},{6,5},{7,6},{8,15},{9,8},{10,9... | collective-permute-start | bytes 2949128 | tf_op jit(solution)/shard_map/ppermute | solution.py:320
  9.5 38.9 %collective-permute-start = (f32[3,4,128,128]{3,2,1,0:T(8,128)S(1)}, f32[3,4,128,128]{3,2,1,0:T(8,128)}, u32[]{:S(2)}, u32[]{:S(2)}) collective-permute-start(f32[3,4,128,128]{3,2,1,0:T(8,128)S(1)} %bitcast.12), channel_id=1, source_target_pairs={{0,1},{1,2},{2,3},{3,4},{4,5},{5,6},{6,7},{7,0},{8,9},{9,10},{10,1... | collective-permute-start | bytes 2359304 | tf_op jit(solution)/shard_map/ppermute | solution.py:320
  9.5 38.9 %collective-permute-start.1 = (f32[3,4,128,128]{3,2,1,0:T(8,128)S(1)}, f32[3,4,128,128]{3,2,1,0:T(8,128)}, u32[]{:S(2)}, u32[]{:S(2)}) collective-permute-start(f32[3,4,128,128]{3,2,1,0:T(8,128)S(1)} %bitcast.13), channel_id=1, source_target_pairs={{0,7},{1,0},{2,1},{3,2},{4,3},{5,4},{6,5},{7,6},{8,15},{9,8},{10,9... | collective-permute-start | bytes 2359304 | tf_op jit(solution)/shard_map/ppermute | solution.py:320
  12.8 47.9 %copy-start.4 = (f32[128,128]{1,0:T(8,128)S(1)}, f32[128,128]{1,0:T(8,128)}, u32[]{:S(2)}) copy-start(f32[128,128]{1,0:T(8,128)} %constant.68.clone.spread.refs_10_) | copy-start | bytes 196612
  12.8 47.9 %copy-start.6 = (f32[256,128]{1,0:T(8,128)S(1)}, f32[256,128]{1,0:T(8,128)}, u32[]{:S(2)}) copy-start(f32[256,128]{1,0:T(8,128)} %constant.70.clone.keep) | copy-start | bytes 393220
  12.8 47.9 %copy-start.7 = (f32[64,256]{1,0:T(8,128)S(1)}, f32[64,256]{1,0:T(8,128)}, u32[]{:S(2)}) copy-start(f32[64,256]{1,0:T(8,128)} %constant.69.clone.fold) | copy-start | bytes 196612
  57.3 27.3 %copy-start.5 = (f32[96,128]{1,0:T(8,128)S(1)}, f32[96,128]{1,0:T(8,128)}, u32[]{:S(2)}) copy-start(f32[96,128]{1,0:T(8,128)} %constant.72.clone.refs_12_.keep) | copy-start | bytes 147460
  57.3 27.3 %copy-start.8 = (f32[24,96]{1,0:T(8,128)S(1)}, f32[24,96]{1,0:T(8,128)}, u32[]{:S(2)}) copy-start(f32[24,96]{1,0:T(8,128)} %constant.71.clone.refs_11_.fold) | copy-start | bytes 27652
  57.4 27.2 %collective-permute-start.4 = (f32[3,4,16,8,128]{4,3,2,1,0:T(8,128)S(1)}, f32[3,4,16,8,128]{4,3,2,1,0:T(8,128)S(1)}, u32[]{:S(2)}, u32[]{:S(2)}) collective-permute-start(f32[3,4,16,8,128]{4,3,2,1,0:T(8,128)S(1)} %shard_map.113.refs_1_), channel_id=1, source_target_pairs={{0,1},{1,2},{2,3},{3,4},{4,5},{5,6},{6,7},{7,0},{8,9},{9,10},{10,1... | collective-permute-start | bytes 2359304 | tf_op jit(solution)/shard_map/ppermute | solution.py:320
  57.4 27.1 %collective-permute-start.5 = (f32[3,4,16,8,128]{4,3,2,1,0:T(8,128)S(1)}, f32[3,4,16,8,128]{4,3,2,1,0:T(8,128)S(1)}, u32[]{:S(2)}, u32[]{:S(2)}) collective-permute-start(f32[3,4,16,8,128]{4,3,2,1,0:T(8,128)S(1)} %shard_map.113.refs_1_), channel_id=1, source_target_pairs={{0,7},{1,0},{2,1},{3,2},{4,3},{5,4},{6,5},{7,6},{8,15},{9,8},{10,9... | collective-permute-start | bytes 2359304 | tf_op jit(solution)/shard_map/ppermute | solution.py:320
  93.6 49.2 %collective-permute-start.6 = (f32[3,4,16,8,128]{4,3,2,1,0:T(8,128)S(1)}, f32[3,4,16,8,128]{4,3,2,1,0:T(8,128)S(1)}, u32[]{:S(2)}, u32[]{:S(2)}) collective-permute-start(f32[3,4,16,8,128]{4,3,2,1,0:T(8,128)S(1)} %get-tuple-element.16.ends), channel_id=1, source_target_pairs={{0,8},{8,16},{16,24},{24,32},{32,40},{40,48},{48,56},{56,64},{64,7... | collective-permute-start | bytes 2359304 | tf_op jit(solution)/shard_map/ppermute | solution.py:329
  108.4 6.5 %collective-permute-start.7 = (f32[192,128]{1,0:T(8,128)S(1)}, f32[192,128]{1,0:T(8,128)S(1)}, u32[]{:S(2)}, u32[]{:S(2)}) collective-permute-start(f32[192,128]{1,0:T(8,128)S(1)} %bitcast.19), channel_id=1, source_target_pairs={{0,16},{8,24},{16,32},{24,40},{32,48},{40,56},{48,0},{56,8},{64,80... | collective-permute-start | bytes 294920 | tf_op jit(solution)/shard_map/ppermute | solution.py:329
  110.0 6.8 %collective-permute-start.8 = (f32[192,128]{1,0:T(8,128)S(1)}, f32[192,128]{1,0:T(8,128)S(1)}, u32[]{:S(2)}, u32[]{:S(2)}) collective-permute-start(f32[192,128]{1,0:T(8,128)S(1)} %bitcast.20), channel_id=1, source_target_pairs={{0,32},{8,40},{16,48},{24,56},{32,0},{40,8},{48,16},{56,24},{64,96... | collective-permute-start | bytes 294920 | tf_op jit(solution)/shard_map/ppermute | solution.py:329
  112.1 5.1 %collective-permute-start.9 = (f32[192,128]{1,0:T(8,128)S(1)}, f32[192,128]{1,0:T(8,128)S(1)}, u32[]{:S(2)}, u32[]{:S(2)}) collective-permute-start(f32[192,128]{1,0:T(8,128)S(1)} %bitcast.21), channel_id=1, source_target_pairs={{0,48},{8,56},{16,0},{24,8},{32,16},{40,24},{48,32},{56,40},{64,11... | collective-permute-start | bytes 294920 | tf_op jit(solution)/shard_map/ppermute | solution.py:329
  114.3 3.1 %collective-permute-start.10 = (f32[192,128]{1,0:T(8,128)S(1)}, f32[192,128]{1,0:T(8,128)S(1)}, u32[]{:S(2)}, u32[]{:S(2)}) collective-permute-start(f32[192,128]{1,0:T(8,128)S(1)} %bitcast.22), channel_id=1, source_target_pairs={{0,8},{8,0},{16,24},{24,16},{32,40},{40,32},{48,56},{56,48},{64,72... | collective-permute-start | bytes 294920 | tf_op jit(solution)/shard_map/ppermute | solution.py:329
  115.0 2.4 %collective-permute-start.11 = (f32[192,128]{1,0:T(8,128)S(1)}, f32[192,128]{1,0:T(8,128)S(1)}, u32[]{:S(2)}, u32[]{:S(2)}) collective-permute-start(f32[192,128]{1,0:T(8,128)S(1)} %collective-permute-done.7.refs_1_), channel_id=1, source_target_pairs={{0,8},{8,0},{16,24},{24,16},{32,40},{40,32},{48,56},{56,48},{64,72... | collective-permute-start | bytes 294920 | tf_op jit(solution)/shard_map/ppermute | solution.py:329
  116.9 1.3 collective-permute-start.12
  117.2 1.3 collective-permute-start.13
  119.1 6.4 %collective-permute-start.14 = (f32[24,8,128]{2,1,0:T(8,128)S(1)}, f32[24,8,128]{2,1,0:T(8,128)S(1)}, u32[]{:S(2)}, u32[]{:S(2)}) collective-permute-start(f32[24,8,128]{2,1,0:T(8,128)S(1)} %get-tuple-element.19), channel_id=1, source_target_pairs={{0,64},{8,72},{16,80},{24,88},{32,96},{40,104},{48,112},{56,120},{... | collective-permute-start | bytes 294920 | tf_op jit(solution)/shard_map/ppermute | solution.py:329
  126.1 6.0 %collective-permute-start.15 = (f32[24,8,128]{2,1,0:T(8,128)S(1)}, f32[24,8,128]{2,1,0:T(8,128)S(1)}, u32[]{:S(2)}, u32[]{:S(2)}) collective-permute-start(f32[24,8,128]{2,1,0:T(8,128)S(1)} %get-tuple-element.21), channel_id=1, source_target_pairs={{0,64},{8,72},{16,80},{24,88},{32,96},{40,104},{48,112},{56,120},{... | collective-permute-start | bytes 294920 | tf_op jit(solution)/shard_map/ppermute | solution.py:329
  132.7 6.5 %collective-permute-start.16 = (f32[24,8,128]{2,1,0:T(8,128)S(1)}, f32[24,8,128]{2,1,0:T(8,128)S(1)}, u32[]{:S(2)}, u32[]{:S(2)}) collective-permute-start(f32[24,8,128]{2,1,0:T(8,128)S(1)} %get-tuple-element.23), channel_id=1, source_target_pairs={{0,64},{8,72},{16,80},{24,88},{32,96},{40,104},{48,112},{56,120},{... | collective-permute-start | bytes 294920 | tf_op jit(solution)/shard_map/ppermute | solution.py:329

commit v2 on v0

v2 whole, which is shorter than its diff:
```python
import functools
from typing import NamedTuple

import jax
import jax.numpy as jnp
from jax import lax
from jax.experimental import pallas as pl
from jax.experimental.pallas import tpu as pltpu
from jax.sharding import PartitionSpec as P


SPECIES_K = (1.0, 0.6, 0.3)
DECAY = 0.5
FINE_DT = 0.1
COARSE_Q = 0.25
COARSE_DT = 0.4
HALF = 4
F32 = jnp.float32
EXACT = lax.Precision.HIGHEST


def coarse_maps(comps):
    def index(shape, axis):
        return lax.broadcasted_iota(jnp.int32, shape, axis)

    def ones(mask):
        return jnp.where(mask, 1.0, 0.0).astype(F32)

    wide, rows = (128, 128), comps * 32
    spread = ones(index(wide, 0) // 4 == index(wide, 1) // 4)
    row = index((comps * 8, rows), 1)
    fold = ones(row // 32 * 8 + row % 2 * 4 + row // 8 % 4 == index((comps * 8, rows), 0))
    keep = ones(index((rows, 128), 0) % 8 // 2 == index((rows, 128), 1) % 4)
    return spread, fold, keep


def fold_rows(rows, spread, fold, keep):
    wide = jnp.dot(rows, spread, precision=EXACT, preferred_element_type=F32) * keep
    return jnp.dot(fold, wide, precision=EXACT, preferred_element_type=F32) * (1.0 / 64.0)


def unfold_rows(coarse, spread, fold, keep):
    wide = lax.dot_general(
        fold, coarse, (((0,), (0,)), ((), ())), precision=EXACT, preferred_element_type=F32
    )
    return lax.dot_general(
        wide * keep, spread, (((1,), (1,)), ((), ())), precision=EXACT, preferred_element_type=F32
    )


def block_rows(load, comps):
    out = []
    for comp in range(comps):
        for yv in range(4):
            parts = [load(comp, z, 4 * yv + j) for z in range(4) for j in range(4)]
            while len(parts) > 1:
                parts = [a + b for a, b in zip(parts[::2], parts[1::2])]
            out.append(parts[0])
    return jnp.concatenate(out, 0)


def strided(ref, *lead):
    return lambda v: ref[(*lead, pl.ds(v, 8, stride=16), slice(None))]


def copy(src, dst, sem):
    moved = pltpu.make_async_copy(src, dst, sem)
    moved.start()
    return moved


def share_kernel(vel, dif, rate, down, up, sem):
    moved = []
    for out, quarter, first in ((down, place().quarters[0], 1), (up, place().quarters[1], 0)):
        rows = pl.ds(pl.multiple_of(quarter * 32, 32), 32)
        planes = pl.ds(first, 3)
        moved.append(copy(vel.at[:, planes, rows], out.at[pl.ds(0, 3)], sem.at[len(moved)]))
        moved.append(copy(dif.at[planes, rows], out.at[3], sem.at[len(moved)]))
        moved.append(copy(rate.at[planes, rows], out.at[4], sem.at[len(moved)]))
    for m in moved:
        m.wait()


def put_coefs(cf, plane, v, raw, scale):
    scaled = [w * scale for w in raw]
    for i, w in enumerate(scaled):
        cf[plane, i, v] = w
    cf[plane, 5, v] = 1.0 - (jnp.abs(scaled[0]) + jnp.abs(scaled[1]) + jnp.abs(scaled[2]))


def coefs_kernel(vel, dif, rate, *refs):
    pieces, (cf, thin, raw, sem) = refs[:8], refs[8:]
    core = place().core
    moved = []
    for side in range(2):
        for j in range(4):
            quarter = place().quarters[side]
            if j in (1, 3):
                quarter = lax.rem(quarter + 2, 4)
            if j >= 2:
                quarter = quarter + 1 - 2 * core
            rows = pl.ds(pl.multiple_of(quarter * 32, 32), 32)
            moved.append(copy(pieces[4 * side + j], raw.at[side, :, :, rows], sem.at[len(moved)]))

    def load(c, z, v):
        if c < 3:
            return strided(vel, c, z)(v)
        return strided(dif if c == 3 else rate, z)(v)

    @pl.loop(0, 4)
    def _(z):
        for v in range(16):
            put_coefs(cf, z + 3, v, [load(c, z, v) for c in range(5)], FINE_DT)

    thin[...] = fold_rows(
        block_rows(lambda c, z, v: cf[z + 3, c, v], 5), *coarse_maps(5)
    ) * (1.0 / FINE_DT)
    for m in moved:
        m.wait()

    has_low, has_high = edges()

    @pl.loop(0, 3)
    def _(z):
        for side, at, scale in ((0, 0, has_low), (1, 7, has_high)):
            for v in range(16):
                put_coefs(cf, z + at, v, [strided(raw, side, c, z)(v) for c in range(5)], FINE_DT * scale)


def pack_kernel(starts, pack):
    part = fold_rows(block_rows(lambda sp, z, v: strided(starts, sp, z)(v), 3), *coarse_maps(3))
    for sp in range(3):
        for z in range(4):
            for v in range(16):
                pack[sp * 64 + z * 16 + v] = strided(starts, sp, z)(v)
        pack[192 + sp] = part[8 * sp:8 * sp + 8]


def gate_kernel(*refs):
    del refs


def fine_cell(load, cf, p, v, dst):
    vel = [cf[p - 1, i, v] for i in range(3)]
    d = cf[p - 1, 3, v]
    base = cf[p - 1, 5, v]
    ahead = [w > 0.0 for w in vel]
    speed = [jnp.abs(w) for w in vel]
    new, old = [], []
    for sp in range(3):
        u = load(sp, p, v)
        old.append(u)
        pairs = (
            (pltpu.roll(u, 1, 1), pltpu.roll(u, 127, 1)),
            (
                load(sp, p, v - 1) if v > 0 else pltpu.roll(load(sp, p, 15), 1, 0),
                load(sp, p, v + 1) if v < 15 else pltpu.roll(load(sp, p, 0), 7, 0),
            ),
            (load(sp, p - 1, v), load(sp, p + 1, v)),
        )
        flow = [s * jnp.where(a, lo_, hi_) for s, a, (lo_, hi_) in zip(speed, ahead, pairs)]
        near = [lo_ + hi_ for lo_, hi_ in pairs]
        k = SPECIES_K[sp]
        mid = base - d * (6.0 * k)
        if sp == 2:
            mid = mid - FINE_DT * DECAY
        lap = (near[0] + near[1]) + near[2]
        new.append((mid * u + (d * k if k != 1.0 else d) * lap) + ((flow[0] + flow[1]) + flow[2]))
    r = cf[p - 1, 4, v] * old[0] * old[1]
    dst[0, p * 16 + v] = new[0] - r
    dst[1, p * 16 + v] = new[1] - r
    dst[2, p * 16 + v] = new[2] + r


def fine_step(src, dst, cf, lo, hi):
    @pl.loop(0, (hi - lo) // 2)
    def _(j):
        for v in range(16):
            for q in range(2):
                fine_cell(lambda sp, p, v: src[sp, p * 16 + v], cf, lo + 2 * j + q, v, dst)


def four_steps(low, own, high, has_low, has_high, buf_a, buf_b, cf):
    def load(sp, p, v):
        if p < 4:
            return low[sp * 64 + p * 16 + v] * has_low
        if p < 8:
            return own[sp * 64 + (p - 4) * 16 + v]
        return high[sp * 64 + (p - 8) * 16 + v] * has_high

    for p in range(1, 11):
        for v in range(16):
            fine_cell(load, cf, p, v, buf_a)
    fine_step(buf_a, buf_b, cf, 2, 10)
    fine_step(buf_b, buf_a, cf, 3, 9)
    fine_step(buf_a, buf_b, cf, 4, 8)


def plane_coefs(thin, y):
    vel = [thin[8 * c + y] * (COARSE_DT * COARSE_Q) for c in range(3)]
    d = thin[24 + y] * (COARSE_DT * COARSE_Q * COARSE_Q)
    up = [jnp.maximum(v, 0.0) for v in vel]
    down = [a - v for a, v in zip(up, vel)]
    out = []
    for sp, k in enumerate(SPECIES_K):
        kd = d * k
        total = 6.0 * kd
        for c in range(3):
            total = total + up[c] + down[c]
            out += [kd + up[c], kd + down[c]]
        out.append(1.0 - total - (COARSE_DT * DECAY if sp == 2 else 0.0))
    return out, thin[32 + y] * COARSE_DT


def coarse_plane_step(state, below, above, thin, has_low, has_high):
    lane = lax.broadcasted_iota(jnp.int32, (8, 128), 1) % 4
    sub = lax.broadcasted_iota(jnp.int32, (8, 128), 0)
    w, react = plane_coefs([thin[8 * c:8 * c + 8] for c in range(5) for _ in range(8)], 0)
    new = []
    for sp in range(3):
        u = state[sp]
        r = pltpu.roll(u, 1, 0)
        y_low = jnp.where(sub == 0, jnp.where(lane == 0, pltpu.roll(r, 125, 1), pltpu.roll(r, 1, 1)), r)
        r = pltpu.roll(u, 7, 0)
        y_high = jnp.where(sub == 7, jnp.where(lane == 3, pltpu.roll(r, 3, 1), pltpu.roll(r, 127, 1)), r)
        near = (pltpu.roll(u, 4, 1), pltpu.roll(u, 124, 1), y_low, y_high, below[sp] * has_low, above[sp] * has_high)
        val = w[7 * sp + 6] * u
        for i in range(6):
            val = val + w[7 * sp + i] * near[i]
        new.append(val)
    r = react * state[0] * state[1]
    return new[0] - r, new[1] - r, new[2] + r


class Place(NamedTuple):
    slice: jax.Array
    z: jax.Array
    group: jax.Array
    y: jax.Array
    core: jax.Array
    quarters: tuple


def place():
    tm = lax.axis_index("tm")
    x, y, core = tm // 8, tm // 2 % 4, tm % 2
    return Place(tm, lax.axis_index("space"), x, y, core, (y % 2 * 2 + core, x % 2 * 2 + core))


def edges():
    z = lax.axis_index("space")
    has_low = jnp.where(z > 0, 1.0, 0.0).astype(F32)
    has_high = jnp.where(z < lax.axis_size("space") - 1, 1.0, 0.0).astype(F32)
    return has_low, has_high


def coarse_rows(pack):
    return [pack[192 + sp] for sp in range(3)]


def first_kernel(thin, own, low, high, cf, out, buf_a, buf_b):
    has_low, has_high = edges()
    four_steps(low, own, high, has_low, has_high, buf_a, buf_b, cf)
    coarse = coarse_plane_step(coarse_rows(own), coarse_rows(low), coarse_rows(high), thin[...], has_low, has_high)
    for sp in range(3):
        out[pl.ds(64 * sp, 64)] = buf_b[sp, 64:128]
        out[192 + sp] = coarse[sp]


def second_kernel(thin, own, low, high, cf, pack, sent, buf_a, buf_b):
    has_low, has_high = edges()
    four_steps(low, own, high, has_low, has_high, buf_a, buf_b, cf)
    part = fold_rows(block_rows(lambda sp, z, v: buf_b[sp, 64 + 16 * z + v], 3), *coarse_maps(3))
    old = coarse_plane_step(coarse_rows(own), coarse_rows(low), coarse_rows(high), thin[...], has_low, has_high)
    first = place().slice == 0
    for sp in range(3):
        own_part = part[8 * sp:8 * sp + 8]
        pack[pl.ds(64 * sp, 64)] = buf_b[sp, 64:128]
        pack[192 + sp] = own_part
        diff = own_part - jnp.where(first, 0.0, old[sp])
        for z in range(8):
            sent[z, 8 * sp:8 * sp + 8] = diff
    for z in range(8):
        sent[z, 24:64] = thin[...]


def coarse_step(load, cf, store):
    lane = lax.broadcasted_iota(jnp.int32, (8, 128), 1) % 4
    rows = [[load(sp, y) for y in range(8)] for sp in range(3)]
    for y in range(8):
        new = []
        for sp in range(3):
            u = rows[sp][y]
            if y > 0:
                below = rows[sp][y - 1]
            else:
                below = jnp.where(lane == 0, pltpu.roll(rows[sp][7], 125, 1), pltpu.roll(rows[sp][7], 1, 1))
            if y < 7:
                above = rows[sp][y + 1]
            else:
                above = jnp.where(lane == 3, pltpu.roll(rows[sp][0], 3, 1), pltpu.roll(rows[sp][0], 127, 1))
            w = [cf[7 * sp + i, y] for i in range(7)]
            val = (w[6] * u + w[2] * below) + (w[3] * above + w[0] * pltpu.roll(u, 4, 1)) + (
                w[1] * pltpu.roll(u, 124, 1) + (w[4] * pltpu.roll(u, 1, 0) + w[5] * pltpu.roll(u, 7, 0)))
            new.append(val)
        r = cf[21, y] * rows[0][y] * rows[1][y]
        store(0, y, new[0] - r)
        store(1, y, new[1] - r)
        store(2, y, new[2] + r)


def own_row(z_at, ref):
    here = lax.broadcasted_iota(jnp.int32, (24, 8, 128), 1) == z_at
    return jnp.sum(jnp.where(here, ref[...], 0.0), axis=1)


def weights_kernel(thin, cf):
    sub = lax.broadcasted_iota(jnp.int32, (8, 128), 0)
    rows = [jnp.concatenate([thin[z, r:r + 1] for z in range(8)], 0) for r in range(40)]
    for y in range(8):
        w, react = plane_coefs(rows, y)
        for i, val in enumerate(w):
            if i % 7 == 4:
                val = jnp.where(sub == 0, 0.0, val)
            if i % 7 == 5:
                val = jnp.where(sub == 7, 0.0, val)
            cf[i, y] = val
        cf[21, y] = react


def run_chain(defects, c_in, cf, keep, state, tmp, line):
    here = place()
    at_y, core = here.y, here.core
    for k in range(4):
        slot = lax.rem(at_y - k + 4, 4) * 2
        line[slot + core] = defects[k][...]
        line[slot + 1 - core] = defects[4 + k][...]
    state[...] = jnp.zeros_like(state) if c_in is None else c_in[...]
    own = 2 * at_y + core

    def put(sp, y, val):
        tmp[8 * sp + y] = val

    @pl.loop(0, 8)
    def _(i):
        @pl.when(i == own)
        def _():
            keep[0] = own_row(here.z, state)

        def add(sp, y, val):
            r = 8 * sp + y
            state[r] = val + line[i, pl.ds(r, 8, stride=24), :]

        coarse_step(lambda sp, y: state[8 * sp + y], cf, put)
        coarse_step(lambda sp, y: tmp[8 * sp + y], cf, add)

        @pl.when(i == own)
        def _():
            keep[1] = own_row(here.z, state)


def chain_kernel(turn, cf, *refs):
    refs = list(refs)
    c_in, kept = (refs.pop(0), refs.pop(0)) if turn else (None, None)
    defects, (c_out, keep, state, tmp, line) = refs[:8], refs[8:]

    @pl.when(place().group != turn)
    def _():
        if turn:
            c_out[...] = c_in[...]
            keep[...] = kept[...]
        else:
            c_out[...] = jnp.zeros_like(c_out)
            keep[...] = jnp.zeros_like(keep)

    @pl.when(place().group == turn)
    def _():
        run_chain(defects, c_in, cf, keep, state, tmp, line)
        c_out[...] = state[...]


def last_kernel(turn, cf, c_in, kept, *refs):
    defects, refs = refs[:8], refs[8:]
    (ends, arrived, starts, new_starts, new_ends,
     keep, state, tmp, line, packs, outs, in_sem, out_sem) = refs
    packed = [copy(arrived, packs.at[0], in_sem.at[0]), copy(ends, packs.at[1], in_sem.at[1])]

    @pl.when(place().group != turn)
    def _():
        keep[...] = kept[...]

    @pl.when(place().group == turn)
    def _():
        run_chain(defects, c_in, cf, keep, state, tmp, line)

    for m in packed:
        m.wait()
    first = place().slice == 0

    @pl.when(first)
    def _():
        copy(starts, outs.at[0], out_sem.at[0]).wait()

    for which in range(2):
        def fill(which=which):
            own = keep[which] - jnp.concatenate([packs[which, 192 + sp] for sp in range(3)], 0)
            back = unfold_rows(own, *coarse_maps(3))
            for sp in range(3):
                for yv in range(4):
                    at = (sp * 4 + yv) * 8
                    cell = back[at:at + 8]
                    for z in range(4):
                        for j in range(4):
                            v = 4 * yv + j
                            outs[which, sp, z, pl.ds(v, 8, stride=16), :] = packs[which, sp * 64 + z * 16 + v] + cell

        if which == 0:
            pl.when(jnp.logical_not(first))(fill)
        else:
            fill()
        copy(outs.at[which], (new_starts, new_ends)[which], out_sem.at[which])
    for which in range(2):
        pltpu.make_async_copy(outs.at[which], (new_starts, new_ends)[which], out_sem.at[which]).wait()


NEAR, FREE = pltpu.VMEM, pl.ANY


def call(kernel, outs, scratch, *args, limit=24, alias=None, cost=2):
    args = [a if isinstance(a, tuple) else (a, NEAR) for a in args]
    return pl.pallas_call(
        kernel,
        out_shape=[jax.ShapeDtypeStruct(s, F32) for s, _ in outs],
        in_specs=[pl.BlockSpec(memory_space=space) for _, space in args],
        out_specs=[pl.BlockSpec(memory_space=space) for _, space in outs],
        scratch_shapes=[
            pltpu.SemaphoreType.DMA((s,)) if isinstance(s, int) else pltpu.VMEM(s, F32) for s in scratch
        ],
        input_output_aliases=alias or {},
        cost_estimate=pl.CostEstimate(flops=0, bytes_accessed=cost * 3_600_000, transcendentals=0),
        compiler_params=pltpu.CompilerParams(vmem_limit_bytes=limit * 1024 * 1024),
    )(*[a for a, _ in args])


def over_z(block, move):
    count = lax.axis_size("space")
    return lax.ppermute(block, "space", [(i, move(i) % count) for i in range(count)])


def both_ways(block):
    return over_z(block, lambda i: i + 1), over_z(block, lambda i: i - 1)


def over_tm(block, move):
    pairs = []
    for i in range(32):
        x, y, c = i // 8, i // 2 % 4, i % 2
        x, y, c = move(x, y, c)
        pairs.append((i, (x % 4) * 8 + (y % 4) * 2 + c))
    return lax.ppermute(block, "tm", pairs)


def shards(starts, velocity, diffusivity, rate):
    slab = starts[0]
    free = lambda *arrays: [(a, FREE) for a in arrays]

    cf_shape, pack_shape, piece_shape = (10, 6, 16, 8, 128), (195, 8, 128), (5, 3, 32, 128)
    down, up = call(
        share_kernel, [(piece_shape, NEAR)] * 2, [6], *free(velocity, diffusivity, rate), limit=60
    )
    c_low = over_z(down, lambda i: i + 1)
    c_high = over_z(up, lambda i: i - 1)
    (own,) = call(pack_kernel, [(pack_shape, NEAR)], [], slab)
    (own,) = call(gate_kernel, [(pack_shape, FREE)], [], *free(own, c_low, c_high), alias={0: 0})
    low, high = both_ways(own)
    swap = lambda block: over_tm(block, lambda x, y, c: (x, y, 1 - c))
    side_low = [c_low, over_tm(c_low, lambda x, y, c: (x, y ^ 1, c))]
    side_high = [c_high, over_tm(c_high, lambda x, y, c: (x ^ 1, y, c))]
    pieces = side_low + [swap(p) for p in side_low] + side_high + [swap(p) for p in side_high]
    cf, thin = call(
        coefs_kernel, [(cf_shape, NEAR), ((40, 128), NEAR)], [(2, 5, 3, 128, 128), 8],
        velocity, diffusivity, rate, *free(*pieces),
    )

    fine_scratch = [(3, 192, 8, 128), (3, 192, 8, 128)]
    (middle,) = call(first_kernel, [(pack_shape, NEAR)], fine_scratch, thin, own, low, high, cf, cost=6)
    low, high = both_ways(middle)
    pack, sent = call(
        second_kernel, [(pack_shape, NEAR), ((8, 64, 128), NEAR)], fine_scratch,
        thin, middle, low, high, cf, cost=6,
    )

    arrived = over_tm(pack, lambda x, y, c: (x + (y + c) // 4, y + c, 1 - c))
    got = lax.all_to_all(sent, "space", 0, 0, tiled=True)
    defect = got[:, :24].reshape(192, 128)
    (coarse_cf,) = call(weights_kernel, [((22, 8, 8, 128), NEAR)], [], got[:, 24:])
    rows = [defect] + [over_tm(defect, lambda x, y, c, k=k: (x, y + k, c)) for k in (1, 2, 3)]
    rows += [swap(r) for r in rows]

    grid = (24, 8, 128)
    chain_scratch = [grid, grid, (8, 192, 128)]
    state = ()
    for turn in range(3):
        out, kept = call(
            functools.partial(chain_kernel, turn), [(grid, NEAR), ((2, 24, 128), NEAR)], chain_scratch,
            coarse_cf, *state, *rows,
        )
        state = (over_tm(out, lambda x, y, c: (x + 1, y, c)), kept)
    new_starts, new_ends = call(
        functools.partial(last_kernel, 3), [((3, 4, 128, 128), FREE)] * 2,
        [(2, 24, 128)] + chain_scratch + [(2, 195, 8, 128), (2, 3, 4, 128, 128), 2, 2],
        coarse_cf, *state, *rows, *free(pack, arrived, slab),
    )
    return (new_starts[None], new_ends[None])


def solution(mesh):
    placed = (
        P("tm", None, "space", None, None),
        P(None, "space", None, None),
        P("space", None, None),
        P("space", None, None),
    )
    return jax.shard_map(
        shards,
        mesh=mesh,
        in_specs=placed,
        out_specs=(P("tm", None, "space", None, None), P("tm", None, "space", None, None)),
        check_vma=False,
    )
```

time: 772 us -> 115 us (0.15)
  waiting for transfers between devices: 341 us -> 53.9 us
  local copies, waits for them, and re-layouts: 156 us -> 1.17 us
  other arithmetic: 83.1 us -> 0 us
  blocking collectives: 80.3 us -> 0 us
  starting transfers between devices: 105 us -> 37.1 us
  Pallas kernels: 0 us -> 21.1 us
    ppermute x48 -> x23, waiting for transfers between devices: 341 us -> 43.5 us  [the longest x6 25.2 us: over_z(): lax.ppermute(block, 'space', [(i, move(i) % count) for i in range(count)])]
    all_gather x3 -> x0, blocking collectives: 80.3 us -> none  [the longest x1 29 us: shards(): lax.all_gather(restrict(slab_state), 'space', axis=1, tiled=True)]
    concatenate x6 -> x0, local copies, waits for them, and re-layouts: 78.8 us -> none  [shards(): coefs = jnp.concatenate([velocity, diffusivity[None], rate[None]], 0)]
    ppermute x48 -> x23, starting transfers between devices: 105 us -> 31.7 us  [the longest x17 19.2 us: over_tm(): return lax.ppermute(block, 'tm', pairs)]
    add x102 -> x0, other arithmetic: 55.6 us -> none  [the longest x70 53.8 us: stencil(): return center + step_dt * (diffuse - advect + react)]
    slice x296 -> x2, local copies, waits for them, and re-layouts: 50.1 us -> 0.02 us  [the longest x1 0.01 us: shards(): got[:, 24:]]
    pallas_call x0 -> x11, Pallas kernels: none -> 21.1 us  [call(): pl.pallas_call(kernel, out_shape=[jax.ShapeDtypeStruct(s, F32) for s, _ i...]
    reduce_sum x2 -> x0, local copies, waits for them, and re-layouts: 16.5 us -> none  [restrict(): return jnp.mean(blocks, axis=(2, 4, 6))]
  transfers between devices with their start and end apart: 48 -> 24, of which waited for: 46 -> 16; matrix products, arithmetic and copies ran while one was open for 15% -> 0% of each run, Pallas kernels for 0% -> 3%
where the time goes in v2:
time: 115 us; the launch traced here: 114 us
  waiting for transfers between devices  53.9 us (47%)
  starting transfers between devices  37.1 us (32%)
  Pallas kernels  21.1 us (18%)
  local copies, waits for them, and re-layouts  1.17 us (1%)
    ppermute x6, waiting for transfers between devices, over_z(): lax.ppermute(block, 'space', [(i, move(i) % count) for i in range(count)])  25.2 us
    pallas_call x11, Pallas kernels, call(): pl.pallas_call(kernel, out_shape=[jax.ShapeDtypeStruct(s, F32) for s, _ i...  21.1 us
    ppermute x17, starting transfers between devices, over_tm(): return lax.ppermute(block, 'tm', pairs)  19.2 us
    ppermute x17, waiting for transfers between devices, over_tm(): return lax.ppermute(block, 'tm', pairs)  18.2 us
    ppermute x6, starting transfers between devices, over_z(): lax.ppermute(block, 'space', [(i, move(i) % count) for i in range(count)])  12.6 us
    all_to_all x1, waiting for transfers between devices, shards(): got = lax.all_to_all(sent, 'space', 0, 0, tiled=True)  10.5 us
    all_to_all x1, starting transfers between devices, shards(): got = lax.all_to_all(sent, 'space', 0, 0, tiled=True)  5.34 us
  transfers between devices with their start and end apart: 24, of which 16 were waited for; matrix products, arithmetic and copies ran while one was open for 0% of the time, Pallas kernels for 3%

profile of v2, /device:TPU:6, one launch (start us, length us, event | category | flops | bytes accessed | tf_op | source)
XLA Modules:
  0.0 114.2 jit_solution(9691268698095794355)
XLA Ops:
  0.7 2.0 %shard_map.59 = (f32[5,3,32,128]{3,2,1,0:T(8,128)}, f32[5,3,32,128]{3,2,1,0:T(8,128)}) custom-call(f32[3,4,128,128]{3,2,1,0:T(8,128)} %vel.3, f32[4,128,128]{2,1,0:T(8,128)} %dif.3, f32[4,128,128]{2,1,0:T(8,128)} %rate.3), custom_call_target="tpu_custom_call" | custom-call | bytes 7200000 | tf_op jit(solution)/shard_map/pallas_call | solution.py:431
  2.6 2.0 %collective-permute-start = (f32[5,3,32,128]{3,2,1,0:T(8,128)}, f32[5,3,32,128]{3,2,1,0:T(8,128)S(1)}, u32[]{:S(2)}, u32[]{:S(2)}) collective-permute-start(f32[5,3,32,128]{3,2,1,0:T(8,128)} %get-tuple-element.16), channel_id=1, source_target_pairs={{0,1},{1,2},{2,3},{3,4},{4,5},{5,6},{6,7},{7,0},{8,9},{9,10},{10,1... | collective-permute-start | bytes 737288 | tf_op jit(solution)/shard_map/ppermute | solution.py:447
  4.6 4.0 %collective-permute-start.4 = (f32[5,3,32,128]{3,2,1,0:T(8,128)}, f32[5,3,32,128]{3,2,1,0:T(8,128)S(1)}, u32[]{:S(2)}, u32[]{:S(2)}) collective-permute-start(f32[5,3,32,128]{3,2,1,0:T(8,128)} %get-tuple-element.17), channel_id=1, source_target_pairs={{0,7},{1,0},{2,1},{3,2},{4,3},{5,4},{6,5},{7,6},{8,15},{9,8},{10,9... | collective-permute-start | bytes 737288 | tf_op jit(solution)/shard_map/ppermute | solution.py:447
  8.7 1.1 copy-done.1
  10.6 4.1 %collective-permute-done.refs_0_.refs_1_ = f32[5,3,32,128]{3,2,1,0:T(8,128)S(1)} collective-permute-done((f32[5,3,32,128]{3,2,1,0:T(8,128)}, f32[5,3,32,128]{3,2,1,0:T(8,128)S(1)}, u32[]{:S(2)}, u32[]{:S(2)}) %collective-permute-start) | collective-permute-done | bytes 245792 | tf_op jit(solution)/shard_map/ppermute | solution.py:447
  14.8 3.2 %collective-permute-start.9 = (f32[195,8,128]{2,1,0:T(8,128)S(1)}, f32[195,8,128]{2,1,0:T(8,128)S(1)}, u32[]{:S(2)}, u32[]{:S(2)}) collective-permute-start(f32[195,8,128]{2,1,0:T(8,128)S(1)} %shard_map.62.own), channel_id=1, source_target_pairs={{0,7},{1,0},{2,1},{3,2},{4,3},{5,4},{6,5},{7,6},{8,15},{9,8},{10,9... | collective-permute-start | bytes 2396168 | tf_op jit(solution)/shard_map/ppermute | solution.py:447
  18.0 1.6 %collective-permute-start.1 = (f32[5,3,32,128]{3,2,1,0:T(8,128)S(1)}, f32[5,3,32,128]{3,2,1,0:T(8,128)S(1)}, u32[]{:S(2)}, u32[]{:S(2)}) collective-permute-start(f32[5,3,32,128]{3,2,1,0:T(8,128)S(1)} %collective-permute-done.refs_0_.refs_1_), channel_id=1, source_target_pairs={{0,16},{8,24},{16,0},{24,8},{32,48},{40,56},{48,32},{56,40},{64,80... | collective-permute-start | bytes 737288 | tf_op jit(solution)/shard_map/ppermute | solution.py:460
  20.4 4.2 %collective-permute-done.1.refs_1_ = f32[5,3,32,128]{3,2,1,0:T(8,128)S(1)} collective-permute-done((f32[5,3,32,128]{3,2,1,0:T(8,128)S(1)}, f32[5,3,32,128]{3,2,1,0:T(8,128)S(1)}, u32[]{:S(2)}, u32[]{:S(2)}) %collective-permute-start.1) | collective-permute-done | bytes 245792 | tf_op jit(solution)/shard_map/ppermute | solution.py:460
  24.6 1.3 %collective-permute-done.5.refs_5_ = f32[5,3,32,128]{3,2,1,0:T(8,128)S(1)} collective-permute-done((f32[5,3,32,128]{3,2,1,0:T(8,128)S(1)}, f32[5,3,32,128]{3,2,1,0:T(8,128)S(1)}, u32[]{:S(2)}, u32[]{:S(2)}) %collective-permute-start.5) | collective-permute-done | bytes 245792 | tf_op jit(solution)/shard_map/ppermute | solution.py:460
  26.4 1.0 collective-permute-done.3.refs_3_
  27.7 2.1 %shard_map.60 = (f32[10,6,16,8,128]{4,3,2,1,0:T(8,128)S(1)}, f32[40,128]{1,0:T(8,128)S(1)}) custom-call(f32[3,4,128,128]{3,2,1,0:T(8,128)S(1)} %copy-done, f32[4,128,128]{2,1,0:T(8,128)S(1)} %copy-done.3, f32[4,128,128]{2,1,0:T(8,128)S(1)} %copy-done.4, f32[5,3,32,128]{3,2,1,0:T(8,128)S(1)} %collective-permute-done.refs_0_.refs_1_, ...), custom_call_target="tpu_custom_call" | custom-call | bytes 7200000 | tf_op jit(solution)/shard_map/pallas_call | solution.py:431
  29.9 5.1 %collective-permute-done.8.low = f32[195,8,128]{2,1,0:T(8,128)S(1)} collective-permute-done((f32[195,8,128]{2,1,0:T(8,128)S(1)}, f32[195,8,128]{2,1,0:T(8,128)S(1)}, u32[]{:S(2)}, u32[]{:S(2)}) %collective-permute-start.8) | collective-permute-done | bytes 798752 | tf_op jit(solution)/shard_map/ppermute | solution.py:447
  35.0 5.0 %shard_map.63.own = f32[195,8,128]{2,1,0:T(8,128)S(1)} custom-call(f32[40,128]{1,0:T(8,128)S(1)} %get-tuple-element.18.thin, f32[195,8,128]{2,1,0:T(8,128)S(1)} %shard_map.62.own, f32[195,8,128]{2,1,0:T(8,128)S(1)} %collective-permute-done.8.low, f32[195,8,128]{2,1,0:T(8,128)S(1)} %collective-permute-done.9.high, f32[10,6,16,8,128]{4,3,2,1,0:T(8,128)S(1)} %get-tuple-element.19.cf), custom_call_target="tpu_custom_call" | custom-call | bytes 21600000 | tf_op jit(solution)/shard_map/pallas_call | solution.py:431
  40.0 1.9 %collective-permute-start.10 = (f32[195,8,128]{2,1,0:T(8,128)S(1)}, f32[195,8,128]{2,1,0:T(8,128)S(1)}, u32[]{:S(2)}, u32[]{:S(2)}) collective-permute-start(f32[195,8,128]{2,1,0:T(8,128)S(1)} %shard_map.63.own), channel_id=1, source_target_pairs={{0,1},{1,2},{2,3},{3,4},{4,5},{5,6},{6,7},{7,0},{8,9},{9,10},{10,1... | collective-permute-start | bytes 2396168 | tf_op jit(solution)/shard_map/ppermute | solution.py:447
  41.9 1.4 %collective-permute-start.11 = (f32[195,8,128]{2,1,0:T(8,128)S(1)}, f32[195,8,128]{2,1,0:T(8,128)S(1)}, u32[]{:S(2)}, u32[]{:S(2)}) collective-permute-start(f32[195,8,128]{2,1,0:T(8,128)S(1)} %shard_map.63.own), channel_id=1, source_target_pairs={{0,7},{1,0},{2,1},{3,2},{4,3},{5,4},{6,5},{7,6},{8,15},{9,8},{10,9... | collective-permute-start | bytes 2396168 | tf_op jit(solution)/shard_map/ppermute | solution.py:447
  43.3 16.0 %collective-permute-done.10.low = f32[195,8,128]{2,1,0:T(8,128)S(1)} collective-permute-done((f32[195,8,128]{2,1,0:T(8,128)S(1)}, f32[195,8,128]{2,1,0:T(8,128)S(1)}, u32[]{:S(2)}, u32[]{:S(2)}) %collective-permute-start.10) | collective-permute-done | bytes 798752 | tf_op jit(solution)/shard_map/ppermute | solution.py:447
  59.3 6.1 %shard_map.64 = (f32[195,8,128]{2,1,0:T(8,128)S(1)}, f32[8,64,128]{2,1,0:T(8,128)}) custom-call(f32[40,128]{1,0:T(8,128)S(1)} %get-tuple-element.18.thin, f32[195,8,128]{2,1,0:T(8,128)S(1)} %shard_map.63.own, f32[195,8,128]{2,1,0:T(8,128)S(1)} %collective-permute-done.10.low, f32[195,8,128]{2,1,0:T(8,128)S(1)} %collective-permute-done.11.high, ...), custom_call_target="tpu_custom_call" | custom-call | bytes 21600000 | tf_op jit(solution)/shard_map/pallas_call | solution.py:431
  65.5 5.3 %all-to-all-start = ((f32[8,64,128]{2,1,0:T(8,128)}), f32[8,64,128]{2,1,0:T(8,128)S(1)}, u32[]{:S(2)}, u32[]{:S(2)}) async-start(f32[8,64,128]{2,1,0:T(8,128)} %get-tuple-element.20), calls=%async_computation | async-start | bytes 524288 | tf_op jit(solution)/shard_map/all_to_all | solution.py:494
  70.8 10.5 %all-to-all-done = f32[8,64,128]{2,1,0:T(8,128)S(1)} async-done(((f32[8,64,128]{2,1,0:T(8,128)}), f32[8,64,128]{2,1,0:T(8,128)S(1)}, u32[]{:S(2)}, u32[]{:S(2)}) %all-to-all-start) | async-done | bytes 262176 | tf_op jit(solution)/shard_map/all_to_all | solution.py:494
  81.3 1.7 %collective-permute-start.12 = (f32[192,128]{1,0:T(8,128)S(1)}, f32[192,128]{1,0:T(8,128)S(1)}, u32[]{:S(2)}, u32[]{:S(2)}) collective-permute-start(f32[192,128]{1,0:T(8,128)S(1)} %bitcast.6), channel_id=1, source_target_pairs={{0,16},{8,24},{16,32},{24,40},{32,48},{40,56},{48,0},{56,8},{64,80... | collective-permute-start | bytes 294920 | tf_op jit(solution)/shard_map/ppermute | solution.py:460
  82.9 2.9 %collective-permute-start.13 = (f32[192,128]{1,0:T(8,128)S(1)}, f32[192,128]{1,0:T(8,128)S(1)}, u32[]{:S(2)}, u32[]{:S(2)}) collective-permute-start(f32[192,128]{1,0:T(8,128)S(1)} %bitcast.7), channel_id=1, source_target_pairs={{0,32},{8,40},{16,48},{24,56},{32,0},{40,8},{48,16},{56,24},{64,96... | collective-permute-start | bytes 294920 | tf_op jit(solution)/shard_map/ppermute | solution.py:460
  85.8 1.3 %collective-permute-start.14 = (f32[192,128]{1,0:T(8,128)S(1)}, f32[192,128]{1,0:T(8,128)S(1)}, u32[]{:S(2)}, u32[]{:S(2)}) collective-permute-start(f32[192,128]{1,0:T(8,128)S(1)} %bitcast.8), channel_id=1, source_target_pairs={{0,48},{8,56},{16,0},{24,8},{32,16},{40,24},{48,32},{56,40},{64,11... | collective-permute-start | bytes 294920 | tf_op jit(solution)/shard_map/ppermute | solution.py:460
  88.0 1.5 %collective-permute-done.13.refs_2_.refs_4_ = f32[192,128]{1,0:T(8,128)S(1)} collective-permute-done((f32[192,128]{1,0:T(8,128)S(1)}, f32[192,128]{1,0:T(8,128)S(1)}, u32[]{:S(2)}, u32[]{:S(2)}) %collective-permute-start.13) | collective-permute-done | bytes 98336 | tf_op jit(solution)/shard_map/ppermute | solution.py:460
  89.5 1.0 collective-permute-done.14.refs_3_.refs_5_
  90.8 1.0 collective-permute-done.18.refs_7_.refs_9_
  91.8 2.9 %collective-permute-start.19 = (f32[24,8,128]{2,1,0:T(8,128)S(1)}, f32[24,8,128]{2,1,0:T(8,128)S(1)}, u32[]{:S(2)}, u32[]{:S(2)}) collective-permute-start(f32[24,8,128]{2,1,0:T(8,128)S(1)} %get-tuple-element.21), channel_id=1, source_target_pairs={{0,64},{8,72},{16,80},{24,88},{32,96},{40,104},{48,112},{56,120},{... | collective-permute-start | bytes 294920 | tf_op jit(solution)/shard_map/ppermute | solution.py:460
  94.6 2.4 %collective-permute-done.19.refs_0_ = f32[24,8,128]{2,1,0:T(8,128)S(1)} collective-permute-done((f32[24,8,128]{2,1,0:T(8,128)S(1)}, f32[24,8,128]{2,1,0:T(8,128)S(1)}, u32[]{:S(2)}, u32[]{:S(2)}) %collective-permute-start.19) | collective-permute-done | bytes 98336 | tf_op jit(solution)/shard_map/ppermute | solution.py:460
  97.0 3.8 %collective-permute-start.20 = (f32[24,8,128]{2,1,0:T(8,128)S(1)}, f32[24,8,128]{2,1,0:T(8,128)S(1)}, u32[]{:S(2)}, u32[]{:S(2)}) collective-permute-start(f32[24,8,128]{2,1,0:T(8,128)S(1)} %get-tuple-element.23), channel_id=1, source_target_pairs={{0,64},{8,72},{16,80},{24,88},{32,96},{40,104},{48,112},{56,120},{... | collective-permute-start | bytes 294920 | tf_op jit(solution)/shard_map/ppermute | solution.py:460
  100.8 2.2 %collective-permute-done.20.refs_0_ = f32[24,8,128]{2,1,0:T(8,128)S(1)} collective-permute-done((f32[24,8,128]{2,1,0:T(8,128)S(1)}, f32[24,8,128]{2,1,0:T(8,128)S(1)}, u32[]{:S(2)}, u32[]{:S(2)}) %collective-permute-start.20) | collective-permute-done | bytes 98336 | tf_op jit(solution)/shard_map/ppermute | solution.py:460
  103.0 3.7 %collective-permute-start.21 = (f32[24,8,128]{2,1,0:T(8,128)S(1)}, f32[24,8,128]{2,1,0:T(8,128)S(1)}, u32[]{:S(2)}, u32[]{:S(2)}) collective-permute-start(f32[24,8,128]{2,1,0:T(8,128)S(1)} %get-tuple-element.25), channel_id=1, source_target_pairs={{0,64},{8,72},{16,80},{24,88},{32,96},{40,104},{48,112},{56,120},{... | collective-permute-start | bytes 294920 | tf_op jit(solution)/shard_map/ppermute | solution.py:460
  106.7 2.5 %collective-permute-done.21.c_in = f32[24,8,128]{2,1,0:T(8,128)S(1)} collective-permute-done((f32[24,8,128]{2,1,0:T(8,128)S(1)}, f32[24,8,128]{2,1,0:T(8,128)S(1)}, u32[]{:S(2)}, u32[]{:S(2)}) %collective-permute-start.21) | collective-permute-done | bytes 98336 | tf_op jit(solution)/shard_map/ppermute | solution.py:460
  109.2 4.9 %shard_map.69 = (f32[3,4,128,128]{3,2,1,0:T(8,128)}, f32[3,4,128,128]{3,2,1,0:T(8,128)}) custom-call(f32[22,8,8,128]{3,2,1,0:T(8,128)S(1)} %shard_map.65.cf, f32[24,8,128]{2,1,0:T(8,128)S(1)} %collective-permute-done.21.c_in, f32[2,24,128]{2,1,0:T(8,128)S(1)} %get-tuple-element.26.kept, f32[192,128]{1,0:T(8,128)S(1)} %bitcast.13, ...), custom_call_target="tpu_custom_call" | custom-call | bytes 7200000 | tf_op jit(solution)/shard_map/pallas_call | solution.py:431
  (39 shorter events, 3.6 us)
Async XLA Ops:
  0.6 27.1 %copy-start = (f32[3,4,128,128]{3,2,1,0:T(8,128)S(1)}, f32[3,4,128,128]{3,2,1,0:T(8,128)}, u32[]{:S(2)}) copy-start(f32[3,4,128,128]{3,2,1,0:T(8,128)} %vel.3) | copy-start | bytes 2359300
  0.6 27.1 %copy-start.3 = (f32[4,128,128]{2,1,0:T(8,128)S(1)}, f32[4,128,128]{2,1,0:T(8,128)}, u32[]{:S(2)}) copy-start(f32[4,128,128]{2,1,0:T(8,128)} %dif.3) | copy-start | bytes 786436
  0.7 27.1 %copy-start.4 = (f32[4,128,128]{2,1,0:T(8,128)S(1)}, f32[4,128,128]{2,1,0:T(8,128)}, u32[]{:S(2)}) copy-start(f32[4,128,128]{2,1,0:T(8,128)} %rate.3) | copy-start | bytes 786436
  2.6 12.1 %collective-permute-start = (f32[5,3,32,128]{3,2,1,0:T(8,128)}, f32[5,3,32,128]{3,2,1,0:T(8,128)S(1)}, u32[]{:S(2)}, u32[]{:S(2)}) collective-permute-start(f32[5,3,32,128]{3,2,1,0:T(8,128)} %get-tuple-element.16), channel_id=1, source_target_pairs={{0,1},{1,2},{2,3},{3,4},{4,5},{5,6},{6,7},{7,0},{8,9},{9,10},{10,1... | collective-permute-start | bytes 737288 | tf_op jit(solution)/shard_map/ppermute | solution.py:447
  4.6 10.1 %collective-permute-start.4 = (f32[5,3,32,128]{3,2,1,0:T(8,128)}, f32[5,3,32,128]{3,2,1,0:T(8,128)S(1)}, u32[]{:S(2)}, u32[]{:S(2)}) collective-permute-start(f32[5,3,32,128]{3,2,1,0:T(8,128)} %get-tuple-element.17), channel_id=1, source_target_pairs={{0,7},{1,0},{2,1},{3,2},{4,3},{5,4},{6,5},{7,6},{8,15},{9,8},{10,9... | collective-permute-start | bytes 737288 | tf_op jit(solution)/shard_map/ppermute | solution.py:447
  8.7 1.1 copy-start.1
  14.7 20.2 %collective-permute-start.8 = (f32[195,8,128]{2,1,0:T(8,128)S(1)}, f32[195,8,128]{2,1,0:T(8,128)S(1)}, u32[]{:S(2)}, u32[]{:S(2)}) collective-permute-start(f32[195,8,128]{2,1,0:T(8,128)S(1)} %shard_map.62.own), channel_id=1, source_target_pairs={{0,1},{1,2},{2,3},{3,4},{4,5},{5,6},{6,7},{7,0},{8,9},{9,10},{10,1... | collective-permute-start | bytes 2396168 | tf_op jit(solution)/shard_map/ppermute | solution.py:447
  14.8 20.2 %collective-permute-start.9 = (f32[195,8,128]{2,1,0:T(8,128)S(1)}, f32[195,8,128]{2,1,0:T(8,128)S(1)}, u32[]{:S(2)}, u32[]{:S(2)}) collective-permute-start(f32[195,8,128]{2,1,0:T(8,128)S(1)} %shard_map.62.own), channel_id=1, source_target_pairs={{0,7},{1,0},{2,1},{3,2},{4,3},{5,4},{6,5},{7,6},{8,15},{9,8},{10,9... | collective-permute-start | bytes 2396168 | tf_op jit(solution)/shard_map/ppermute | solution.py:447
  18.0 6.6 %collective-permute-start.1 = (f32[5,3,32,128]{3,2,1,0:T(8,128)S(1)}, f32[5,3,32,128]{3,2,1,0:T(8,128)S(1)}, u32[]{:S(2)}, u32[]{:S(2)}) collective-permute-start(f32[5,3,32,128]{3,2,1,0:T(8,128)S(1)} %collective-permute-done.refs_0_.refs_1_), channel_id=1, source_target_pairs={{0,16},{8,24},{16,0},{24,8},{32,48},{40,56},{48,32},{56,40},{64,80... | collective-permute-start | bytes 737288 | tf_op jit(solution)/shard_map/ppermute | solution.py:460
  19.6 6.3 %collective-permute-start.5 = (f32[5,3,32,128]{3,2,1,0:T(8,128)S(1)}, f32[5,3,32,128]{3,2,1,0:T(8,128)S(1)}, u32[]{:S(2)}, u32[]{:S(2)}) collective-permute-start(f32[5,3,32,128]{3,2,1,0:T(8,128)S(1)} %collective-permute-done.4.refs_4_.refs_2_), channel_id=1, source_target_pairs={{0,64},{8,72},{16,80},{24,88},{32,96},{40,104},{48,112},{56,120},{... | collective-permute-start | bytes 737288 | tf_op jit(solution)/shard_map/ppermute | solution.py:460
  20.4 5.5 %collective-permute-start.2 = (f32[5,3,32,128]{3,2,1,0:T(8,128)S(1)}, f32[5,3,32,128]{3,2,1,0:T(8,128)S(1)}, u32[]{:S(2)}, u32[]{:S(2)}) collective-permute-start(f32[5,3,32,128]{3,2,1,0:T(8,128)S(1)} %collective-permute-done.refs_0_.refs_1_), channel_id=1, source_target_pairs={{0,8},{8,0},{16,24},{24,16},{32,40},{40,32},{48,56},{56,48},{64,72... | collective-permute-start | bytes 737288 | tf_op jit(solution)/shard_map/ppermute | solution.py:460
  24.6 1.8 %collective-permute-start.6 = (f32[5,3,32,128]{3,2,1,0:T(8,128)S(1)}, f32[5,3,32,128]{3,2,1,0:T(8,128)S(1)}, u32[]{:S(2)}, u32[]{:S(2)}) collective-permute-start(f32[5,3,32,128]{3,2,1,0:T(8,128)S(1)} %collective-permute-done.4.refs_4_.refs_2_), channel_id=1, source_target_pairs={{0,8},{8,0},{16,24},{24,16},{32,40},{40,32},{48,56},{56,48},{64,72... | collective-permute-start | bytes 737288 | tf_op jit(solution)/shard_map/ppermute | solution.py:460
  25.9 1.5 %collective-permute-start.3 = (f32[5,3,32,128]{3,2,1,0:T(8,128)S(1)}, f32[5,3,32,128]{3,2,1,0:T(8,128)S(1)}, u32[]{:S(2)}, u32[]{:S(2)}) collective-permute-start(f32[5,3,32,128]{3,2,1,0:T(8,128)S(1)} %collective-permute-done.1.refs_1_), channel_id=1, source_target_pairs={{0,8},{8,0},{16,24},{24,16},{32,40},{40,32},{48,56},{56,48},{64,72... | collective-permute-start | bytes 737288 | tf_op jit(solution)/shard_map/ppermute | solution.py:460
  25.9 1.9 %collective-permute-start.7 = (f32[5,3,32,128]{3,2,1,0:T(8,128)S(1)}, f32[5,3,32,128]{3,2,1,0:T(8,128)S(1)}, u32[]{:S(2)}, u32[]{:S(2)}) collective-permute-start(f32[5,3,32,128]{3,2,1,0:T(8,128)S(1)} %collective-permute-done.5.refs_5_), channel_id=1, source_target_pairs={{0,8},{8,0},{16,24},{24,16},{32,40},{40,32},{48,56},{56,48},{64,72... | collective-permute-start | bytes 737288 | tf_op jit(solution)/shard_map/ppermute | solution.py:460
  40.0 19.4 %collective-permute-start.10 = (f32[195,8,128]{2,1,0:T(8,128)S(1)}, f32[195,8,128]{2,1,0:T(8,128)S(1)}, u32[]{:S(2)}, u32[]{:S(2)}) collective-permute-start(f32[195,8,128]{2,1,0:T(8,128)S(1)} %shard_map.63.own), channel_id=1, source_target_pairs={{0,1},{1,2},{2,3},{3,4},{4,5},{5,6},{6,7},{7,0},{8,9},{9,10},{10,1... | collective-permute-start | bytes 2396168 | tf_op jit(solution)/shard_map/ppermute | solution.py:447
  41.9 17.5 %collective-permute-start.11 = (f32[195,8,128]{2,1,0:T(8,128)S(1)}, f32[195,8,128]{2,1,0:T(8,128)S(1)}, u32[]{:S(2)}, u32[]{:S(2)}) collective-permute-start(f32[195,8,128]{2,1,0:T(8,128)S(1)} %shard_map.63.own), channel_id=1, source_target_pairs={{0,7},{1,0},{2,1},{3,2},{4,3},{5,4},{6,5},{7,6},{8,15},{9,8},{10,9... | collective-permute-start | bytes 2396168 | tf_op jit(solution)/shard_map/ppermute | solution.py:447
  65.5 43.7 %copy-start.2 = (f32[1,3,4,128,128]{4,3,2,1,0:T(8,128)S(1)}, f32[1,3,4,128,128]{4,3,2,1,0:T(8,128)}, u32[]{:S(2)}) copy-start(f32[1,3,4,128,128]{4,3,2,1,0:T(8,128)} %param.4) | copy-start | bytes 2359300
  65.5 15.8 %all-to-all-start = ((f32[8,64,128]{2,1,0:T(8,128)}), f32[8,64,128]{2,1,0:T(8,128)S(1)}, u32[]{:S(2)}, u32[]{:S(2)}) async-start(f32[8,64,128]{2,1,0:T(8,128)} %get-tuple-element.20), calls=%async_computation | async-start | bytes 524288 | tf_op jit(solution)/shard_map/all_to_all | solution.py:494
  70.8 35.9 %collective-permute-start.22 = (f32[195,8,128]{2,1,0:T(8,128)S(1)}, f32[195,8,128]{2,1,0:T(8,128)S(1)}, u32[]{:S(2)}, u32[]{:S(2)}) collective-permute-start(f32[195,8,128]{2,1,0:T(8,128)S(1)} %get-tuple-element.27.refs_8_), channel_id=1, source_target_pairs={{0,8},{8,16},{16,24},{24,32},{32,40},{40,48},{48,56},{56,64},{64,7... | collective-permute-start | bytes 2396168 | tf_op jit(solution)/shard_map/ppermute | solution.py:460
  81.3 6.7 %collective-permute-start.12 = (f32[192,128]{1,0:T(8,128)S(1)}, f32[192,128]{1,0:T(8,128)S(1)}, u32[]{:S(2)}, u32[]{:S(2)}) collective-permute-start(f32[192,128]{1,0:T(8,128)S(1)} %bitcast.6), channel_id=1, source_target_pairs={{0,16},{8,24},{16,32},{24,40},{32,48},{40,56},{48,0},{56,8},{64,80... | collective-permute-start | bytes 294920 | tf_op jit(solution)/shard_map/ppermute | solution.py:460
  82.9 6.5 %collective-permute-start.13 = (f32[192,128]{1,0:T(8,128)S(1)}, f32[192,128]{1,0:T(8,128)S(1)}, u32[]{:S(2)}, u32[]{:S(2)}) collective-permute-start(f32[192,128]{1,0:T(8,128)S(1)} %bitcast.7), channel_id=1, source_target_pairs={{0,32},{8,40},{16,48},{24,56},{32,0},{40,8},{48,16},{56,24},{64,96... | collective-permute-start | bytes 294920 | tf_op jit(solution)/shard_map/ppermute | solution.py:460
  85.8 4.6 %collective-permute-start.14 = (f32[192,128]{1,0:T(8,128)S(1)}, f32[192,128]{1,0:T(8,128)S(1)}, u32[]{:S(2)}, u32[]{:S(2)}) collective-permute-start(f32[192,128]{1,0:T(8,128)S(1)} %bitcast.8), channel_id=1, source_target_pairs={{0,48},{8,56},{16,0},{24,8},{32,16},{40,24},{48,32},{56,40},{64,11... | collective-permute-start | bytes 294920 | tf_op jit(solution)/shard_map/ppermute | solution.py:460
  87.2 3.5 %collective-permute-start.15 = (f32[192,128]{1,0:T(8,128)S(1)}, f32[192,128]{1,0:T(8,128)S(1)}, u32[]{:S(2)}, u32[]{:S(2)}) collective-permute-start(f32[192,128]{1,0:T(8,128)S(1)} %bitcast.9), channel_id=1, source_target_pairs={{0,8},{8,0},{16,24},{24,16},{32,40},{40,32},{48,56},{56,48},{64,72... | collective-permute-start | bytes 294920 | tf_op jit(solution)/shard_map/ppermute | solution.py:460
  87.9 2.7 %collective-permute-start.16 = (f32[192,128]{1,0:T(8,128)S(1)}, f32[192,128]{1,0:T(8,128)S(1)}, u32[]{:S(2)}, u32[]{:S(2)}) collective-permute-start(f32[192,128]{1,0:T(8,128)S(1)} %collective-permute-done.12.refs_1_.refs_3_), channel_id=1, source_target_pairs={{0,8},{8,0},{16,24},{24,16},{32,40},{40,32},{48,56},{56,48},{64,72... | collective-permute-start | bytes 294920 | tf_op jit(solution)/shard_map/ppermute | solution.py:460
  89.5 1.3 %collective-permute-start.17 = (f32[192,128]{1,0:T(8,128)S(1)}, f32[192,128]{1,0:T(8,128)S(1)}, u32[]{:S(2)}, u32[]{:S(2)}) collective-permute-start(f32[192,128]{1,0:T(8,128)S(1)} %collective-permute-done.13.refs_2_.refs_4_), channel_id=1, source_target_pairs={{0,8},{8,0},{16,24},{24,16},{32,40},{40,32},{48,56},{56,48},{64,72... | collective-permute-start | bytes 294920 | tf_op jit(solution)/shard_map/ppermute | solution.py:460
  90.5 1.3 %collective-permute-start.18 = (f32[192,128]{1,0:T(8,128)S(1)}, f32[192,128]{1,0:T(8,128)S(1)}, u32[]{:S(2)}, u32[]{:S(2)}) collective-permute-start(f32[192,128]{1,0:T(8,128)S(1)} %collective-permute-done.14.refs_3_.refs_5_), channel_id=1, source_target_pairs={{0,8},{8,0},{16,24},{24,16},{32,40},{40,32},{48,56},{56,48},{64,72... | collective-permute-start | bytes 294920 | tf_op jit(solution)/shard_map/ppermute | solution.py:460
  91.8 5.2 %collective-permute-start.19 = (f32[24,8,128]{2,1,0:T(8,128)S(1)}, f32[24,8,128]{2,1,0:T(8,128)S(1)}, u32[]{:S(2)}, u32[]{:S(2)}) collective-permute-start(f32[24,8,128]{2,1,0:T(8,128)S(1)} %get-tuple-element.21), channel_id=1, source_target_pairs={{0,64},{8,72},{16,80},{24,88},{32,96},{40,104},{48,112},{56,120},{... | collective-permute-start | bytes 294920 | tf_op jit(solution)/shard_map/ppermute | solution.py:460
  97.0 6.0 %collective-permute-start.20 = (f32[24,8,128]{2,1,0:T(8,128)S(1)}, f32[24,8,128]{2,1,0:T(8,128)S(1)}, u32[]{:S(2)}, u32[]{:S(2)}) collective-permute-start(f32[24,8,128]{2,1,0:T(8,128)S(1)} %get-tuple-element.23), channel_id=1, source_target_pairs={{0,64},{8,72},{16,80},{24,88},{32,96},{40,104},{48,112},{56,120},{... | collective-permute-start | bytes 294920 | tf_op jit(solution)/shard_map/ppermute | solution.py:460
  103.0 6.2 %collective-permute-start.21 = (f32[24,8,128]{2,1,0:T(8,128)S(1)}, f32[24,8,128]{2,1,0:T(8,128)S(1)}, u32[]{:S(2)}, u32[]{:S(2)}) collective-permute-start(f32[24,8,128]{2,1,0:T(8,128)S(1)} %get-tuple-element.25), channel_id=1, source_target_pairs={{0,64},{8,72},{16,80},{24,88},{32,96},{40,104},{48,112},{56,120},{... | collective-permute-start | bytes 294920 | tf_op jit(solution)/shard_map/ppermute | solution.py:460

commit v3 on v2

v3 whole, which is shorter than its diff:
```python
import functools
from typing import NamedTuple

import jax
import jax.numpy as jnp
from jax import lax
from jax.experimental import pallas as pl
from jax.experimental.pallas import tpu as pltpu
from jax.sharding import PartitionSpec as P


SPECIES_K = (1.0, 0.6, 0.3)
DECAY = 0.5
FINE_DT = 0.1
COARSE_Q = 0.25
COARSE_DT = 0.4
HALF = 4
F32 = jnp.float32
EXACT = lax.Precision.HIGHEST


def coarse_maps(comps):
    def index(shape, axis):
        return lax.broadcasted_iota(jnp.int32, shape, axis)

    def ones(mask):
        return jnp.where(mask, 1.0, 0.0).astype(F32)

    wide, rows = (128, 128), comps * 32
    spread = ones(index(wide, 0) // 4 == index(wide, 1) // 4)
    row = index((comps * 8, rows), 1)
    fold = ones(row // 32 * 8 + row % 2 * 4 + row // 8 % 4 == index((comps * 8, rows), 0))
    keep = ones(index((rows, 128), 0) % 8 // 2 == index((rows, 128), 1) % 4)
    return spread, fold, keep


def fold_rows(rows, spread, fold, keep):
    wide = jnp.dot(rows, spread, precision=EXACT, preferred_element_type=F32) * keep
    return jnp.dot(fold, wide, precision=EXACT, preferred_element_type=F32) * (1.0 / 64.0)


def unfold_rows(coarse, spread, fold, keep):
    wide = lax.dot_general(
        fold, coarse, (((0,), (0,)), ((), ())), precision=EXACT, preferred_element_type=F32
    )
    return lax.dot_general(
        wide * keep, spread, (((1,), (1,)), ((), ())), precision=EXACT, preferred_element_type=F32
    )


def block_rows(load, comps):
    out = []
    for comp in range(comps):
        for yv in range(4):
            parts = [load(comp, z, 4 * yv + j) for z in range(4) for j in range(4)]
            while len(parts) > 1:
                parts = [a + b for a, b in zip(parts[::2], parts[1::2])]
            out.append(parts[0])
    return jnp.concatenate(out, 0)


def strided(ref, *lead):
    return lambda v: ref[(*lead, pl.ds(v, 8, stride=16), slice(None))]


def copy(src, dst, sem):
    moved = pltpu.make_async_copy(src, dst, sem)
    moved.start()
    return moved


def odd_slab():
    return lax.rem(lax.axis_index("space"), 2)


def share_kernel(vel, dif, rate, first, second, sem):
    moved = []
    for out, quarter, to_next in ((first, place().quarters[0], odd_slab() == 0), (second, place().quarters[1], odd_slab() == 1)):
        rows = pl.ds(pl.multiple_of(quarter * 32, 32), 32)
        planes = pl.ds(jnp.where(to_next, 1, 0), 3)
        moved.append(copy(vel.at[:, planes, rows], out.at[pl.ds(0, 3)], sem.at[len(moved)]))
        moved.append(copy(dif.at[planes, rows], out.at[3], sem.at[len(moved)]))
        moved.append(copy(rate.at[planes, rows], out.at[4], sem.at[len(moved)]))
    for m in moved:
        m.wait()


def put_coefs(cf, plane, v, raw, scale):
    vel = [w * scale for w in raw[:3]]
    base = 1.0 - (jnp.abs(vel[0]) + jnp.abs(vel[1]) + jnp.abs(vel[2]))
    d = raw[3] * scale
    cf[plane, 3, v] = d
    cf[plane, 4, v] = raw[4] * scale
    for i in range(3):
        cf[plane, i, v] = vel[i]
        cf[plane, 5 + i, v] = base - d * (6.0 * SPECIES_K[i]) - (FINE_DT * DECAY if i == 2 else 0.0)


def coefs_kernel(vel, dif, rate, *refs):
    pieces, (cf, thin, part, raw, sem) = refs[:8], refs[8:]
    core = place().core
    moved = []
    for pair in range(2):
        side = 1 - odd_slab() if pair == 0 else odd_slab()
        for j in range(4):
            quarter = place().quarters[pair]
            if j in (1, 3):
                quarter = lax.rem(quarter + 2, 4)
            if j >= 2:
                quarter = quarter + 1 - 2 * core
            rows = pl.ds(pl.multiple_of(quarter * 32, 32), 32)
            moved.append(copy(pieces[4 * pair + j], raw.at[side, :, :, rows], sem.at[len(moved)]))

    def load(c, z, v):
        if c < 3:
            return strided(vel, c, z)(v)
        return strided(dif if c == 3 else rate, z)(v)

    @pl.loop(0, 4)
    def _(z):
        for v in range(16):
            put_coefs(cf, z + 3, v, [load(c, z, v) for c in range(5)], FINE_DT)

    thin[...] = fold_rows(
        block_rows(lambda c, z, v: cf[z + 3, c, v], 5), *coarse_maps(5)
    ) * (1.0 / FINE_DT)
    own = place().y * 2 + core
    rows = jnp.zeros((5, 128), F32)
    for k in range(8):
        rows = jnp.where(own == k, thin[5 * k:5 * k + 5], rows)
    part[...] = jnp.concatenate([rows, jnp.zeros((3, 128), F32)], 0)
    for m in moved:
        m.wait()

    has_low, has_high = edges()

    @pl.loop(0, 3)
    def _(z):
        for side, at, scale in ((0, 0, has_low), (1, 7, has_high)):
            for v in range(16):
                put_coefs(cf, z + at, v, [strided(raw, side, c, z)(v) for c in range(5)], FINE_DT * scale)


def pack_kernel(starts, pack):
    part = fold_rows(block_rows(lambda sp, z, v: strided(starts, sp, z)(v), 3), *coarse_maps(3))
    for sp in range(3):
        for z in range(4):
            for v in range(16):
                pack[sp * 64 + z * 16 + v] = strided(starts, sp, z)(v)
        pack[192 + sp] = part[8 * sp:8 * sp + 8]


def gate_kernel(*refs):
    del refs


def fine_cell(load, cf, p, v, dst):
    vel = [cf[p - 1, i, v] for i in range(3)]
    d = cf[p - 1, 3, v]
    ahead = [w > 0.0 for w in vel]
    speed = [jnp.abs(w) for w in vel]
    new, old = [], []
    for sp in range(3):
        u = load(sp, p, v)
        old.append(u)
        pairs = (
            (pltpu.roll(u, 1, 1), pltpu.roll(u, 127, 1)),
            (
                load(sp, p, v - 1) if v > 0 else pltpu.roll(load(sp, p, 15), 1, 0),
                load(sp, p, v + 1) if v < 15 else pltpu.roll(load(sp, p, 0), 7, 0),
            ),
            (load(sp, p - 1, v), load(sp, p + 1, v)),
        )
        flow = [s * jnp.where(a, lo_, hi_) for s, a, (lo_, hi_) in zip(speed, ahead, pairs)]
        near = [lo_ + hi_ for lo_, hi_ in pairs]
        lap = (near[0] + near[1]) + near[2]
        new.append((cf[p - 1, 5 + sp, v] * u + (d if sp == 0 else d * SPECIES_K[sp]) * lap) + ((flow[0] + flow[1]) + flow[2]))
    r = cf[p - 1, 4, v] * old[0] * old[1]
    dst[0, p * 16 + v] = new[0] - r
    dst[1, p * 16 + v] = new[1] - r
    dst[2, p * 16 + v] = new[2] + r


def fine_step(load, cf, lo, hi, dst):
    for v in range(16):
        for p in range(lo, hi):
            fine_cell(load, cf, p, v, dst)


def four_steps(load, buf_a, buf_b, cf):
    has_low, has_high = edges()

    def masked(sp, p, v):
        val = load(sp, p, v)
        return val * has_low if p < 4 else val * has_high if p >= 8 else val

    def held(buf):
        return lambda sp, p, v: buf[sp, p * 16 + v]

    fine_step(masked, cf, 1, 11, buf_a)
    fine_step(held(buf_a), cf, 2, 10, buf_b)
    fine_step(held(buf_b), cf, 3, 9, buf_a)
    fine_step(held(buf_a), cf, 4, 8, buf_b)


def plane_coefs(thin, y):
    vel = [thin[8 * c + y] * (COARSE_DT * COARSE_Q) for c in range(3)]
    d = thin[24 + y] * (COARSE_DT * COARSE_Q * COARSE_Q)
    up = [jnp.maximum(v, 0.0) for v in vel]
    down = [a - v for a, v in zip(up, vel)]
    out = []
    for sp, k in enumerate(SPECIES_K):
        kd = d * k
        total = 6.0 * kd
        for c in range(3):
            total = total + up[c] + down[c]
            out += [kd + up[c], kd + down[c]]
        out.append(1.0 - total - (COARSE_DT * DECAY if sp == 2 else 0.0))
    return out, thin[32 + y] * COARSE_DT


def coarse_plane_step(state, below, above, thin):
    has_low, has_high = edges()
    lane = lax.broadcasted_iota(jnp.int32, (8, 128), 1) % 4
    sub = lax.broadcasted_iota(jnp.int32, (8, 128), 0)
    w, react = plane_coefs([thin[8 * c:8 * c + 8] for c in range(5) for _ in range(8)], 0)
    new = []
    for sp in range(3):
        u = state[sp]
        r = pltpu.roll(u, 1, 0)
        y_low = jnp.where(sub == 0, jnp.where(lane == 0, pltpu.roll(r, 125, 1), pltpu.roll(r, 1, 1)), r)
        r = pltpu.roll(u, 7, 0)
        y_high = jnp.where(sub == 7, jnp.where(lane == 3, pltpu.roll(r, 3, 1), pltpu.roll(r, 127, 1)), r)
        near = (pltpu.roll(u, 4, 1), pltpu.roll(u, 124, 1), y_low, y_high, below[sp] * has_low, above[sp] * has_high)
        val = w[7 * sp + 6] * u
        for i in range(6):
            val = val + w[7 * sp + i] * near[i]
        new.append(val)
    r = react * state[0] * state[1]
    return new[0] - r, new[1] - r, new[2] + r


class Place(NamedTuple):
    slice: jax.Array
    z: jax.Array
    group: jax.Array
    y: jax.Array
    core: jax.Array
    quarters: tuple


def place():
    tm = lax.axis_index("tm")
    x, y, core = tm // 8, tm // 2 % 4, tm % 2
    return Place(tm, lax.axis_index("space"), x, y, core, (y % 2 * 2 + core, x % 2 * 2 + core))


def edges():
    z = lax.axis_index("space")
    has_low = jnp.where(z > 0, 1.0, 0.0).astype(F32)
    has_high = jnp.where(z < lax.axis_size("space") - 1, 1.0, 0.0).astype(F32)
    return has_low, has_high


def coarse_rows(pack, at):
    return [pack[at + sp] for sp in range(3)]


def slabs(low, own, high):
    return lambda sp, p, v: (low, own, high)[p // 4][sp * 64 + p % 4 * 16 + v]


def first_kernel(thin, own, low, high, cf, out, buf_a, buf_b):
    four_steps(slabs(low, own, high), buf_a, buf_b, cf)
    coarse = coarse_plane_step(*[coarse_rows(r, 192) for r in (own, low, high)], thin[...])
    for sp in range(3):
        out[pl.ds(64 * sp, 64)] = buf_b[sp, 64:128]
        out[192 + sp] = coarse[sp]


def second_kernel(thin, part_cf, own, low, high, cf, pack, sent, buf_a, buf_b):
    four_steps(slabs(low, own, high), buf_a, buf_b, cf)
    part = fold_rows(block_rows(lambda sp, z, v: buf_b[sp, 64 + 16 * z + v], 3), *coarse_maps(3))
    old = coarse_plane_step(*[coarse_rows(r, 192) for r in (own, low, high)], thin[...])
    first = place().slice == 0
    block = []
    for sp in range(3):
        own_part = part[8 * sp:8 * sp + 8]
        pack[pl.ds(64 * sp, 64)] = buf_b[sp, 64:128]
        pack[192 + sp] = own_part
        block.append(own_part - jnp.where(first, 0.0, old[sp]))
    block.append(part_cf[...])
    for to in range(8):
        for j in range(4):
            sent[to, 8 * j:8 * j + 8] = block[j]


def coarse_step(rows, cf):
    lane = lax.broadcasted_iota(jnp.int32, (8, 128), 1) % 4
    out = [[], [], []]
    for y in range(8):
        new = []
        for sp in range(3):
            u = rows[sp][y]
            if y > 0:
                below = rows[sp][y - 1]
            else:
                below = jnp.where(lane == 0, pltpu.roll(rows[sp][7], 125, 1), pltpu.roll(rows[sp][7], 1, 1))
            if y < 7:
                above = rows[sp][y + 1]
            else:
                above = jnp.where(lane == 3, pltpu.roll(rows[sp][0], 3, 1), pltpu.roll(rows[sp][0], 127, 1))
            w = [cf[7 * sp + i, y] for i in range(7)]
            val = (w[6] * u + w[2] * below) + (w[3] * above + w[0] * pltpu.roll(u, 4, 1)) + (
                w[1] * pltpu.roll(u, 124, 1) + (w[4] * pltpu.roll(u, 1, 0) + w[5] * pltpu.roll(u, 7, 0)))
            new.append(val)
        r = cf[21, y] * rows[0][y] * rows[1][y]
        for sp, val in enumerate((new[0] - r, new[1] - r, new[2] + r)):
            out[sp].append(val)
    return out


def own_row(z_at, state):
    here = lax.broadcasted_iota(jnp.int32, (24, 8, 128), 1) == z_at
    return jnp.sum(jnp.where(here, state, 0.0), axis=1)


def weights_kernel(*refs):
    got, (after, cf, line) = refs[:8], refs[8:]
    del after
    here = place()
    for k in range(4):
        slot = lax.rem(here.y - k + 4, 4) * 2
        line[slot + here.core] = got[k][...]
        line[slot + 1 - here.core] = got[4 + k][...]
    sub = lax.broadcasted_iota(jnp.int32, (8, 128), 0)
    rows = [line[r // 5, pl.ds(24 + r % 5, 8, stride=32), :] for r in range(40)]
    for y in range(8):
        w, react = plane_coefs(rows, y)
        for i, val in enumerate(w):
            if i % 7 == 4:
                val = jnp.where(sub == 0, 0.0, val)
            if i % 7 == 5:
                val = jnp.where(sub == 7, 0.0, val)
            cf[i, y] = val
        cf[21, y] = react


def run_chain(line, c_in, cf, keep, states):
    here = place()

    def put(i, rows):
        for sp in range(3):
            for y in range(8):
                states[i, 8 * sp + y] = rows[sp][y]

    zero = jnp.zeros((8, 128), F32)
    rows = [[zero if c_in is None else c_in[8 * sp + y] for y in range(8)] for sp in range(3)]
    put(0, rows)
    for i in range(8):
        rows = coarse_step(coarse_step(rows, cf), cf)
        rows = [
            [rows[sp][y] + line[i, pl.ds(8 * sp + y, 8, stride=32), :] for y in range(8)] for sp in range(3)
        ]
        put(i + 1, rows)
    own = 2 * here.y + here.core
    for j in range(2):
        keep[j] = states[own + j]


def chain_kernel(turn, cf, *refs):
    refs = list(refs)
    c_in, kept = (refs.pop(0), refs.pop(0)) if turn else (None, None)
    line, c_out, keep, states = refs

    @pl.when(place().group != turn)
    def _():
        if turn:
            c_out[...] = c_in[...]
            keep[...] = kept[...]
        else:
            c_out[...] = jnp.zeros_like(c_out)
            keep[...] = jnp.zeros_like(keep)

    @pl.when(place().group == turn)
    def _():
        run_chain(line, c_in, cf, keep, states)
        c_out[...] = states[8]


def last_kernel(
    turn, cf, c_in, kept, line, ends, arrived, starts, new_starts, new_ends,
    keep, states, packs, outs, in_sem, out_sem,
):
    packed = [copy(arrived, packs.at[0], in_sem.at[0]), copy(ends, packs.at[1], in_sem.at[1])]

    @pl.when(place().group != turn)
    def _():
        keep[...] = kept[...]

    @pl.when(place().group == turn)
    def _():
        run_chain(line, c_in, cf, keep, states)

    for m in packed:
        m.wait()
    first = place().slice == 0

    @pl.when(first)
    def _():
        copy(starts, outs.at[0], out_sem.at[0]).wait()

    z_at = lax.axis_index("space")
    own = [
        own_row(z_at, keep[which]) - jnp.concatenate([packs[which, 192 + sp] for sp in range(3)], 0)
        for which in range(2)
    ]
    back = unfold_rows(jnp.concatenate(own, 0), *coarse_maps(6))
    for which, dst in ((1, new_ends), (0, new_starts)):
        for sp in range(3):
            def fill(which=which, sp=sp):
                for yv in range(4):
                    at = ((which * 3 + sp) * 4 + yv) * 8
                    cell = back[at:at + 8]
                    for z in range(4):
                        for j in range(4):
                            v = 4 * yv + j
                            outs[which, sp, z, pl.ds(v, 8, stride=16), :] = packs[which, sp * 64 + z * 16 + v] + cell

            if which == 0:
                pl.when(jnp.logical_not(first))(fill)
            else:
                fill()
            copy(outs.at[which, sp], dst.at[sp], out_sem.at[3 * which + sp])
    for which, dst in ((1, new_ends), (0, new_starts)):
        for sp in range(3):
            pltpu.make_async_copy(outs.at[which, sp], dst.at[sp], out_sem.at[3 * which + sp]).wait()


NEAR, FREE = pltpu.VMEM, pl.ANY


def call(kernel, outs, scratch, *args, limit=24, alias=None, cost=2):
    args = [a if isinstance(a, tuple) else (a, NEAR) for a in args]
    return pl.pallas_call(
        kernel,
        out_shape=[jax.ShapeDtypeStruct(s, F32) for s, _ in outs],
        in_specs=[pl.BlockSpec(memory_space=space) for _, space in args],
        out_specs=[pl.BlockSpec(memory_space=space) for _, space in outs],
        scratch_shapes=[
            pltpu.SemaphoreType.DMA((s,)) if isinstance(s, int) else pltpu.VMEM(s, F32) for s in scratch
        ],
        input_output_aliases=alias or {},
        cost_estimate=pl.CostEstimate(flops=int(cost * 1e9), bytes_accessed=1_000_000, transcendentals=0),
        compiler_params=pltpu.CompilerParams(vmem_limit_bytes=limit * 1024 * 1024),
    )(*[a for a, _ in args])


def over_z(block, move):
    count = lax.axis_size("space")
    return lax.ppermute(block, "space", [(i, move(i) % count) for i in range(count)])


def over_tm(block, move):
    pairs = []
    for i in range(32):
        x, y, c = move(i // 8, i // 2 % 4, i % 2)
        pairs.append((i, (x % 4) * 8 + (y % 4) * 2 + c))
    return lax.ppermute(block, "tm", pairs)


def shards(starts, velocity, diffusivity, rate):
    slab = starts[0]
    free = lambda *arrays: [(a, FREE) for a in arrays]

    cf_shape, pack_shape, piece_shape = (10, 8, 16, 8, 128), (195, 8, 128), (5, 3, 32, 128)
    up_by, down_by = (lambda i: i + 1), (lambda i: i - 1)
    first, second = call(
        share_kernel, [(piece_shape, NEAR)] * 2, [6], *free(velocity, diffusivity, rate), limit=60
    )
    first = over_z(first, lambda i: i ^ 1)
    second = over_z(second, lambda i: ((i + 1) ^ 1) - 1)
    (own,) = call(pack_kernel, [(pack_shape, NEAR)], [], slab)
    low, high = over_z(own, up_by), over_z(own, down_by)
    swap = lambda block: over_tm(block, lambda x, y, c: (x, y, 1 - c))
    first = [first, over_tm(first, lambda x, y, c: (x, y ^ 1, c))]
    second = [second, over_tm(second, lambda x, y, c: (x ^ 1, y, c))]
    pieces = first + [swap(p) for p in first] + second + [swap(p) for p in second]
    cf, thin, part_cf = call(
        coefs_kernel, [(cf_shape, NEAR), ((40, 128), NEAR), ((8, 128), NEAR)], [(2, 5, 3, 128, 128), 8],
        velocity, diffusivity, rate, *free(*pieces),
    )

    fine_scratch = [(3, 192, 8, 128), (3, 192, 8, 128)]
    (middle,) = call(first_kernel, [(pack_shape, NEAR)], fine_scratch, thin, own, low, high, cf, cost=6)
    low, high = over_z(middle, up_by), over_z(middle, down_by)
    pack, sent = call(
        second_kernel, [(pack_shape, NEAR), ((8, 32, 128), NEAR)], fine_scratch,
        thin, part_cf, middle, low, high, cf, cost=6,
    )

    arrived = over_tm(pack, lambda x, y, c: (x + (y + c) // 4, y + c, 1 - c))
    defect = lax.all_to_all(sent, "space", 0, 0, tiled=True).reshape(256, 128)
    two = over_tm(defect, lambda x, y, c: (x, y + 2, c))
    one, three = [over_tm(defect, lambda x, y, c, k=k: (x, y + k, c)) for k in (1, 3)]
    rows = [defect, one, two, three]
    coarse_cf, line = call(
        weights_kernel, [((22, 8, 8, 128), NEAR), ((8, 256, 128), NEAR)], [],
        *rows, *[swap(r) for r in rows], *free(arrived),
    )

    grid = (24, 8, 128)
    chain_scratch = [(9, 24, 8, 128)]
    state = ()
    for turn in range(3):
        out, kept = call(
            functools.partial(chain_kernel, turn), [(grid, NEAR), ((2, 24, 8, 128), NEAR)], chain_scratch,
            coarse_cf, *state, line,
        )
        state = (over_tm(out, lambda x, y, c: (x + 1, y, c)), kept)
    new_starts, new_ends = call(
        functools.partial(last_kernel, 3), [((3, 4, 128, 128), FREE)] * 2,
        [(2, 24, 8, 128)] + chain_scratch + [(2, 195, 8, 128), (2, 3, 4, 128, 128), 2, 6],
        coarse_cf, *state, line, *free(pack, arrived, slab),
    )
    return (new_starts[None], new_ends[None])


def solution(mesh):
    placed = (
        P("tm", None, "space", None, None),
        P(None, "space", None, None),
        P("space", None, None),
        P("space", None, None),
    )
    return jax.shard_map(
        shards,
        mesh=mesh,
        in_specs=placed,
        out_specs=(P("tm", None, "space", None, None), P("tm", None, "space", None, None)),
        check_vma=False,
    )
```

time: 115 us -> 112 us (0.974)
  blocking collectives: 0 us -> 15.5 us
  waiting for transfers between devices: 53.9 us -> 42.4 us
  starting transfers between devices: 37.1 us -> 33.8 us
  Pallas kernels: 21.1 us -> 18.9 us
    all_to_all x0 -> x1, blocking collectives: none -> 15.5 us  [shards(): defect = lax.all_to_all(sent, 'space', 0, 0, tiled=True).reshape(256, 128)]
    all_to_all x1 -> x0, waiting for transfers between devices: 10.5 us -> none  [shards(): got = lax.all_to_all(sent, 'space', 0, 0, tiled=True)]
    all_to_all x1 -> x0, starting transfers between devices: 5.34 us -> none  [shards(): got = lax.all_to_all(sent, 'space', 0, 0, tiled=True)]
    pallas_call x11 -> x10, Pallas kernels: 21.1 us -> 18.9 us  [call(): pl.pallas_call(kernel, out_shape=[jax.ShapeDtypeStruct(s, F32) for s, _ i...]
    ppermute x6, waiting for transfers between devices: 25.2 us -> 23.6 us  [over_z(): lax.ppermute(block, 'space', [(i, move(i) % count) for i in range(count)])]
  transfers between devices with their start and end apart: 24 -> 23, of which waited for: 16 -> 15; matrix products, arithmetic and copies ran while one was open for 0% -> 0% of each run, Pallas kernels for 3% -> 3%
where the time goes in v3:
time: 112 us
  waiting for transfers between devices  42.4 us (38%)
  starting transfers between devices  33.8 us (30%)
  Pallas kernels  18.9 us (17%)
  blocking collectives  15.5 us (14%)
    ppermute x6, waiting for transfers between devices, over_z(): lax.ppermute(block, 'space', [(i, move(i) % count) for i in range(count)])  23.6 us
    ppermute x17, starting transfers between devices, over_tm(): return lax.ppermute(block, 'tm', pairs)  20.1 us
    pallas_call x10, Pallas kernels, call(): pl.pallas_call(kernel, out_shape=[jax.ShapeDtypeStruct(s, F32) for s, _ i...  18.9 us
    ppermute x17, waiting for transfers between devices, over_tm(): return lax.ppermute(block, 'tm', pairs)  18.8 us
    all_to_all x1, blocking collectives, shards(): defect = lax.all_to_all(sent, 'space', 0, 0, tiled=True).reshape(256, 128)  15.5 us
    ppermute x6, starting transfers between devices, over_z(): lax.ppermute(block, 'space', [(i, move(i) % count) for i in range(count)])  13.7 us
  transfers between devices with their start and end apart: 23, of which 15 were waited for; matrix products, arithmetic and copies ran while one was open for 0% of the time, Pallas kernels for 3%

profile of v3, /device:TPU:6, one launch (start us, length us, event | category | flops | bytes accessed | tf_op | source)
XLA Modules:
  0.0 111.6 jit_solution(2691136269786608672)
XLA Ops:
  0.6 2.0 %shard_map.59 = (f32[5,3,32,128]{3,2,1,0:T(8,128)}, f32[5,3,32,128]{3,2,1,0:T(8,128)}) custom-call(f32[3,4,128,128]{3,2,1,0:T(8,128)} %vel.3, f32[4,128,128]{2,1,0:T(8,128)} %dif.3, f32[4,128,128]{2,1,0:T(8,128)} %rate.3), custom_call_target="tpu_custom_call" | custom-call | flops 2000000000 | bytes 1000000 | tf_op jit(solution)/shard_map/pallas_call | solution.py:445
  2.6 2.0 %collective-permute-start = (f32[5,3,32,128]{3,2,1,0:T(8,128)}, f32[5,3,32,128]{3,2,1,0:T(8,128)S(1)}, u32[]{:S(2)}, u32[]{:S(2)}) collective-permute-start(f32[5,3,32,128]{3,2,1,0:T(8,128)} %get-tuple-element.19), channel_id=1, source_target_pairs={{0,1},{1,0},{2,3},{3,2},{4,5},{5,4},{6,7},{7,6},{8,9},{9,8},{10,11... | collective-permute-start | bytes 737288 | tf_op jit(solution)/shard_map/ppermute | solution.py:461
  4.6 4.9 %collective-permute-start.4 = (f32[5,3,32,128]{3,2,1,0:T(8,128)}, f32[5,3,32,128]{3,2,1,0:T(8,128)S(1)}, u32[]{:S(2)}, u32[]{:S(2)}) collective-permute-start(f32[5,3,32,128]{3,2,1,0:T(8,128)} %get-tuple-element.20), channel_id=1, source_target_pairs={{0,7},{1,2},{2,1},{3,4},{4,3},{5,6},{6,5},{7,0},{8,15},{9,10},{10,... | collective-permute-start | bytes 737288 | tf_op jit(solution)/shard_map/ppermute | solution.py:461
  9.6 0.8 shard_map.61.own
  10.4 3.2 %collective-permute-start.9 = (f32[195,8,128]{2,1,0:T(8,128)S(1)}, f32[195,8,128]{2,1,0:T(8,128)S(1)}, u32[]{:S(2)}, u32[]{:S(2)}) collective-permute-start(f32[195,8,128]{2,1,0:T(8,128)S(1)} %shard_map.61.own), channel_id=1, source_target_pairs={{0,7},{1,0},{2,1},{3,2},{4,3},{5,4},{6,5},{7,6},{8,15},{9,8},{10,9... | collective-permute-start | bytes 2396168 | tf_op jit(solution)/shard_map/ppermute | solution.py:461
  13.7 1.6 %collective-permute-start.1 = (f32[5,3,32,128]{3,2,1,0:T(8,128)S(1)}, f32[5,3,32,128]{3,2,1,0:T(8,128)S(1)}, u32[]{:S(2)}, u32[]{:S(2)}) collective-permute-start(f32[5,3,32,128]{3,2,1,0:T(8,128)S(1)} %collective-permute-done.refs_0_), channel_id=1, source_target_pairs={{0,16},{8,24},{16,0},{24,8},{32,48},{40,56},{48,32},{56,40},{64,80... | collective-permute-start | bytes 737288 | tf_op jit(solution)/shard_map/ppermute | solution.py:469
  15.3 1.4 %collective-permute-done.4.refs_4_ = f32[5,3,32,128]{3,2,1,0:T(8,128)S(1)} collective-permute-done((f32[5,3,32,128]{3,2,1,0:T(8,128)}, f32[5,3,32,128]{3,2,1,0:T(8,128)S(1)}, u32[]{:S(2)}, u32[]{:S(2)}) %collective-permute-start.4) | collective-permute-done | bytes 245792 | tf_op jit(solution)/shard_map/ppermute | solution.py:461
  16.6 0.8 collective-permute-start.5
  17.4 2.8 %collective-permute-done.1.refs_1_ = f32[5,3,32,128]{3,2,1,0:T(8,128)S(1)} collective-permute-done((f32[5,3,32,128]{3,2,1,0:T(8,128)S(1)}, f32[5,3,32,128]{3,2,1,0:T(8,128)S(1)}, u32[]{:S(2)}, u32[]{:S(2)}) %collective-permute-start.1) | collective-permute-done | bytes 245792 | tf_op jit(solution)/shard_map/ppermute | solution.py:469
  20.2 2.6 %collective-permute-done.5.refs_5_ = f32[5,3,32,128]{3,2,1,0:T(8,128)S(1)} collective-permute-done((f32[5,3,32,128]{3,2,1,0:T(8,128)S(1)}, f32[5,3,32,128]{3,2,1,0:T(8,128)S(1)}, u32[]{:S(2)}, u32[]{:S(2)}) %collective-permute-start.5) | collective-permute-done | bytes 245792 | tf_op jit(solution)/shard_map/ppermute | solution.py:469
  22.8 0.5 collective-permute-start.7
  23.3 1.0 collective-permute-done.3.refs_3_
  24.7 2.3 %shard_map.60 = (f32[10,8,16,8,128]{4,3,2,1,0:T(8,128)S(1)}, f32[40,128]{1,0:T(8,128)S(1)}, f32[8,128]{1,0:T(8,128)S(1)}) custom-call(f32[3,4,128,128]{3,2,1,0:T(8,128)S(1)} %copy-done, f32[4,128,128]{2,1,0:T(8,128)S(1)} %copy-done.2, f32[4,128,128]{2,1,0:T(8,128)S(1)} %copy-done.3, f32[5,3,32,128]{3,2,1,0:T(8,128)S(1)} %collective-permute-done.refs_0_, ...), custom_call_target="tpu_custom_call" | custom-call | flops 2000000000 | bytes 1000000 | tf_op jit(solution)/shard_map/pallas_call | solution.py:445
  27.0 5.5 %collective-permute-done.8.low = f32[195,8,128]{2,1,0:T(8,128)S(1)} collective-permute-done((f32[195,8,128]{2,1,0:T(8,128)S(1)}, f32[195,8,128]{2,1,0:T(8,128)S(1)}, u32[]{:S(2)}, u32[]{:S(2)}) %collective-permute-start.8) | collective-permute-done | bytes 798752 | tf_op jit(solution)/shard_map/ppermute | solution.py:461
  32.6 4.4 %shard_map.62.own = f32[195,8,128]{2,1,0:T(8,128)S(1)} custom-call(f32[40,128]{1,0:T(8,128)S(1)} %get-tuple-element.21.thin, f32[195,8,128]{2,1,0:T(8,128)S(1)} %shard_map.61.own, f32[195,8,128]{2,1,0:T(8,128)S(1)} %collective-permute-done.8.low, f32[195,8,128]{2,1,0:T(8,128)S(1)} %collective-permute-done.9.high, f32[10,8,16,8,128]{4,3,2,1,0:T(8,128)S(1)} %get-tuple-element.23.cf), custom_call_target="tpu_custom_call" | custom-call | flops 6000000000 | bytes 1000000 | tf_op jit(solution)/shard_map/pallas_call | solution.py:445
  37.3 3.2 %collective-permute-start.11 = (f32[195,8,128]{2,1,0:T(8,128)S(1)}, f32[195,8,128]{2,1,0:T(8,128)S(1)}, u32[]{:S(2)}, u32[]{:S(2)}) collective-permute-start(f32[195,8,128]{2,1,0:T(8,128)S(1)} %shard_map.62.own), channel_id=1, source_target_pairs={{0,7},{1,0},{2,1},{3,2},{4,3},{5,4},{6,5},{7,6},{8,15},{9,8},{10,9... | collective-permute-start | bytes 2396168 | tf_op jit(solution)/shard_map/ppermute | solution.py:461
  40.5 16.6 %collective-permute-done.10.low = f32[195,8,128]{2,1,0:T(8,128)S(1)} collective-permute-done((f32[195,8,128]{2,1,0:T(8,128)S(1)}, f32[195,8,128]{2,1,0:T(8,128)S(1)}, u32[]{:S(2)}, u32[]{:S(2)}) %collective-permute-start.10) | collective-permute-done | bytes 798752 | tf_op jit(solution)/shard_map/ppermute | solution.py:461
  57.2 5.0 %shard_map.63 = (f32[195,8,128]{2,1,0:T(8,128)S(1)}, f32[8,32,128]{2,1,0:T(8,128)S(1)}) custom-call(f32[40,128]{1,0:T(8,128)S(1)} %get-tuple-element.21.thin, f32[8,128]{1,0:T(8,128)S(1)} %get-tuple-element.22.part_cf, f32[195,8,128]{2,1,0:T(8,128)S(1)} %shard_map.62.own, f32[195,8,128]{2,1,0:T(8,128)S(1)} %collective-permute-done.10.low, ...), custom_call_target="tpu_custom_call" | custom-call | flops 6000000000 | bytes 1000000 | tf_op jit(solution)/shard_map/pallas_call | solution.py:445
  62.2 15.5 %all_to_all.5 = f32[8,32,128]{2,1,0:T(8,128)S(1)} all-to-all(f32[8,32,128]{2,1,0:T(8,128)S(1)} %get-tuple-element.24), channel_id=1, replica_groups=mesh['tm'=32,'space'=8] {'space'}, dimensions={0} | all-to-all | bytes 262144 | tf_op jit(solution)/shard_map/all_to_all | solution.py:503
  77.8 1.6 %collective-permute-start.12 = (f32[256,128]{1,0:T(8,128)S(1)}, f32[256,128]{1,0:T(8,128)S(1)}, u32[]{:S(2)}, u32[]{:S(2)}) collective-permute-start(f32[256,128]{1,0:T(8,128)S(1)} %bitcast.4), channel_id=1, source_target_pairs={{0,16},{8,24},{16,32},{24,40},{32,48},{40,56},{48,0},{56,8},{64,80... | collective-permute-start | bytes 393224 | tf_op jit(solution)/shard_map/ppermute | solution.py:469
  79.3 2.1 %collective-permute-start.13 = (f32[256,128]{1,0:T(8,128)S(1)}, f32[256,128]{1,0:T(8,128)S(1)}, u32[]{:S(2)}, u32[]{:S(2)}) collective-permute-start(f32[256,128]{1,0:T(8,128)S(1)} %bitcast.5), channel_id=1, source_target_pairs={{0,32},{8,40},{16,48},{24,56},{32,0},{40,8},{48,16},{56,24},{64,96... | collective-permute-start | bytes 393224 | tf_op jit(solution)/shard_map/ppermute | solution.py:469
  81.4 2.3 %collective-permute-start.14 = (f32[256,128]{1,0:T(8,128)S(1)}, f32[256,128]{1,0:T(8,128)S(1)}, u32[]{:S(2)}, u32[]{:S(2)}) collective-permute-start(f32[256,128]{1,0:T(8,128)S(1)} %bitcast.6), channel_id=1, source_target_pairs={{0,48},{8,56},{16,0},{24,8},{32,16},{40,24},{48,32},{56,40},{64,11... | collective-permute-start | bytes 393224 | tf_op jit(solution)/shard_map/ppermute | solution.py:469
  83.7 1.2 %collective-permute-done.12.refs_1_ = f32[256,128]{1,0:T(8,128)S(1)} collective-permute-done((f32[256,128]{1,0:T(8,128)S(1)}, f32[256,128]{1,0:T(8,128)S(1)}, u32[]{:S(2)}, u32[]{:S(2)}) %collective-permute-start.12) | collective-permute-done | bytes 131104 | tf_op jit(solution)/shard_map/ppermute | solution.py:469
  85.0 2.7 %collective-permute-done.13.refs_2_ = f32[256,128]{1,0:T(8,128)S(1)} collective-permute-done((f32[256,128]{1,0:T(8,128)S(1)}, f32[256,128]{1,0:T(8,128)S(1)}, u32[]{:S(2)}, u32[]{:S(2)}) %collective-permute-start.13) | collective-permute-done | bytes 131104 | tf_op jit(solution)/shard_map/ppermute | solution.py:469
  88.2 0.8 collective-permute-done.17.refs_6_
  89.8 3.3 %collective-permute-start.20 = (f32[24,8,128]{2,1,0:T(8,128)S(1)}, f32[24,8,128]{2,1,0:T(8,128)S(1)}, u32[]{:S(2)}, u32[]{:S(2)}) collective-permute-start(f32[24,8,128]{2,1,0:T(8,128)S(1)} %get-tuple-element.28), channel_id=1, source_target_pairs={{0,64},{8,72},{16,80},{24,88},{32,96},{40,104},{48,112},{56,120},{... | collective-permute-start | bytes 294920 | tf_op jit(solution)/shard_map/ppermute | solution.py:469
  93.1 2.5 %collective-permute-done.20.refs_0_ = f32[24,8,128]{2,1,0:T(8,128)S(1)} collective-permute-done((f32[24,8,128]{2,1,0:T(8,128)S(1)}, f32[24,8,128]{2,1,0:T(8,128)S(1)}, u32[]{:S(2)}, u32[]{:S(2)}) %collective-permute-start.20) | collective-permute-done | bytes 98336 | tf_op jit(solution)/shard_map/ppermute | solution.py:469
  95.7 3.8 %collective-permute-start.21 = (f32[24,8,128]{2,1,0:T(8,128)S(1)}, f32[24,8,128]{2,1,0:T(8,128)S(1)}, u32[]{:S(2)}, u32[]{:S(2)}) collective-permute-start(f32[24,8,128]{2,1,0:T(8,128)S(1)} %get-tuple-element.30), channel_id=1, source_target_pairs={{0,64},{8,72},{16,80},{24,88},{32,96},{40,104},{48,112},{56,120},{... | collective-permute-start | bytes 294920 | tf_op jit(solution)/shard_map/ppermute | solution.py:469
  99.4 2.2 %collective-permute-done.21.refs_0_ = f32[24,8,128]{2,1,0:T(8,128)S(1)} collective-permute-done((f32[24,8,128]{2,1,0:T(8,128)S(1)}, f32[24,8,128]{2,1,0:T(8,128)S(1)}, u32[]{:S(2)}, u32[]{:S(2)}) %collective-permute-start.21) | collective-permute-done | bytes 98336 | tf_op jit(solution)/shard_map/ppermute | solution.py:469
  101.7 3.7 %collective-permute-start.22 = (f32[24,8,128]{2,1,0:T(8,128)S(1)}, f32[24,8,128]{2,1,0:T(8,128)S(1)}, u32[]{:S(2)}, u32[]{:S(2)}) collective-permute-start(f32[24,8,128]{2,1,0:T(8,128)S(1)} %get-tuple-element.32), channel_id=1, source_target_pairs={{0,64},{8,72},{16,80},{24,88},{32,96},{40,104},{48,112},{56,120},{... | collective-permute-start | bytes 294920 | tf_op jit(solution)/shard_map/ppermute | solution.py:469
  105.4 2.2 %collective-permute-done.22.c_in = f32[24,8,128]{2,1,0:T(8,128)S(1)} collective-permute-done((f32[24,8,128]{2,1,0:T(8,128)S(1)}, f32[24,8,128]{2,1,0:T(8,128)S(1)}, u32[]{:S(2)}, u32[]{:S(2)}) %collective-permute-start.22) | collective-permute-done | bytes 98336 | tf_op jit(solution)/shard_map/ppermute | solution.py:469
  107.6 3.9 %shard_map.68 = (f32[3,4,128,128]{3,2,1,0:T(8,128)}, f32[3,4,128,128]{3,2,1,0:T(8,128)}) custom-call(f32[22,8,8,128]{3,2,1,0:T(8,128)S(1)} %get-tuple-element.26.cf, f32[24,8,128]{2,1,0:T(8,128)S(1)} %collective-permute-done.22.c_in, f32[2,24,8,128]{3,2,1,0:T(8,128)S(1)} %get-tuple-element.33.kept, ...), custom_call_target="tpu_custom_call" | custom-call | flops 2000000000 | bytes 1000000 | tf_op jit(solution)/shard_map/pallas_call | solution.py:445
  (33 shorter events, 2.0 us)
Async XLA Ops:
  0.6 9.0 %copy-start.1 = (f32[1,3,4,128,128]{4,3,2,1,0:T(8,128)S(1)}, f32[1,3,4,128,128]{4,3,2,1,0:T(8,128)}, u32[]{:S(2)}) copy-start(f32[1,3,4,128,128]{4,3,2,1,0:T(8,128)} %param.4) | copy-start | bytes 2359300
  2.6 22.1 %copy-start = (f32[3,4,128,128]{3,2,1,0:T(8,128)S(1)}, f32[3,4,128,128]{3,2,1,0:T(8,128)}, u32[]{:S(2)}) copy-start(f32[3,4,128,128]{3,2,1,0:T(8,128)} %vel.3) | copy-start | bytes 2359300
  2.6 22.1 %copy-start.2 = (f32[4,128,128]{2,1,0:T(8,128)S(1)}, f32[4,128,128]{2,1,0:T(8,128)}, u32[]{:S(2)}) copy-start(f32[4,128,128]{2,1,0:T(8,128)} %dif.3) | copy-start | bytes 786436
  2.6 22.1 %copy-start.3 = (f32[4,128,128]{2,1,0:T(8,128)S(1)}, f32[4,128,128]{2,1,0:T(8,128)}, u32[]{:S(2)}) copy-start(f32[4,128,128]{2,1,0:T(8,128)} %rate.3) | copy-start | bytes 786436
  2.6 11.0 %collective-permute-start = (f32[5,3,32,128]{3,2,1,0:T(8,128)}, f32[5,3,32,128]{3,2,1,0:T(8,128)S(1)}, u32[]{:S(2)}, u32[]{:S(2)}) collective-permute-start(f32[5,3,32,128]{3,2,1,0:T(8,128)} %get-tuple-element.19), channel_id=1, source_target_pairs={{0,1},{1,0},{2,3},{3,2},{4,5},{5,4},{6,7},{7,6},{8,9},{9,8},{10,11... | collective-permute-start | bytes 737288 | tf_op jit(solution)/shard_map/ppermute | solution.py:461
  4.6 12.0 %collective-permute-start.4 = (f32[5,3,32,128]{3,2,1,0:T(8,128)}, f32[5,3,32,128]{3,2,1,0:T(8,128)S(1)}, u32[]{:S(2)}, u32[]{:S(2)}) collective-permute-start(f32[5,3,32,128]{3,2,1,0:T(8,128)} %get-tuple-element.20), channel_id=1, source_target_pairs={{0,7},{1,2},{2,1},{3,4},{4,3},{5,6},{6,5},{7,0},{8,15},{9,10},{10,... | collective-permute-start | bytes 737288 | tf_op jit(solution)/shard_map/ppermute | solution.py:461
  10.4 22.2 %collective-permute-start.8 = (f32[195,8,128]{2,1,0:T(8,128)S(1)}, f32[195,8,128]{2,1,0:T(8,128)S(1)}, u32[]{:S(2)}, u32[]{:S(2)}) collective-permute-start(f32[195,8,128]{2,1,0:T(8,128)S(1)} %shard_map.61.own), channel_id=1, source_target_pairs={{0,1},{1,2},{2,3},{3,4},{4,5},{5,6},{6,7},{7,0},{8,9},{9,10},{10,1... | collective-permute-start | bytes 2396168 | tf_op jit(solution)/shard_map/ppermute | solution.py:461
  10.4 22.2 %collective-permute-start.9 = (f32[195,8,128]{2,1,0:T(8,128)S(1)}, f32[195,8,128]{2,1,0:T(8,128)S(1)}, u32[]{:S(2)}, u32[]{:S(2)}) collective-permute-start(f32[195,8,128]{2,1,0:T(8,128)S(1)} %shard_map.61.own), channel_id=1, source_target_pairs={{0,7},{1,0},{2,1},{3,2},{4,3},{5,4},{6,5},{7,6},{8,15},{9,8},{10,9... | collective-permute-start | bytes 2396168 | tf_op jit(solution)/shard_map/ppermute | solution.py:461
  13.7 6.6 %collective-permute-start.1 = (f32[5,3,32,128]{3,2,1,0:T(8,128)S(1)}, f32[5,3,32,128]{3,2,1,0:T(8,128)S(1)}, u32[]{:S(2)}, u32[]{:S(2)}) collective-permute-start(f32[5,3,32,128]{3,2,1,0:T(8,128)S(1)} %collective-permute-done.refs_0_), channel_id=1, source_target_pairs={{0,16},{8,24},{16,0},{24,8},{32,48},{40,56},{48,32},{56,40},{64,80... | collective-permute-start | bytes 737288 | tf_op jit(solution)/shard_map/ppermute | solution.py:469
  16.6 6.2 %collective-permute-start.5 = (f32[5,3,32,128]{3,2,1,0:T(8,128)S(1)}, f32[5,3,32,128]{3,2,1,0:T(8,128)S(1)}, u32[]{:S(2)}, u32[]{:S(2)}) collective-permute-start(f32[5,3,32,128]{3,2,1,0:T(8,128)S(1)} %collective-permute-done.4.refs_4_), channel_id=1, source_target_pairs={{0,64},{8,72},{16,80},{24,88},{32,96},{40,104},{48,112},{56,120},{... | collective-permute-start | bytes 737288 | tf_op jit(solution)/shard_map/ppermute | solution.py:469
  17.4 5.4 %collective-permute-start.2 = (f32[5,3,32,128]{3,2,1,0:T(8,128)S(1)}, f32[5,3,32,128]{3,2,1,0:T(8,128)S(1)}, u32[]{:S(2)}, u32[]{:S(2)}) collective-permute-start(f32[5,3,32,128]{3,2,1,0:T(8,128)S(1)} %collective-permute-done.refs_0_), channel_id=1, source_target_pairs={{0,8},{8,0},{16,24},{24,16},{32,40},{40,32},{48,56},{56,48},{64,72... | collective-permute-start | bytes 737288 | tf_op jit(solution)/shard_map/ppermute | solution.py:469
  20.2 3.1 %collective-permute-start.6 = (f32[5,3,32,128]{3,2,1,0:T(8,128)S(1)}, f32[5,3,32,128]{3,2,1,0:T(8,128)S(1)}, u32[]{:S(2)}, u32[]{:S(2)}) collective-permute-start(f32[5,3,32,128]{3,2,1,0:T(8,128)S(1)} %collective-permute-done.4.refs_4_), channel_id=1, source_target_pairs={{0,8},{8,0},{16,24},{24,16},{32,40},{40,32},{48,56},{56,48},{64,72... | collective-permute-start | bytes 737288 | tf_op jit(solution)/shard_map/ppermute | solution.py:469
  22.8 1.5 %collective-permute-start.3 = (f32[5,3,32,128]{3,2,1,0:T(8,128)S(1)}, f32[5,3,32,128]{3,2,1,0:T(8,128)S(1)}, u32[]{:S(2)}, u32[]{:S(2)}) collective-permute-start(f32[5,3,32,128]{3,2,1,0:T(8,128)S(1)} %collective-permute-done.1.refs_1_), channel_id=1, source_target_pairs={{0,8},{8,0},{16,24},{24,16},{32,40},{40,32},{48,56},{56,48},{64,72... | collective-permute-start | bytes 737288 | tf_op jit(solution)/shard_map/ppermute | solution.py:469
  22.8 1.9 %collective-permute-start.7 = (f32[5,3,32,128]{3,2,1,0:T(8,128)S(1)}, f32[5,3,32,128]{3,2,1,0:T(8,128)S(1)}, u32[]{:S(2)}, u32[]{:S(2)}) collective-permute-start(f32[5,3,32,128]{3,2,1,0:T(8,128)S(1)} %collective-permute-done.5.refs_5_), channel_id=1, source_target_pairs={{0,8},{8,0},{16,24},{24,16},{32,40},{40,32},{48,56},{56,48},{64,72... | collective-permute-start | bytes 737288 | tf_op jit(solution)/shard_map/ppermute | solution.py:469
  37.0 20.1 %collective-permute-start.10 = (f32[195,8,128]{2,1,0:T(8,128)S(1)}, f32[195,8,128]{2,1,0:T(8,128)S(1)}, u32[]{:S(2)}, u32[]{:S(2)}) collective-permute-start(f32[195,8,128]{2,1,0:T(8,128)S(1)} %shard_map.62.own), channel_id=1, source_target_pairs={{0,1},{1,2},{2,3},{3,4},{4,5},{5,6},{6,7},{7,0},{8,9},{9,10},{10,1... | collective-permute-start | bytes 2396168 | tf_op jit(solution)/shard_map/ppermute | solution.py:461
  37.3 19.9 %collective-permute-start.11 = (f32[195,8,128]{2,1,0:T(8,128)S(1)}, f32[195,8,128]{2,1,0:T(8,128)S(1)}, u32[]{:S(2)}, u32[]{:S(2)}) collective-permute-start(f32[195,8,128]{2,1,0:T(8,128)S(1)} %shard_map.62.own), channel_id=1, source_target_pairs={{0,7},{1,0},{2,1},{3,2},{4,3},{5,4},{6,5},{7,6},{8,15},{9,8},{10,9... | collective-permute-start | bytes 2396168 | tf_op jit(solution)/shard_map/ppermute | solution.py:461
  62.1 27.1 %collective-permute-start.19 = (f32[195,8,128]{2,1,0:T(8,128)S(1)}, f32[195,8,128]{2,1,0:T(8,128)S(1)}, u32[]{:S(2)}, u32[]{:S(2)}) collective-permute-start(f32[195,8,128]{2,1,0:T(8,128)S(1)} %get-tuple-element.25.ends), channel_id=1, source_target_pairs={{0,8},{8,16},{16,24},{24,32},{32,40},{40,48},{48,56},{56,64},{64,7... | collective-permute-start | bytes 2396168 | tf_op jit(solution)/shard_map/ppermute | solution.py:469
  77.8 7.2 %collective-permute-start.12 = (f32[256,128]{1,0:T(8,128)S(1)}, f32[256,128]{1,0:T(8,128)S(1)}, u32[]{:S(2)}, u32[]{:S(2)}) collective-permute-start(f32[256,128]{1,0:T(8,128)S(1)} %bitcast.4), channel_id=1, source_target_pairs={{0,16},{8,24},{16,32},{24,40},{32,48},{40,56},{48,0},{56,8},{64,80... | collective-permute-start | bytes 393224 | tf_op jit(solution)/shard_map/ppermute | solution.py:469
  79.3 8.3 %collective-permute-start.13 = (f32[256,128]{1,0:T(8,128)S(1)}, f32[256,128]{1,0:T(8,128)S(1)}, u32[]{:S(2)}, u32[]{:S(2)}) collective-permute-start(f32[256,128]{1,0:T(8,128)S(1)} %bitcast.5), channel_id=1, source_target_pairs={{0,32},{8,40},{16,48},{24,56},{32,0},{40,8},{48,16},{56,24},{64,96... | collective-permute-start | bytes 393224 | tf_op jit(solution)/shard_map/ppermute | solution.py:469
  81.4 6.4 %collective-permute-start.14 = (f32[256,128]{1,0:T(8,128)S(1)}, f32[256,128]{1,0:T(8,128)S(1)}, u32[]{:S(2)}, u32[]{:S(2)}) collective-permute-start(f32[256,128]{1,0:T(8,128)S(1)} %bitcast.6), channel_id=1, source_target_pairs={{0,48},{8,56},{16,0},{24,8},{32,16},{40,24},{48,32},{56,40},{64,11... | collective-permute-start | bytes 393224 | tf_op jit(solution)/shard_map/ppermute | solution.py:469
  83.7 4.5 %collective-permute-start.15 = (f32[256,128]{1,0:T(8,128)S(1)}, f32[256,128]{1,0:T(8,128)S(1)}, u32[]{:S(2)}, u32[]{:S(2)}) collective-permute-start(f32[256,128]{1,0:T(8,128)S(1)} %bitcast.7), channel_id=1, source_target_pairs={{0,8},{8,0},{16,24},{24,16},{32,40},{40,32},{48,56},{56,48},{64,72... | collective-permute-start | bytes 393224 | tf_op jit(solution)/shard_map/ppermute | solution.py:469
  85.0 3.2 %collective-permute-start.16 = (f32[256,128]{1,0:T(8,128)S(1)}, f32[256,128]{1,0:T(8,128)S(1)}, u32[]{:S(2)}, u32[]{:S(2)}) collective-permute-start(f32[256,128]{1,0:T(8,128)S(1)} %collective-permute-done.12.refs_1_), channel_id=1, source_target_pairs={{0,8},{8,0},{16,24},{24,16},{32,40},{40,32},{48,56},{56,48},{64,72... | collective-permute-start | bytes 393224 | tf_op jit(solution)/shard_map/ppermute | solution.py:469
  87.7 1.3 %collective-permute-start.17 = (f32[256,128]{1,0:T(8,128)S(1)}, f32[256,128]{1,0:T(8,128)S(1)}, u32[]{:S(2)}, u32[]{:S(2)}) collective-permute-start(f32[256,128]{1,0:T(8,128)S(1)} %collective-permute-done.13.refs_2_), channel_id=1, source_target_pairs={{0,8},{8,0},{16,24},{24,16},{32,40},{40,32},{48,56},{56,48},{64,72... | collective-permute-start | bytes 393224 | tf_op jit(solution)/shard_map/ppermute | solution.py:469
  87.9 1.4 %collective-permute-start.18 = (f32[256,128]{1,0:T(8,128)S(1)}, f32[256,128]{1,0:T(8,128)S(1)}, u32[]{:S(2)}, u32[]{:S(2)}) collective-permute-start(f32[256,128]{1,0:T(8,128)S(1)} %collective-permute-done.14.refs_3_), channel_id=1, source_target_pairs={{0,8},{8,0},{16,24},{24,16},{32,40},{40,32},{48,56},{56,48},{64,72... | collective-permute-start | bytes 393224 | tf_op jit(solution)/shard_map/ppermute | solution.py:469
  89.8 5.9 %collective-permute-start.20 = (f32[24,8,128]{2,1,0:T(8,128)S(1)}, f32[24,8,128]{2,1,0:T(8,128)S(1)}, u32[]{:S(2)}, u32[]{:S(2)}) collective-permute-start(f32[24,8,128]{2,1,0:T(8,128)S(1)} %get-tuple-element.28), channel_id=1, source_target_pairs={{0,64},{8,72},{16,80},{24,88},{32,96},{40,104},{48,112},{56,120},{... | collective-permute-start | bytes 294920 | tf_op jit(solution)/shard_map/ppermute | solution.py:469
  95.7 6.0 %collective-permute-start.21 = (f32[24,8,128]{2,1,0:T(8,128)S(1)}, f32[24,8,128]{2,1,0:T(8,128)S(1)}, u32[]{:S(2)}, u32[]{:S(2)}) collective-permute-start(f32[24,8,128]{2,1,0:T(8,128)S(1)} %get-tuple-element.30), channel_id=1, source_target_pairs={{0,64},{8,72},{16,80},{24,88},{32,96},{40,104},{48,112},{56,120},{... | collective-permute-start | bytes 294920 | tf_op jit(solution)/shard_map/ppermute | solution.py:469
  101.7 5.9 %collective-permute-start.22 = (f32[24,8,128]{2,1,0:T(8,128)S(1)}, f32[24,8,128]{2,1,0:T(8,128)S(1)}, u32[]{:S(2)}, u32[]{:S(2)}) collective-permute-start(f32[24,8,128]{2,1,0:T(8,128)S(1)} %get-tuple-element.32), channel_id=1, source_target_pairs={{0,64},{8,72},{16,80},{24,88},{32,96},{40,104},{48,112},{56,120},{... | collective-permute-start | bytes 294920 | tf_op jit(solution)/shard_map/ppermute | solution.py:469
